TPU v7x, 32 devices: a whole 2x2x4 slice. The times are simulated.
32 devices in a mesh: items: 4 (over y, x), heads: 8 (over z, core).
Axes of the slice: x: 2, y: 2, z: 4, core: 2. Of those that a mesh axis runs over, the one named last changes fastest.
Arguments:
- frames: bfloat16 [2, 8192, 1024], P(None, ('items', 'heads')), may hold values from -6 to 6
- cotangent: bfloat16 [2, 8192, 1024], P(None, ('items', 'heads')), may hold values from -6 to 6
- bucket_counts: int32 [2, 4, 2], P(None, 'items'), may hold values from 0 to 4, as said below
- gains: float32 [6, 1024], replicated, may hold values from 0.1 to 1.9
- w_ffn1_in: bfloat16 [1024, 4096], replicated, may hold values from -0.1875 to 0.1875
- w_ffn1_out: bfloat16 [4096, 1024], replicated, may hold values from -0.1875 to 0.1875
- w_qkv: bfloat16 [1024, 3072], replicated, may hold values from -0.1875 to 0.1875
- w_out: bfloat16 [1024, 1024], replicated, may hold values from -1 to 1
- w_point_in: bfloat16 [1024, 2048], replicated, may hold values from -0.1875 to 0.1875
- w_depth: bfloat16 [5, 1024], replicated, may hold values from -2.5 to 2.5
- w_point_out: bfloat16 [1024, 1024], replicated, may hold values from -0.1875 to 0.1875
- w_ffn2_in: bfloat16 [1024, 4096], replicated, may hold values from -0.1875 to 0.1875
- w_ffn2_out: bfloat16 [4096, 1024], replicated, may hold values from -0.1875 to 0.1875
Outputs:
- layer_out: bfloat16 [2, 8192, 1024], P(None, ('items', 'heads'))
- frames_grad: bfloat16 [2, 8192, 1024], P(None, ('items', 'heads'))
- gains_grad: float32 [6, 1024], replicated
- ffn1_in_grad: float32 [1024, 4096], P('heads', 'items')
- ffn1_out_grad: float32 [4096, 1024], P('heads', 'items')
- qkv_grad: float32 [1024, 3072], P('heads', 'items')
- out_grad: float32 [1024, 1024], P('heads', 'items')
- point_in_grad: float32 [1024, 2048], P('heads', 'items')
- depth_grad: float32 [5, 1024], replicated
- point_out_grad: float32 [1024, 1024], P('heads', 'items')
- ffn2_in_grad: float32 [1024, 4096], P('heads', 'items')
- ffn2_out_grad: float32 [4096, 1024], P('heads', 'items')
Inputs may be any that keep to these rules, and one draw needn't show every extreme that they name: bucket_counts[m, g] = (n_long, n_short): group g of micro-batch m holds n_long utterances of 1500 frames first, then n_short = (2048 - n_long 1500) // 500 utterances of 500 frames, then any remaining frames as one more utterance.
All inputs are finite; a program needn't handle non-finite values.
Results may differ from a plain program's by a relative error of at most 0.02.
Values may be sent and summed in bfloat16 or wider, within the bound.
No kernel may reach another device: no remote copies, remote signals or barrier semaphores. Data moves between devices by JAX's collectives and lax.ppermute only.
A program may use at most 320 MiB of HBM per device.

v0:
```python
import jax
import jax.numpy as jnp
from jax import lax
from jax.sharding import PartitionSpec as P

HEADS = 16
KERNEL = 5
LONG = 1500
SHORT = 500


EPS = 1e-05
MASKED = -1e30
ROPE_BASE = 10000.0


def shortened(shard):
    return jax.tree.map(lambda a: a.astype(jnp.bfloat16) if a.dtype == jnp.float32 else a, shard)


def padded(block, sides, width):
    for axis, dim in sides:
        count = lax.axis_size(axis)
        forward = [(i, i + 1) for i in range(count - 1)]
        backward = [(target, source) for source, target in forward]
        low = lax.ppermute(
            lax.slice_in_dim(block, block.shape[dim] - width, None, axis=dim), axis, forward
        )
        high = lax.ppermute(lax.slice_in_dim(block, 0, width, axis=dim), axis, backward)
        block = jnp.concatenate([low, block, high], axis=dim)
    return block


def matmul(left, right):
    return jnp.dot(left, right, preferred_element_type=jnp.float32)


def matmul_left(left, right):
    return lax.dot_general(
        left, right, (((0,), (0,)), ((), ())), preferred_element_type=jnp.float32
    )


def matmul_right(left, right):
    return lax.dot_general(
        left, right, (((1,), (1,)), ((), ())), preferred_element_type=jnp.float32
    )


def silu_slope(field):
    gate_sig = jax.nn.sigmoid(field)
    return gate_sig * (1.0 + field * (1.0 - gate_sig))


def layer_norm(field, gain_row):
    centred = field - jnp.mean(field, -1, keepdims=True)
    inverse = lax.rsqrt(jnp.mean(centred * centred, -1, keepdims=True) + EPS)
    normed = centred * inverse
    return (normed * gain_row, normed, inverse)


def norm_back(upstream, normed, inverse, gain_row):
    scaled = upstream * gain_row
    through = inverse * (
        scaled
        - jnp.mean(scaled, -1, keepdims=True)
        - normed * jnp.mean(scaled * normed, -1, keepdims=True)
    )
    return (through, jnp.sum(upstream * normed, 0))


def rope_tables(position, half_dim):
    freqs = jnp.exp(
        -jnp.log(jnp.float32(ROPE_BASE)) * jnp.arange(half_dim, dtype=jnp.float32) / half_dim
    )
    angles = (position.astype(jnp.float32)[:, None] * freqs[None, :])[:, None, :]
    return (jnp.cos(angles), jnp.sin(angles))


def rotate(field, cosines, sines):
    half_dim = field.shape[-1] // 2
    first = field[..., :half_dim]
    second = field[..., half_dim:]
    return jnp.concatenate([first * cosines - second * sines, second * cosines + first * sines], -1)


def unrotate(field, cosines, sines):
    half_dim = field.shape[-1] // 2
    first = field[..., :half_dim]
    second = field[..., half_dim:]
    return jnp.concatenate([first * cosines + second * sines, second * cosines - first * sines], -1)


def segment_ids(position, long_count, short_count, group_len):
    long_end = long_count * LONG
    short_end = long_end + short_count * SHORT
    segments = jnp.where(
        position < long_end, position // LONG, long_count + (position - long_end) // SHORT
    )
    segments = jnp.where(position < short_end, segments, long_count + short_count)
    return jnp.where((position < 0) | (position >= group_len), -1, segments)


def ffn_forward(stream, gain_row, weight_in, weight_out):
    shaped, normed, inverse = layer_norm(stream, gain_row)
    entered = shaped.astype(jnp.bfloat16)
    pre_act = matmul(entered, weight_in)
    hidden = (pre_act * jax.nn.sigmoid(pre_act)).astype(jnp.bfloat16)
    return (matmul(hidden, weight_out), (normed, inverse, entered, pre_act, hidden))


def ffn_backward(upstream, kept, gain_row, weight_in, weight_out):
    normed, inverse, entered, pre_act, hidden = kept
    grad_branch = (0.5 * upstream).astype(jnp.bfloat16)
    grad_weight_out = matmul_left(hidden, grad_branch)
    grad_pre = (matmul_right(grad_branch, weight_out) * silu_slope(pre_act)).astype(jnp.bfloat16)
    grad_weight_in = matmul_left(entered, grad_pre)
    through, grad_gain = norm_back(matmul_right(grad_pre, weight_in), normed, inverse, gain_row)
    return (upstream + through, grad_gain, grad_weight_in, grad_weight_out)


def block_scores(queries, keys_all, segments, score_scale, begin_row, block_rows):
    query_block = lax.dynamic_slice_in_dim(queries, begin_row, block_rows, 0)
    scores = (
        jnp.einsum("qhd,khd->hqk", query_block, keys_all, preferred_element_type=jnp.float32)
        * score_scale
    )
    same_utt = (
        lax.dynamic_slice_in_dim(segments, begin_row, block_rows, 0)[:, None] == segments[None, :]
    )
    return (jnp.where(same_utt[None], scores, MASKED), query_block)


def attend_forward(queries, keys_all, values_all, segments, score_scale):
    group_len = queries.shape[0]
    block_rows = min(512, group_len)
    starts = jnp.arange(group_len // block_rows, dtype=jnp.int32) * block_rows

    def one_block(begin_row):
        scores = block_scores(queries, keys_all, segments, score_scale, begin_row, block_rows)[0]
        row_max = jnp.max(scores, -1, keepdims=True)
        powers = jnp.exp(scores - row_max)
        row_total = jnp.sum(powers, -1, keepdims=True)
        weights_low = (powers / row_total).astype(jnp.bfloat16)
        context = jnp.einsum(
            "hqk,khd->qhd", weights_low, values_all, preferred_element_type=jnp.float32
        )
        return (context, (row_max + jnp.log(row_total))[..., 0])

    context, log_totals = lax.map(one_block, starts)
    return (context.reshape(group_len, -1), log_totals)


def attend_backward(queries, keys_all, values_all, segments, score_scale, log_totals, grad_context):
    group_len = queries.shape[0]
    block_rows = min(512, group_len)
    starts = jnp.arange(group_len // block_rows, dtype=jnp.int32) * block_rows

    def one_block(carried, element):
        grad_keys, grad_values = carried
        begin_row, log_block = element
        scores, query_block = block_scores(
            queries, keys_all, segments, score_scale, begin_row, block_rows
        )
        weights = jnp.exp(scores - log_block[..., None])
        grad_block = lax.dynamic_slice_in_dim(grad_context, begin_row, block_rows, 0)
        grad_weights = jnp.einsum(
            "qhd,khd->hqk", grad_block, values_all, preferred_element_type=jnp.float32
        )
        grad_scores = (
            weights * (grad_weights - jnp.sum(weights * grad_weights, -1, keepdims=True))
        ).astype(jnp.bfloat16)
        grad_query = (
            jnp.einsum("hqk,khd->qhd", grad_scores, keys_all, preferred_element_type=jnp.float32)
            * score_scale
        )
        grad_keys = (
            grad_keys
            + jnp.einsum(
                "hqk,qhd->khd", grad_scores, query_block, preferred_element_type=jnp.float32
            )
            * score_scale
        )
        grad_values = grad_values + jnp.einsum(
            "hqk,qhd->khd",
            weights.astype(jnp.bfloat16),
            grad_block,
            preferred_element_type=jnp.float32,
        )
        return ((grad_keys, grad_values), grad_query)

    zero_keys = jnp.zeros(keys_all.shape, jnp.float32)
    (grad_keys, grad_values), grad_query = lax.scan(
        one_block, (zero_keys, zero_keys), (starts, log_totals)
    )
    return (grad_query.reshape(keys_all.shape), grad_keys, grad_values)


def spread_end(gradients):
    row_shares = jax.tree.map(
        lambda part: part.astype(jnp.float32),
        lax.psum_scatter(shortened(gradients), "heads", scatter_dimension=0, tiled=True),
    )
    return jax.tree.map(
        lambda part: part.astype(jnp.float32),
        lax.psum_scatter(shortened(row_shares), "items", scatter_dimension=1, tiled=True),
    )


def body(
    frames,
    cotangent,
    bucket_counts,
    gains,
    w_ffn1_in,
    w_ffn1_out,
    w_qkv,
    w_out,
    w_point_in,
    w_depth,
    w_point_out,
    w_ffn2_in,
    w_ffn2_out,
):
    batches, frames_here, model_width = frames.shape
    head_ways = lax.axis_size("heads")
    group_len = frames_here * head_ways
    heads_here = HEADS // head_ways
    head_size = model_width // HEADS
    score_scale = head_size ** (-0.5)
    reach_half = (KERNEL - 1) // 2
    first_frame = lax.axis_index("heads") * frames_here
    own_position = first_frame + jnp.arange(frames_here, dtype=jnp.int32)
    cosines, sines = rope_tables(own_position, head_size // 2)
    frame_heads = (frames_here, HEADS, head_size)
    depth_rows = w_depth.astype(jnp.float32)
    outputs = []
    input_grads = []
    big_total = None
    small_total = None
    for number in range(batches):
        stream = frames[number].astype(jnp.float32)
        long_count = bucket_counts[number, 0, 0]
        short_count = bucket_counts[number, 0, 1]
        wide_position = (
            first_frame - reach_half + jnp.arange(frames_here + 2 * reach_half, dtype=jnp.int32)
        )
        seg_wide = segment_ids(wide_position, long_count, short_count, group_len)
        seg_own = seg_wide[reach_half : reach_half + frames_here]
        seg_group = segment_ids(
            jnp.arange(group_len, dtype=jnp.int32), long_count, short_count, group_len
        )
        branch_one, keep_one = ffn_forward(stream, gains[0], w_ffn1_in, w_ffn1_out)
        stream_one = stream + 0.5 * branch_one
        shaped, att_normed, att_inverse = layer_norm(stream_one, gains[1])
        att_entered = shaped.astype(jnp.bfloat16)
        projected = matmul(att_entered, w_qkv)
        rot_query = (
            rotate(projected[:, :model_width].reshape(frame_heads), cosines, sines)
            .reshape(frames_here, model_width)
            .astype(jnp.bfloat16)
        )
        rot_keys = (
            rotate(projected[:, model_width : 2 * model_width].reshape(frame_heads), cosines, sines)
            .reshape(frames_here, model_width)
            .astype(jnp.bfloat16)
        )
        plain_values = projected[:, 2 * model_width :].astype(jnp.bfloat16)
        queries, keys_all, values_all = (
            lax.all_to_all(rot_query, "heads", split_axis=1, concat_axis=0, tiled=True),
            lax.all_to_all(rot_keys, "heads", split_axis=1, concat_axis=0, tiled=True),
            lax.all_to_all(plain_values, "heads", split_axis=1, concat_axis=0, tiled=True),
        )
        head_shape = (group_len, heads_here, head_size)
        queries = queries.reshape(head_shape)
        keys_all = keys_all.reshape(head_shape)
        values_all = values_all.reshape(head_shape)
        context_heads, log_totals = attend_forward(
            queries, keys_all, values_all, seg_group, score_scale
        )
        context = lax.all_to_all(
            context_heads.astype(jnp.bfloat16), "heads", split_axis=0, concat_axis=1, tiled=True
        )
        stream_two = stream_one + matmul(context, w_out)
        shaped, conv_normed, conv_inverse = layer_norm(stream_two, gains[2])
        conv_entered = shaped.astype(jnp.bfloat16)
        pointwise = matmul(conv_entered, w_point_in)
        linear = pointwise[:, :model_width]
        sigmoid_gate = jax.nn.sigmoid(pointwise[:, model_width:])
        gated_low = (linear * sigmoid_gate).astype(jnp.bfloat16)
        widened = padded(gated_low, (("heads", 0),), reach_half)
        depth_out = jnp.zeros((frames_here, model_width), jnp.float32)
        for offset in range(KERNEL):
            same_fwd = (seg_wide[offset : offset + frames_here] == seg_own)[:, None]
            depth_out = depth_out + depth_rows[offset] * jnp.where(
                same_fwd, widened[offset : offset + frames_here], 0.0
            )
        depth_shaped, depth_normed, depth_inverse = layer_norm(depth_out, gains[3])
        mixed_low = (depth_shaped * jax.nn.sigmoid(depth_shaped)).astype(jnp.bfloat16)
        stream_three = stream_two + matmul(mixed_low, w_point_out)
        branch_two, keep_two = ffn_forward(stream_three, gains[4], w_ffn2_in, w_ffn2_out)
        stream_four = stream_three + 0.5 * branch_two
        shaped, final_normed, final_inverse = layer_norm(stream_four, gains[5])
        outputs.append(shaped.astype(jnp.bfloat16))
        grad_four, gain_five = norm_back(
            cotangent[number].astype(jnp.float32), final_normed, final_inverse, gains[5]
        )
        grad_three, gain_four, grad_f2_in, grad_f2_out = ffn_backward(
            grad_four, keep_two, gains[4], w_ffn2_in, w_ffn2_out
        )
        grad_mix = grad_three.astype(jnp.bfloat16)
        grad_point_out = matmul_left(mixed_low, grad_mix)
        grad_norm_in = matmul_right(grad_mix, w_point_out) * silu_slope(depth_shaped)
        grad_depth, gain_three = norm_back(grad_norm_in, depth_normed, depth_inverse, gains[3])
        grad_depth_low = grad_depth.astype(jnp.bfloat16)
        grad_widened = padded(grad_depth_low, (("heads", 0),), reach_half)
        grad_depth_full = grad_depth_low.astype(jnp.float32)
        tap_grads = []
        grad_gated = jnp.zeros((frames_here, model_width), jnp.float32)
        for offset in range(KERNEL):
            same_fwd = (seg_wide[offset : offset + frames_here] == seg_own)[:, None]
            tap_grads.append(
                jnp.sum(
                    jnp.where(
                        same_fwd, grad_depth_full * widened[offset : offset + frames_here], 0.0
                    ),
                    0,
                )
            )
            mirror = 2 * reach_half - offset
            same_back = (seg_wide[mirror : mirror + frames_here] == seg_own)[:, None]
            grad_gated = grad_gated + depth_rows[offset] * jnp.where(
                same_back, grad_widened[mirror : mirror + frames_here], 0.0
            )
        grad_point = jnp.concatenate(
            [grad_gated * sigmoid_gate, grad_gated * linear * sigmoid_gate * (1.0 - sigmoid_gate)],
            1,
        ).astype(jnp.bfloat16)
        grad_point_in = matmul_left(conv_entered, grad_point)
        through, gain_two = norm_back(
            matmul_right(grad_point, w_point_in), conv_normed, conv_inverse, gains[2]
        )
        grad_two = grad_three + through
        grad_attn_out = grad_two.astype(jnp.bfloat16)
        grad_out_proj = matmul_left(context, grad_attn_out)
        grad_context = matmul_right(grad_attn_out, w_out).astype(jnp.bfloat16)
        grad_context_heads = lax.all_to_all(
            grad_context, "heads", split_axis=1, concat_axis=0, tiled=True
        ).reshape(head_shape)
        grad_query, grad_keys, grad_values = attend_backward(
            queries, keys_all, values_all, seg_group, score_scale, log_totals, grad_context_heads
        )
        flat_shape = (group_len, heads_here * head_size)
        back_query, back_keys, back_values = (
            lax.all_to_all(
                grad_query.astype(jnp.bfloat16).reshape(flat_shape),
                "heads",
                split_axis=0,
                concat_axis=1,
                tiled=True,
            ),
            lax.all_to_all(
                grad_keys.astype(jnp.bfloat16).reshape(flat_shape),
                "heads",
                split_axis=0,
                concat_axis=1,
                tiled=True,
            ),
            lax.all_to_all(
                grad_values.astype(jnp.bfloat16).reshape(flat_shape),
                "heads",
                split_axis=0,
                concat_axis=1,
                tiled=True,
            ),
        )
        plain_query = (
            unrotate(back_query.astype(jnp.float32).reshape(frame_heads), cosines, sines)
            .reshape(frames_here, model_width)
            .astype(jnp.bfloat16)
        )
        plain_keys = (
            unrotate(back_keys.astype(jnp.float32).reshape(frame_heads), cosines, sines)
            .reshape(frames_here, model_width)
            .astype(jnp.bfloat16)
        )
        grad_qkv = jnp.concatenate([plain_query, plain_keys, back_values], 1)
        grad_qkv_proj = matmul_left(att_entered, grad_qkv)
        through, gain_one = norm_back(
            matmul_right(grad_qkv, w_qkv), att_normed, att_inverse, gains[1]
        )
        grad_one = grad_two + through
        grad_zero, gain_zero, grad_f1_in, grad_f1_out = ffn_backward(
            grad_one, keep_one, gains[0], w_ffn1_in, w_ffn1_out
        )
        input_grads.append(grad_zero.astype(jnp.bfloat16))
        big_now = (
            grad_f1_in,
            grad_f1_out,
            grad_qkv_proj,
            grad_out_proj,
            grad_point_in,
            grad_point_out,
            grad_f2_in,
            grad_f2_out,
        )
        small_now = (
            jnp.stack([gain_zero, gain_one, gain_two, gain_three, gain_four, gain_five], 0),
            jnp.stack(tap_grads, 0),
        )
        big_total = big_now if big_total is None else jax.tree.map(jnp.add, big_total, big_now)
        small_total = (
            small_now if small_total is None else jax.tree.map(jnp.add, small_total, small_now)
        )
    big_total = spread_end(big_total)
    gains_total, depth_total = lax.psum(small_total, ("items", "heads"))
    return (
        jnp.stack(outputs, 0),
        jnp.stack(input_grads, 0),
        gains_total,
        big_total[0],
        big_total[1],
        big_total[2],
        big_total[3],
        big_total[4],
        depth_total,
        big_total[5],
        big_total[6],
        big_total[7],
    )


def solution(mesh):
    in_specs = (
        P(None, ("items", "heads"), None),
        P(None, ("items", "heads"), None),
        P(None, "items", None),
        P(),
        P(),
        P(),
        P(),
        P(),
        P(),
        P(),
        P(),
        P(),
        P(),
    )
    out_specs = (
        P(None, ("items", "heads"), None),
        P(None, ("items", "heads"), None),
        P(),
        P("heads", "items"),
        P("heads", "items"),
        P("heads", "items"),
        P("heads", "items"),
        P("heads", "items"),
        P(),
        P("heads", "items"),
        P("heads", "items"),
        P("heads", "items"),
    )
    return jax.shard_map(body, mesh=mesh, in_specs=in_specs, out_specs=out_specs, check_vma=False)
```

profile of v0, /device:TPU:0, one launch (start us, length us, event | category | flops | bytes accessed | tf_op | source)
XLA Modules:
  0.0 1454.8 jit_solution(2923734315898820828)
XLA Ops:
  12.3 6.1 fusion.248
  31.5 6.0 fusion.245
  37.4 7.4 fusion.276
  59.4 6.3 all-to-all-start.5
  67.7 13.5 all-to-all-done.5
  86.7 13.2 all-to-all-done.4
  105.9 13.5 all-to-all-done.6
  162.7 48.6 %while.55 = (s32[]{:T(128)}, bf16[4,512,2,64]{1,3,2,0:T(8,128)(2,1)}, f32[4,2,512]{2,1,0:T(2,128)S(1)}, s32[4]{0:T(128)S(1)}, s32[2048]{0:T(1024)S(1)}, /*index=...) while((s32[]{:T(128)}, ...), condition=%wide.region_23.24_spmd, body=%wide.region_20.23_spmd.sunk | while | flops 563084288 | bytes 30849704 | solution.py:150
  225.5 5.2 all-to-all-start.7
  235.1 48.6 %while.54 = (s32[]{:T(128)}, bf16[4,512,2,64]{1,3,2,0:T(8,128)(2,1)}, f32[4,2,512]{2,1,0:T(2,128)S(1)}, s32[4]{0:T(128)S(1)}, s32[2048]{0:T(1024)S(1)}, /*index=...) while((s32[]{:T(128)}, ...), condition=%wide.region_7.8_spmd, body=%wide.region_4.7_spmd.sunk | while | flops 563084288 | bytes 30849704 | solution.py:150
  339.5 6.5 fusion.72
  346.0 7.4 multiply_reduce_fusion.6
  353.4 10.4 fusion.74
  363.8 6.8 fusion.284
  426.8 8.9 all-to-all-done.12
  443.4 110.7 %while.57 = (s32[]{:T(128)}, f32[2048,2,64]{0,2,1:T(8,128)S(1)}, f32[2048,2,64]{0,2,1:T(8,128)}, bf16[4,512,2,64]{1,3,2,0:T(8,128)(2,1)}, s32[4]{0:T(128)S(1)}, ...) while((s32[]{:T(128)}, f32[2048,2,64]{0,2,1:T(8,128)S(1)}, ...), condition=%wide.region_57.58_spmd.clone, body=%wide.region_55.57_spmd.clone.sunk | while | flops 1376058368 | bytes 140815120 | solution.py:193
  571.5 5.6 all-to-all-done.13
  582.3 111.0 %while.56 = (s32[]{:T(128)}, f32[2048,2,64]{0,2,1:T(8,128)S(1)}, f32[2048,2,64]{0,2,1:T(8,128)}, bf16[4,512,2,64]{1,3,2,0:T(8,128)(2,1)}, s32[4]{0:T(128)S(1)}, ...) while((s32[]{:T(128)}, f32[2048,2,64]{0,2,1:T(8,128)S(1)}, ...), condition=%wide.region_42.43_spmd.clone, body=%wide.region_40.42_spmd.clone.sunk | while | flops 1376058368 | bytes 140815120 | solution.py:193
  701.8 14.3 all-to-all-done.9
  721.9 13.0 all-to-all-done.10
  747.0 8.0 all-to-all-done.11
  761.6 7.9 fusion.166
  775.3 9.4 add_convert_fusion.4
  785.9 11.1 fusion.200
  797.1 11.1 add_convert_fusion
  809.4 10.1 fusion.252
  819.5 11.8 add_convert_fusion.1
  832.8 5.3 multiply_reduce_fusion.9
  838.2 5.3 multiply_reduce_fusion.5
  846.5 8.3 fusion.201
  854.8 13.9 add_convert_fusion.2
  869.9 7.4 fusion.73
  877.4 8.3 fusion.243
  885.8 6.3 fusion.75
  893.5 11.8 add_convert_fusion.3
  908.1 35.7 %reduce-scatter.45.cloned.1.call-done = bf16[512,1024]{1,0:T(8,128)(2,1)} async-done(((bf16[4096,1024]{1,0:T(8,128)(2,1)}), bf16[512,1024]{1,0:T(8,128)(2,1)}) %reduce-scatter.45.cloned.1.call-update) | async-done | bytes 1048592 | tf_op jit(solution)/shard_map/reduce_scatter | solution.py:202
  943.8 90.1 %reduce-scatter.41.cloned.1.call-done = bf16[128,4096]{1,0:T(8,128)(2,1)} async-done(((bf16[1024,4096]{1,0:T(8,128)(2,1)}), bf16[128,4096]{1,0:T(8,128)(2,1)}) %reduce-scatter.41.cloned.1.call-update) | async-done | bytes 1048592 | tf_op jit(solution)/shard_map/reduce_scatter | solution.py:202
  1034.0 90.2 %reduce-scatter.21.cloned.1.call-done = bf16[512,1024]{1,0:T(8,128)(2,1)} async-done(((bf16[4096,1024]{1,0:T(8,128)(2,1)}), bf16[512,1024]{1,0:T(8,128)(2,1)}) %reduce-scatter.21.cloned.1.call-update) | async-done | bytes 1048592 | tf_op jit(solution)/shard_map/reduce_scatter | solution.py:202
  1125.8 7.6 fusion.285
  1133.4 81.1 %reduce-scatter.17.cloned.1.call-done = bf16[128,4096]{1,0:T(8,128)(2,1)} async-done(((bf16[1024,4096]{1,0:T(8,128)(2,1)}), bf16[128,4096]{1,0:T(8,128)(2,1)}) %reduce-scatter.17.cloned.1.call-update) | async-done | bytes 1048592 | tf_op jit(solution)/shard_map/reduce_scatter | solution.py:202
  1214.6 7.3 fusion.116
  1222.1 38.7 %all-reduce = (f32[6,1024]{1,0:T(8,128)}, f32[5,1024]{1,0:T(8,128)}) all-reduce(f32[6,1024]{1,0:T(8,128)S(1)} %add.549, f32[5,1024]{1,0:T(8,128)S(1)} %add.555), channel_id=1, replica_groups=mesh['items'=4,'heads'=8] {'items','heads'}, use_global_device_ids=true, to_apply=%region_74.75 | all-reduce | flops 11264 | bytes 90112 | tf_op jit(solution)/shard_map/psum | solution.py:416
  1268.1 26.1 %reduce-scatter.35.cloned.1.call-done = bf16[128,512]{1,0:T(8,128)(2,1)} async-done(((bf16[128,2048]{1,0:T(8,128)(2,1)}), bf16[128,512]{1,0:T(8,128)(2,1)}) %reduce-scatter.35.cloned.1.call-update) | async-done | bytes 131088 | tf_op jit(solution)/shard_map/reduce_scatter | solution.py:206
  1295.9 27.5 %reduce-scatter.27.cloned.1.call-done = bf16[128,768]{1,0:T(8,128)(2,1)} async-done(((bf16[128,3072]{1,0:T(8,128)(2,1)}), bf16[128,768]{1,0:T(8,128)(2,1)}) %reduce-scatter.27.cloned.1.call-update) | async-done | bytes 196624 | tf_op jit(solution)/shard_map/reduce_scatter | solution.py:206
  1325.1 29.2 %reduce-scatter.47.cloned.1.call-done = bf16[512,256]{1,0:T(8,128)(2,1)} async-done(((bf16[512,1024]{1,0:T(8,128)(2,1)}), bf16[512,256]{1,0:T(8,128)(2,1)}) %reduce-scatter.47.cloned.1.call-update) | async-done | bytes 262160 | tf_op jit(solution)/shard_map/reduce_scatter | solution.py:206
  1356.1 28.7 %reduce-scatter.43.cloned.1.call-done = bf16[128,1024]{1,0:T(8,128)(2,1)} async-done(((bf16[128,4096]{1,0:T(8,128)(2,1)}), bf16[128,1024]{1,0:T(8,128)(2,1)}) %reduce-scatter.43.cloned.1.call-update) | async-done | bytes 262160 | tf_op jit(solution)/shard_map/reduce_scatter | solution.py:206
  1386.6 29.0 %reduce-scatter.23.cloned.1.call-done = bf16[512,256]{1,0:T(8,128)(2,1)} async-done(((bf16[512,1024]{1,0:T(8,128)(2,1)}), bf16[512,256]{1,0:T(8,128)(2,1)}) %reduce-scatter.23.cloned.1.call-update) | async-done | bytes 262160 | tf_op jit(solution)/shard_map/reduce_scatter | solution.py:206
  1417.3 28.7 %reduce-scatter.19.cloned.1.call-done = bf16[128,1024]{1,0:T(8,128)(2,1)} async-done(((bf16[128,4096]{1,0:T(8,128)(2,1)}), bf16[128,1024]{1,0:T(8,128)(2,1)}) %reduce-scatter.19.cloned.1.call-update) | async-done | bytes 262160 | tf_op jit(solution)/shard_map/reduce_scatter | solution.py:206
  (871 shorter events, 600.4 us)
Async XLA Ops:
  7.2 314.0 %copy-start = (bf16[1024,1024]{1,0:T(8,128)(2,1)S(1)}, bf16[1024,1024]{1,0:T(8,128)(2,1)}, u32[]{:S(2)}) copy-start(bf16[1024,1024]{1,0:T(8,128)(2,1)} %param.31) | copy-start | bytes 6291460
  59.4 21.7 %all-to-all-start.5 = ((bf16[256,8,128]{0,2,1:T(8,128)(2,1)}), bf16[256,8,128]{0,2,1:T(8,128)(2,1)S(1)}, u32[]{:S(2)}, u32[]{:S(2)}) async-start(bf16[256,8,128]{0,2,1:T(8,128)(2,1)} %bitcast.39), calls=%async_computation.5 | async-start | bytes 1048576 | tf_op jit(solution)/shard_map/all_to_all | solution.py:271
  81.1 18.8 %all-to-all-start.4 = ((bf16[256,8,128]{0,2,1:T(8,128)(2,1)}), bf16[256,8,128]{0,2,1:T(8,128)(2,1)S(1)}, u32[]{:S(2)}, u32[]{:S(2)}) async-start(bf16[256,8,128]{0,2,1:T(8,128)(2,1)} %bitcast.457), calls=%async_computation.4 | async-start | bytes 1048576 | tf_op jit(solution)/shard_map/all_to_all | solution.py:270
  99.9 19.5 %all-to-all-start.6 = ((bf16[256,8,128]{2,0,1:T(8,128)(2,1)}), bf16[256,8,128]{2,0,1:T(8,128)(2,1)}, u32[]{:S(2)}, u32[]{:S(2)}) async-start(bf16[256,8,128]{2,0,1:T(8,128)(2,1)} %copy_bitcast_fusion.2), calls=%async_computation.6 | async-start | bytes 1048576 | tf_op jit(solution)/shard_map/all_to_all | solution.py:272
  119.4 18.8 %all-to-all-start.1 = ((bf16[256,8,128]{0,2,1:T(8,128)(2,1)}), bf16[256,8,128]{0,2,1:T(8,128)(2,1)S(1)}, u32[]{:S(2)}, u32[]{:S(2)}) async-start(bf16[256,8,128]{0,2,1:T(8,128)(2,1)} %bitcast.454), calls=%async_computation.1 | async-start | bytes 1048576 | tf_op jit(solution)/shard_map/all_to_all | solution.py:271
  138.2 19.5 %all-to-all-start = ((bf16[256,8,128]{0,2,1:T(8,128)(2,1)}), bf16[256,8,128]{0,2,1:T(8,128)(2,1)}, u32[]{:S(2)}, u32[]{:S(2)}) async-start(bf16[256,8,128]{0,2,1:T(8,128)(2,1)} %bitcast.455), calls=%async_computation | async-start | bytes 1048576 | tf_op jit(solution)/shard_map/all_to_all | solution.py:270
  157.7 67.8 %all-to-all-start.2 = ((bf16[256,8,128]{2,0,1:T(8,128)(2,1)}), bf16[256,8,128]{2,0,1:T(8,128)(2,1)}, u32[]{:S(2)}, u32[]{:S(2)}) async-start(bf16[256,8,128]{2,0,1:T(8,128)(2,1)} %copy_bitcast_fusion.3), calls=%async_computation.2 | async-start | bytes 1048576 | tf_op jit(solution)/shard_map/all_to_all | solution.py:272
  225.5 64.8 %all-to-all-start.7 = ((bf16[8,256,128]{1,2,0:T(8,128)(2,1)}), bf16[8,256,128]{1,2,0:T(8,128)(2,1)}, u32[]{:S(2)}, u32[]{:S(2)}) async-start(bf16[8,256,128]{1,2,0:T(8,128)(2,1)} %copy.120), calls=%async_computation.7 | async-start | bytes 1048576 | tf_op jit(solution)/shard_map/all_to_all | solution.py:281
  290.3 20.6 %all-to-all-start.3 = ((bf16[8,256,128]{1,2,0:T(8,128)(2,1)}), bf16[8,256,128]{1,2,0:T(8,128)(2,1)}, u32[]{:S(2)}, u32[]{:S(2)}) async-start(bf16[8,256,128]{1,2,0:T(8,128)(2,1)} %copy.112), calls=%async_computation.3 | async-start | bytes 1048576 | tf_op jit(solution)/shard_map/all_to_all | solution.py:281
  295.4 610.1 %reduce-scatter.37.cloned.1.call-start = ((), (), s32[]{:S(2)}) async-start(), calls=%async_computation.42 | async-start | bytes 2359296 | tf_op jit(solution)/shard_map/reduce_scatter | solution.py:202
  302.2 16.8 %collective-permute-start.2 = (bf16[2,1024]{1,0:T(2,128)(2,1)S(1)}, bf16[2,1024]{1,0:T(2,128)(2,1)S(1)}, u32[]{:S(2)}, u32[]{:S(2)}) collective-permute-start(bf16[2,1024]{1,0:T(2,128)(2,1)S(1)} %get-tuple-element.522), channel_id=1, source_target_pairs={{0,1},{1,2},{2,3},{3,4},{4,5},{5,6},{6,7},{8,9},{9,10},{10,11},{11... | collective-permute-start | bytes 12296 | tf_op jit(solution)/shard_map/ppermute | solution.py:26
  304.6 14.4 collective-permute-start.3
  315.7 12.4 collective-permute-start
  317.5 10.6 collective-permute-start.1
  387.3 14.0 collective-permute-start.4
  388.6 12.7 collective-permute-start.5
  395.4 10.4 collective-permute-start.6
  396.9 8.9 collective-permute-start.7
  415.9 19.9 %all-to-all-start.12 = ((bf16[256,8,128]{2,0,1:T(8,128)(2,1)}), bf16[256,8,128]{2,0,1:T(8,128)(2,1)}, u32[]{:S(2)}, u32[]{:S(2)}) async-start(bf16[256,8,128]{2,0,1:T(8,128)(2,1)} %bitcast.456), calls=%async_computation.12 | async-start | bytes 1048576 | tf_op jit(solution)/shard_map/all_to_all | solution.py:347
  420.2 486.0 %reduce-scatter.29.cloned.1.call-start = ((), (), s32[]{:S(2)}) async-start(), calls=%async_computation.38 | async-start | bytes 2359296 | tf_op jit(solution)/shard_map/reduce_scatter | solution.py:202
  435.7 120.9 %all-to-all-start.8 = ((bf16[256,8,128]{2,0,1:T(8,128)(2,1)}), bf16[256,8,128]{2,0,1:T(8,128)(2,1)}, u32[]{:S(2)}, u32[]{:S(2)}) async-start(bf16[256,8,128]{2,0,1:T(8,128)(2,1)} %bitcast.366), calls=%async_computation.8 | async-start | bytes 1048576 | tf_op jit(solution)/shard_map/all_to_all | solution.py:347
  556.6 20.5 %all-to-all-start.13 = ((bf16[8,256,128]{1,2,0:T(8,128)(2,1)}), bf16[8,256,128]{1,2,0:T(8,128)(2,1)}, u32[]{:S(2)}, u32[]{:S(2)}) async-start(bf16[8,256,128]{1,2,0:T(8,128)(2,1)} %copy.130), calls=%async_computation.13 | async-start | bytes 1048576 | tf_op jit(solution)/shard_map/all_to_all | solution.py:355
  561.7 345.1 %reduce-scatter.33.cloned.1.call-start = ((), (), s32[]{:S(2)}) async-start(), calls=%async_computation.40 | async-start | bytes 4718592 | tf_op jit(solution)/shard_map/reduce_scatter | solution.py:202
  577.1 118.7 %all-to-all-start.14 = ((bf16[8,256,128]{1,2,0:T(8,128)(2,1)}), bf16[8,256,128]{1,2,0:T(8,128)(2,1)}, u32[]{:S(2)}, u32[]{:S(2)}) async-start(bf16[8,256,128]{1,2,0:T(8,128)(2,1)} %copy.131), calls=%async_computation.14 | async-start | bytes 1048576 | tf_op jit(solution)/shard_map/all_to_all | solution.py:362
  695.8 20.3 %all-to-all-start.9 = ((bf16[8,256,128]{1,2,0:T(8,128)(2,1)}), bf16[8,256,128]{1,2,0:T(8,128)(2,1)S(1)}, u32[]{:S(2)}, u32[]{:S(2)}) async-start(bf16[8,256,128]{1,2,0:T(8,128)(2,1)} %copy.124), calls=%async_computation.9 | async-start | bytes 1048576 | tf_op jit(solution)/shard_map/all_to_all | solution.py:355
  716.1 18.8 %all-to-all-start.10 = ((bf16[8,256,128]{1,2,0:T(8,128)(2,1)}), bf16[8,256,128]{1,2,0:T(8,128)(2,1)S(1)}, u32[]{:S(2)}, u32[]{:S(2)}) async-start(bf16[8,256,128]{1,2,0:T(8,128)(2,1)} %copy.125), calls=%async_computation.10 | async-start | bytes 1048576 | tf_op jit(solution)/shard_map/all_to_all | solution.py:362
  735.7 19.2 %all-to-all-start.11 = ((bf16[8,256,128]{1,2,0:T(8,128)(2,1)}), bf16[8,256,128]{1,2,0:T(8,128)(2,1)S(1)}, u32[]{:S(2)}, u32[]{:S(2)}) async-start(bf16[8,256,128]{1,2,0:T(8,128)(2,1)} %copy.126), calls=%async_computation.11 | async-start | bytes 1048576 | tf_op jit(solution)/shard_map/all_to_all | solution.py:369
  755.7 18.8 %all-to-all-start.15 = ((bf16[8,256,128]{1,2,0:T(8,128)(2,1)}), bf16[8,256,128]{1,2,0:T(8,128)(2,1)S(1)}, u32[]{:S(2)}, u32[]{:S(2)}) async-start(bf16[8,256,128]{1,2,0:T(8,128)(2,1)} %copy.132), calls=%async_computation.15 | async-start | bytes 1048576 | tf_op jit(solution)/shard_map/all_to_all | solution.py:369
  759.2 148.3 %reduce-scatter.25.cloned.1.call-start = ((), (), s32[]{:S(2)}) async-start(), calls=%async_computation.36 | async-start | bytes 7077888 | tf_op jit(solution)/shard_map/reduce_scatter | solution.py:202
  784.8 159.0 %reduce-scatter.45.cloned.1.call-start = ((), (), s32[]{:S(2)}) async-start(), calls=%async_computation.46 | async-start | bytes 9437184 | tf_op jit(solution)/shard_map/reduce_scatter | solution.py:202
  808.2 225.7 %reduce-scatter.41.cloned.1.call-start = ((), (), s32[]{:S(2)}) async-start(), calls=%async_computation.44 | async-start | bytes 9437184 | tf_op jit(solution)/shard_map/reduce_scatter | solution.py:202
  831.3 292.9 %reduce-scatter.21.cloned.1.call-start = ((), (), s32[]{:S(2)}) async-start(), calls=%async_computation.34 | async-start | bytes 9437184 | tf_op jit(solution)/shard_map/reduce_scatter | solution.py:202
  868.8 345.7 %reduce-scatter.17.cloned.1.call-start = ((), (), s32[]{:S(2)}) async-start(), calls=%async_computation.32 | async-start | bytes 9437184 | tf_op jit(solution)/shard_map/reduce_scatter | solution.py:202
  905.3 219.3 %copy-start.152 = (f32[1024]{0:T(1024)S(1)}, f32[1024]{0:T(1024)}, u32[]{:S(2)}) copy-start(f32[1024]{0:T(1024)} %get-tuple-element.380) | copy-start | bytes 12292
  905.3 219.3 %copy-start.153 = (f32[1024]{0:T(1024)S(1)}, f32[1024]{0:T(1024)}, u32[]{:S(2)}) copy-start(f32[1024]{0:T(1024)} %get-tuple-element.381) | copy-start | bytes 12292
  905.4 219.3 %copy-start.154 = (f32[1024]{0:T(1024)S(1)}, f32[1024]{0:T(1024)}, u32[]{:S(2)}) copy-start(f32[1024]{0:T(1024)} %get-tuple-element.387) | copy-start | bytes 12292
  905.4 219.3 %copy-start.155 = (f32[1024]{0:T(1024)S(1)}, f32[1024]{0:T(1024)}, u32[]{:S(2)}) copy-start(f32[1024]{0:T(1024)} %get-tuple-element.388) | copy-start | bytes 12292
  905.4 219.3 %copy-start.156 = (f32[1024]{0:T(1024)S(1)}, f32[1024]{0:T(1024)}, u32[]{:S(2)}) copy-start(f32[1024]{0:T(1024)} %get-tuple-element.389) | copy-start | bytes 12292
  905.4 219.3 %copy-start.93 = (bf16[1,256,1024]{2,1,0:T(8,128)(2,1)S(1)}, bf16[1,256,1024]{2,1,0:T(8,128)(2,1)}, u32[]{:S(2)}) copy-start(bf16[1,256,1024]{2,1,0:T(8,128)(2,1)} %get-tuple-element.511) | copy-start | bytes 1572868
  905.4 219.3 %copy-start.94 = (bf16[1,256,1024]{2,1,0:T(8,128)(2,1)S(1)}, bf16[1,256,1024]{2,1,0:T(8,128)(2,1)}, u32[]{:S(2)}) copy-start(bf16[1,256,1024]{2,1,0:T(8,128)(2,1)} %get-tuple-element.513) | copy-start | bytes 1572868
  905.4 359.6 %reduce-scatter.39.cloned.1.call-start = ((), (), s32[]{:S(2)}) async-start(), calls=%async_computation.43 | async-start | bytes 327680 | tf_op jit(solution)/shard_map/reduce_scatter | solution.py:206
  906.1 360.5 %reduce-scatter.31.cloned.1.call-start = ((), (), s32[]{:S(2)}) async-start(), calls=%async_computation.39 | async-start | bytes 327680 | tf_op jit(solution)/shard_map/reduce_scatter | solution.py:206
  906.7 387.5 %reduce-scatter.35.cloned.1.call-start = ((), (), s32[]{:S(2)}) async-start(), calls=%async_computation.41 | async-start | bytes 655360 | tf_op jit(solution)/shard_map/reduce_scatter | solution.py:206
  907.5 415.9 %reduce-scatter.27.cloned.1.call-start = ((), (), s32[]{:S(2)}) async-start(), calls=%async_computation.37 | async-start | bytes 983040 | tf_op jit(solution)/shard_map/reduce_scatter | solution.py:206
  908.0 446.3 %reduce-scatter.47.cloned.1.call-start = ((), (), s32[]{:S(2)}) async-start(), calls=%async_computation.47 | async-start | bytes 1310720 | tf_op jit(solution)/shard_map/reduce_scatter | solution.py:206
  943.8 441.0 %reduce-scatter.43.cloned.1.call-start = ((), (), s32[]{:S(2)}) async-start(), calls=%async_computation.45 | async-start | bytes 1310720 | tf_op jit(solution)/shard_map/reduce_scatter | solution.py:206
  1033.9 381.6 %reduce-scatter.23.cloned.1.call-start = ((), (), s32[]{:S(2)}) async-start(), calls=%async_computation.35 | async-start | bytes 1310720 | tf_op jit(solution)/shard_map/reduce_scatter | solution.py:206
  1124.2 321.9 %reduce-scatter.19.cloned.1.call-start = ((), (), s32[]{:S(2)}) async-start(), calls=%async_computation.33 | async-start | bytes 1310720 | tf_op jit(solution)/shard_map/reduce_scatter | solution.py:206
  (216 other events, 3586.1 us)
Sparse Core Ops, SparseCore 0:
  380.3 37.3 reduce-scatter.36
  426.9 42.5 reduce-scatter.28
  568.1 59.8 reduce-scatter.32
  784.8 68.7 reduce-scatter.24
  855.8 87.9 reduce-scatter.44
  945.9 87.9 reduce-scatter.40
  1036.2 87.9 reduce-scatter.20
  1126.5 87.9 reduce-scatter.16
  1217.2 22.3 reduce-scatter.38
  1242.5 24.1 reduce-scatter.30
  1269.5 24.7 reduce-scatter.34
  1297.3 26.0 reduce-scatter.26
  1326.6 27.7 reduce-scatter.46
  1357.1 27.7 reduce-scatter.42
  1387.8 27.7 reduce-scatter.22
  1418.3 27.7 reduce-scatter.18
where the time goes:
time: 1470 us; the launch traced here: 1450 us
  waiting for transfers between devices  577 us (39%)
  matrix products  457 us (31%)
  other arithmetic  132 us (9%)
  local copies, waits for them, and re-layouts  107 us (7%)
  starting transfers between devices  89.1 us (6%)
  blocking collectives  38.7 us (3%)
  loops' own time  31.6 us (2%)
  between operations  22.9 us (2%)
    reduce_scatter x8, waiting for transfers between devices, spread_end(): lax.psum_scatter(shortened(gradients), 'heads', scatter_dimension=0, tile...  297 us
    reduce_scatter x8, waiting for transfers between devices, spread_end(): lax.psum_scatter(shortened(row_shares), 'items', scatter_dimension=1, til...  169 us
    dot_general x16, matrix products, matmul_left(): lax.dot_general(left, right, (((0,), (0,)), ((), ())), preferred_element_...  118 us
    dot_general x16, matrix products, matmul_right(): lax.dot_general(left, right, (((1,), (1,)), ((), ())), preferred_element_...  83.5 us
    dot_general x16, matrix products, matmul(): return jnp.dot(left, right, preferred_element_type=jnp.float32)  46.6 us
    dot_general x16, matrix products, block_scores(): jnp.einsum('qhd,khd->hqk', query_block, keys_all, preferred_element_type=...  42.8 us
    dot_general x8, matrix products, one_block(): jnp.einsum('hqk,qhd->khd', weights.astype(jnp.bfloat16), grad_block, pref...  38.8 us
    psum x1, blocking collectives, body(): gains_total, depth_total = lax.psum(small_total, ('items', 'heads'))  38.7 us
  transfers between devices with their start and end apart: 40, of which 23 were waited for; matrix products, arithmetic and copies ran while one was open for 39% of the time, Pallas kernels for 0%

commit v1 on v0

v1 whole, which is shorter than its diff:
```python
import functools

import jax
import jax.numpy as jnp
from jax import lax
from jax.experimental import pallas as pl
from jax.experimental.pallas import tpu as pltpu
from jax.sharding import PartitionSpec as P

HEADS = 16
KERNEL = 5
LONG = 1500
SHORT = 500
EPS = 1e-05
ROPE_BASE = 10000.0
BLOCK = 256
LANES = 128
BIG = 1e30
VMEM_LIMIT = 56 << 20
F32 = jnp.float32
BF16 = jnp.bfloat16
NN = (((1,), (0,)), ((), ()))
NT = (((1,), (1,)), ((), ()))
EVERY = ("items", "heads")


def dot(left, right, dims=NN):
    return lax.dot_general(left, right, dims, preferred_element_type=F32)


def matmul_left(left, right):
    return lax.dot_general(left, right, (((0,), (0,)), ((), ())), preferred_element_type=F32)


def silu_slope(field):
    gate_sig = jax.nn.sigmoid(field)
    return gate_sig * (1.0 + field * (1.0 - gate_sig))


def layer_norm(field, gain_row):
    centred = field - jnp.mean(field, -1, keepdims=True)
    inverse = lax.rsqrt(jnp.mean(centred * centred, -1, keepdims=True) + EPS)
    normed = centred * inverse
    return (normed * gain_row, normed, inverse)


def norm_back(upstream, normed, inverse, gain_row):
    scaled = upstream * gain_row
    through = inverse * (
        scaled
        - jnp.mean(scaled, -1, keepdims=True)
        - normed * jnp.mean(scaled * normed, -1, keepdims=True)
    )
    return (through, jnp.sum(upstream * normed, 0, keepdims=True))


def segment_ids(position, long_count, short_count, group_len):
    long_end = long_count * LONG
    short_end = long_end + short_count * SHORT
    segments = jnp.where(
        position < long_end, position // LONG, long_count + (position - long_end) // SHORT
    )
    segments = jnp.where(position < short_end, segments, long_count + short_count)
    return jnp.where((position < 0) | (position >= group_len), -1, segments)


def compiler_params():
    return pltpu.CompilerParams(vmem_limit_bytes=VMEM_LIMIT)


def whole(shape):
    return pl.BlockSpec(shape, lambda *_: (0,) * len(shape))


def cost(flops, bytes_accessed, transcendentals=0):
    return pl.CostEstimate(
        flops=flops, bytes_accessed=bytes_accessed, transcendentals=transcendentals
    )


def head_lanes(shape, head, size):
    lane = lax.broadcasted_iota(jnp.int32, shape, 1)
    return (lane >= head * size) & (lane < (head + 1) * size)


def split_three(v):
    hi = v.astype(BF16).astype(F32)
    rest = v - hi
    mid = rest.astype(BF16).astype(F32)
    return (hi, mid, rest - mid)


def spread_columns(columns, shape):
    lane = lax.broadcasted_iota(jnp.int32, shape, 1)
    out = jnp.zeros(shape, F32)
    for place, column in enumerate(columns):
        out = jnp.where(lane == place, column, out)
    return out


def attn_fwd_kernel(heads, size, group, low_ref, high_ref, qkv_ref, segc_ref, out_ref, full_ref, lse_ref, kcat, v_all, s_scr):
    step = pl.program_id(0)
    width = heads * size
    blocks = group // BLOCK

    @pl.when(step == 0)
    def _():
        k = qkv_ref[:, 1].reshape(group, width)
        seg = segc_ref[...]
        lane = lax.broadcasted_iota(jnp.int32, (group, LANES), 1)
        kcat[:, :width] = k
        if width < LANES:
            kcat[:, width:LANES] = jnp.zeros((group, LANES - width), BF16)
        kcat[:, LANES:] = jnp.where(lane == seg, 0.0, -BIG).astype(BF16)
        v_all[...] = qkv_ref[:, 2].reshape(group, width)

    chunk = qkv_ref.shape[2]
    per = BLOCK // chunk if BLOCK > chunk else 1
    rows = pl.ds(pl.multiple_of(step * BLOCK, BLOCK), BLOCK)
    if BLOCK == chunk:
        q = qkv_ref[step, 0]
    else:
        q = qkv_ref[pl.ds(step * per, per), 0].reshape(BLOCK, width)
    q = q.astype(F32) * (size ** -0.5)
    lane = lax.broadcasted_iota(jnp.int32, (BLOCK, LANES), 1)
    member = jnp.where(lane == segc_ref[rows, :], 1.0, 0.0).astype(BF16)
    queries = []
    for head in range(heads):
        mine = q if heads == 1 else jnp.where(head_lanes(q.shape, head, size), q, 0.0)
        mine = mine.astype(BF16)
        if width < LANES:
            mine = jnp.concatenate([mine, jnp.zeros((BLOCK, LANES - width), BF16)], 1)
        queries.append(jnp.concatenate([mine, member], 1))
    low, high = low_ref[step], high_ref[step]

    def scores(j, tops):
        keys = kcat[pl.ds(pl.multiple_of(j * BLOCK, BLOCK), BLOCK), :]
        new = []
        for head in range(heads):
            s = dot(queries[head], keys, NT)
            s_scr[head, j] = s
            top = tops[head]
            for part in range(BLOCK // LANES):
                top = jnp.maximum(top, s[:, part * LANES:(part + 1) * LANES])
            new.append(top)
        return tuple(new)

    start = tuple(jnp.full((BLOCK, LANES), -BIG, F32) for _ in range(heads))
    tops = lax.fori_loop(low, high, scores, start)
    tops = [jnp.max(t, 1, keepdims=True) for t in tops]
    tops = [jnp.broadcast_to(t, (BLOCK, LANES)) for t in tops]

    def weigh(j, carried):
        sums, accs = carried
        values = v_all[pl.ds(pl.multiple_of(j * BLOCK, BLOCK), BLOCK), :]
        new_sums, new_accs = [], []
        for head in range(heads):
            total = sums[head]
            parts = []
            for part in range(BLOCK // LANES):
                p = jnp.exp(s_scr[head, j, :, part * LANES:(part + 1) * LANES] - tops[head])
                total = total + p
                parts.append(p.astype(BF16))
            new_sums.append(total)
            new_accs.append(accs[head] + dot(jnp.concatenate(parts, 1), values))
        return (tuple(new_sums), tuple(new_accs))

    zeros = tuple(jnp.zeros((BLOCK, LANES), F32) for _ in range(heads))
    blank = tuple(jnp.zeros((BLOCK, width), F32) for _ in range(heads))
    sums, accs = lax.fori_loop(low, high, weigh, (zeros, blank))
    result = None
    for head in range(heads):
        total = jnp.sum(sums[head], 1, keepdims=True)
        mine = accs[head] / total
        result = mine if result is None else jnp.where(head_lanes(mine.shape, head, size), mine, result)
        lse_ref[head] = tops[head] + jnp.log(jnp.broadcast_to(total, (BLOCK, LANES)))
    full_ref[...] = result
    out_ref[...] = result.astype(BF16)


def attend_forward(qkv, seg_column, low, high, size):
    sources, _, chunk, width = qkv.shape
    group = sources * chunk
    heads = width // size
    steps = group // BLOCK
    smem = pl.BlockSpec(memory_space=pltpu.SMEM)
    return pl.pallas_call(
        functools.partial(attn_fwd_kernel, heads, size, group),
        grid=(steps,),
        in_specs=[
            smem,
            smem,
            pl.BlockSpec(qkv.shape, lambda i: (0, 0, 0, 0)),
            pl.BlockSpec((group, 1), lambda i: (0, 0)),
        ],
        out_specs=[
            pl.BlockSpec((BLOCK, width), lambda i: (i, 0)),
            pl.BlockSpec((BLOCK, width), lambda i: (i, 0)),
            pl.BlockSpec((heads, BLOCK, LANES), lambda i: (0, i, 0)),
        ],
        out_shape=[
            jax.ShapeDtypeStruct((group, width), BF16),
            jax.ShapeDtypeStruct((group, width), F32),
            jax.ShapeDtypeStruct((heads, group, LANES), F32),
        ],
        scratch_shapes=[
            pltpu.VMEM((group, 2 * LANES), BF16),
            pltpu.VMEM((group, width), BF16),
            pltpu.VMEM((heads, steps, BLOCK, BLOCK), F32),
        ],
        compiler_params=pltpu.CompilerParams(vmem_limit_bytes=VMEM_LIMIT),
        cost_estimate=pl.CostEstimate(flops=16 * group * group * LANES, bytes_accessed=6 << 20, transcendentals=heads * group * group),
        name="attend_forward",
    )(low, high, qkv, seg_column)


def attn_bwd_kernel(heads, size, group, low_ref, high_ref, qkv_ref, segc_ref, full_ref, lse_ref, grad_ref, out_ref, qcat, gcat, k_turned, dq_turned):
    step = pl.program_id(0)
    width = heads * size
    blocks = group // BLOCK
    chunk = qkv_ref.shape[2]
    per = BLOCK // chunk if BLOCK > chunk else 1

    def block_of(part, j):
        if BLOCK == chunk:
            return qkv_ref[j, part]
        return qkv_ref[pl.ds(j * per, per), part].reshape(BLOCK, width)

    def grad_of(j):
        if BLOCK == chunk:
            return grad_ref[j]
        return grad_ref[pl.ds(j * per, per)].reshape(BLOCK, width)

    def widened(v):
        if width < LANES:
            return jnp.concatenate([v, jnp.zeros((BLOCK, LANES - width), v.dtype)], 1)
        return v

    @pl.when(step == 0)
    def _():
        dq_turned[...] = jnp.zeros_like(dq_turned)

        def prepare(j, _):
            rows = pl.ds(pl.multiple_of(j * BLOCK, BLOCK), BLOCK)
            lane = lax.broadcasted_iota(jnp.int32, (BLOCK, LANES), 1)
            seg = segc_ref[rows, :]
            q = widened(block_of(0, j).astype(F32) * (size ** -0.5))
            g = widened(grad_of(j).astype(F32))
            o = widened(full_ref[rows, :])
            product = g * o
            member = jnp.where(lane == seg + 3, 1.0, 0.0)
            for head in range(heads):
                own = head_lanes((BLOCK, LANES), head, size)
                lse = lse_ref[head, rows, :]
                tail = jnp.where(lane < 3, -spread_columns(split_three(lse), (BLOCK, LANES)), member)
                delta = jnp.broadcast_to(jnp.sum(jnp.where(own, product, 0.0), 1, keepdims=True), (BLOCK, LANES))
                qcat[head, rows, :LANES] = jnp.where(own, q, 0.0).astype(BF16)
                qcat[head, rows, LANES:] = tail.astype(BF16)
                gcat[head, rows, :LANES] = jnp.where(own, g, 0.0).astype(BF16)
                gcat[head, rows, LANES:] = (-spread_columns(split_three(delta), (BLOCK, LANES))).astype(BF16)
            k = widened(block_of(1, j).astype(F32))
            k_turned[j] = jnp.transpose(k).astype(BF16)
            return 0

        lax.fori_loop(0, blocks, prepare, 0)

    lane = lax.broadcasted_iota(jnp.int32, (BLOCK, LANES), 1)
    rows = pl.ds(pl.multiple_of(step * BLOCK, BLOCK), BLOCK)
    seg = segc_ref[rows, :]
    tail = jnp.where(lane < 3, 1.0, jnp.where(lane == seg + 3, 0.0, -BIG)).astype(BF16)
    keys = jnp.concatenate([widened(block_of(1, step)), tail], 1)
    ones = jnp.where(lane < 3, 1.0, 0.0).astype(BF16)
    values = jnp.concatenate([widened(block_of(2, step)), ones], 1)

    def one(j, carried):
        dk, dv = carried
        cols = pl.ds(pl.multiple_of(j * BLOCK, BLOCK), BLOCK)
        for head in range(heads):
            qc = qcat[head, cols, :]
            gc = gcat[head, cols, :]
            p = jnp.exp(dot(keys, qc, NT))
            ds = (p * dot(values, gc, NT)).astype(BF16)
            dv = dv + dot(p.astype(BF16), gc[:, :LANES])
            dk = dk + dot(ds, qc[:, :LANES])
            turned = k_turned[step, head * size:(head + 1) * size, :]
            dq_turned[j, head * size:(head + 1) * size, :] += dot(turned, ds)
        return (dk, dv)

    zero = jnp.zeros((BLOCK, LANES), F32)
    dk, dv = lax.fori_loop(low_ref[step], high_ref[step], one, (zero, zero))
    dk = dk[:, :width].astype(BF16)
    dv = dv[:, :width].astype(BF16)
    if BLOCK == chunk:
        out_ref[step, 1] = dk
        out_ref[step, 2] = dv
    else:
        out_ref[pl.ds(step * per, per), 1] = dk.reshape(per, chunk, width)
        out_ref[pl.ds(step * per, per), 2] = dv.reshape(per, chunk, width)

    @pl.when(step == blocks - 1)
    def _():
        def finish(j, _):
            dq = (jnp.transpose(dq_turned[j]) * (size ** -0.5))[:, :width].astype(BF16)
            if BLOCK == chunk:
                out_ref[j, 0] = dq
            else:
                out_ref[pl.ds(j * per, per), 0] = dq.reshape(per, chunk, width)
            return 0

        lax.fori_loop(0, blocks, finish, 0)


def attend_backward(qkv, seg_column, low, high, size, full, lse, grad):
    sources, _, chunk, width = qkv.shape
    group = sources * chunk
    heads = width // size
    steps = group // BLOCK
    smem = pl.BlockSpec(memory_space=pltpu.SMEM)
    whole = lambda shape: pl.BlockSpec(shape, lambda i: (0,) * len(shape))
    return pl.pallas_call(
        functools.partial(attn_bwd_kernel, heads, size, group),
        grid=(steps,),
        in_specs=[
            smem,
            smem,
            whole(qkv.shape),
            whole((group, 1)),
            whole(full.shape),
            whole(lse.shape),
            whole(grad.shape),
        ],
        out_specs=whole(qkv.shape),
        out_shape=jax.ShapeDtypeStruct(qkv.shape, BF16),
        scratch_shapes=[
            pltpu.VMEM((heads, group, 2 * LANES), BF16),
            pltpu.VMEM((heads, group, 2 * LANES), BF16),
            pltpu.VMEM((steps, LANES, BLOCK), BF16),
            pltpu.VMEM((steps, LANES, BLOCK), F32),
        ],
        compiler_params=pltpu.CompilerParams(vmem_limit_bytes=VMEM_LIMIT),
        cost_estimate=pl.CostEstimate(flops=32 * group * group * LANES, bytes_accessed=9 << 20, transcendentals=heads * group * group),
        name="attend_backward",
    )(low, high, qkv, seg_column, full, lse, grad)


def block_ranges(seg):
    blocks = seg.reshape(-1, BLOCK)
    first, last = blocks[:, 0], blocks[:, -1]
    low = jnp.sum(seg[None, :] < first[:, None], 1) // BLOCK
    high = (jnp.sum(seg[None, :] <= last[:, None], 1) + BLOCK - 1) // BLOCK
    return (low.astype(jnp.int32), high.astype(jnp.int32))


def ffn_fwd_kernel(x_ref, gain_ref, win_ref, wout_ref, out_ref, pre_ref, entered, total):
    step = pl.program_id(0)

    @pl.when(step == 0)
    def _():
        entered[...] = layer_norm(x_ref[...].astype(F32), gain_ref[...])[0].astype(BF16)
        total[...] = jnp.zeros_like(total)

    pre = dot(entered[...], win_ref[...])
    pre_ref[...] = pre
    hidden = (pre * jax.nn.sigmoid(pre)).astype(BF16)
    total[...] += dot(hidden, wout_ref[...])

    @pl.when(step == pl.num_programs(0) - 1)
    def _():
        out_ref[...] = x_ref[...].astype(F32) + 0.5 * total[...]


def ffn_forward(stream, gain_row, weight_in, weight_out):
    rows, model = stream.shape
    hidden = weight_in.shape[1]
    wide = 512
    return pl.pallas_call(
        ffn_fwd_kernel,
        grid=(hidden // wide,),
        in_specs=[
            whole((rows, model)),
            whole((1, model)),
            pl.BlockSpec((model, wide), lambda s: (0, s)),
            pl.BlockSpec((wide, model), lambda s: (s, 0)),
        ],
        out_specs=[whole((rows, model)), pl.BlockSpec((rows, wide), lambda s: (0, s))],
        out_shape=[
            jax.ShapeDtypeStruct((rows, model), F32),
            jax.ShapeDtypeStruct((rows, hidden), F32),
        ],
        scratch_shapes=[pltpu.VMEM((rows, model), BF16), pltpu.VMEM((rows, model), F32)],
        compiler_params=compiler_params(),
        cost_estimate=cost(4 * rows * model * hidden, 4 * model * hidden + 4 * rows * hidden),
        name="ffn_forward",
    )(stream, gain_row, weight_in, weight_out)


def turned_rows(value, rows_each, core, target):
    model = value.shape[1]
    shares = model // rows_each
    for share in range(shares):
        part = jnp.transpose(value[:, share * rows_each : (share + 1) * rows_each]).astype(BF16)
        place = (share // 2) * rows_each + jnp.where(
            core == share % 2, 0, (shares // 2) * rows_each
        )
        target[pl.ds(pl.multiple_of(place, rows_each), rows_each), :] = part


def ffn_bwd_kernel(
    core_ref, x_ref, gain_ref, up_ref, pre_ref, win_ref, wout_ref,
    down_ref, gain_grad_ref, in_keep, in_send, out_keep, out_send,
    entered, turned, turned_up, total,
):
    step = pl.program_id(0)
    core = core_ref[0]
    model = x_ref.shape[1]
    rows_each = in_keep.shape[1]
    half = model // 2

    @pl.when(step == 0)
    def _():
        shaped = layer_norm(x_ref[...].astype(F32), gain_ref[...])[0]
        turned_rows(shaped, rows_each, core, turned)
        halved = 0.5 * up_ref[...]
        turned_up[...] = jnp.transpose(halved).astype(BF16)
        entered[...] = halved.astype(BF16)
        total[...] = jnp.zeros_like(total)

    pre = pre_ref[...]
    gate = jax.nn.sigmoid(pre)
    hidden = (pre * gate).astype(BF16)
    grad_hidden = dot(entered[...], wout_ref[...], NT)
    grad_pre = (grad_hidden * (gate * (1.0 + pre * (1.0 - gate)))).astype(BF16)
    total[...] += dot(grad_pre, win_ref[...], NT)
    grad_in = dot(turned[...], grad_pre).astype(BF16)
    in_keep[...] = grad_in[:half].reshape(in_keep.shape)
    in_send[...] = grad_in[half:].reshape(in_send.shape)
    grad_out = dot(turned_up[...], hidden).astype(BF16)
    wide = grad_out.shape[1]

    def place(target):
        for group in range(model // rows_each):
            target[0, :, group * wide : (group + 1) * wide] = grad_out[
                group * rows_each : (group + 1) * rows_each
            ]

    @pl.when(step % 2 == 0)
    def _():
        place(out_keep)

    @pl.when(step % 2 == 1)
    def _():
        place(out_send)

    @pl.when(step == pl.num_programs(0) - 1)
    def _():
        gain = gain_ref[...]
        normed, inverse = layer_norm(x_ref[...].astype(F32), gain)[1:]
        through, grad_gain = norm_back(total[...], normed, inverse, gain)
        down_ref[...] = (up_ref[...] + through).astype(down_ref.dtype)
        gain_grad_ref[...] = grad_gain


def ffn_backward(upstream, stream, pre_act, gain_row, weight_in, weight_out, heads, core, down_type):
    rows, model = stream.shape
    hidden = weight_in.shape[1]
    wide = hidden // heads
    rows_each = model // heads
    places = heads // 2

    def at(s, core):
        return 2 * (s // 2) + (s + core[0]) % 2

    share = jax.ShapeDtypeStruct((places, rows_each, hidden), BF16)
    grid_spec = pltpu.PrefetchScalarGridSpec(
        num_scalar_prefetch=1,
        grid=(heads,),
        in_specs=[
            whole((rows, model)),
            whole((1, model)),
            whole((rows, model)),
            pl.BlockSpec((rows, wide), lambda s, core: (0, at(s, core))),
            pl.BlockSpec((model, wide), lambda s, core: (0, at(s, core))),
            pl.BlockSpec((wide, model), lambda s, core: (at(s, core), 0)),
        ],
        out_specs=[
            whole((rows, model)),
            whole((1, model)),
            pl.BlockSpec((places, rows_each, wide), lambda s, core: (0, 0, at(s, core))),
            pl.BlockSpec((places, rows_each, wide), lambda s, core: (0, 0, at(s, core))),
            pl.BlockSpec((1, rows_each, hidden), lambda s, core: (s // 2, 0, 0)),
            pl.BlockSpec((1, rows_each, hidden), lambda s, core: (s // 2, 0, 0)),
        ],
        scratch_shapes=[
            pltpu.VMEM((rows, model), BF16),
            pltpu.VMEM((model, rows), BF16),
            pltpu.VMEM((model, rows), BF16),
            pltpu.VMEM((rows, model), F32),
        ],
    )
    return pl.pallas_call(
        ffn_bwd_kernel,
        grid_spec=grid_spec,
        out_shape=[
            jax.ShapeDtypeStruct((rows, model), down_type),
            jax.ShapeDtypeStruct((1, model), F32),
            share, share, share, share,
        ],
        compiler_params=compiler_params(),
        cost_estimate=cost(
            8 * rows * model * hidden, 8 * model * hidden + 4 * rows * hidden + 8 * rows * model
        ),
        name="ffn_backward",
    )(core, stream, gain_row, upstream, pre_act, weight_in, weight_out)


def turn(field, cosines, sines, size):
    lane = lax.broadcasted_iota(jnp.int32, field.shape, 1)
    half = size // 2
    width = field.shape[1]
    swapped = jnp.where(
        lane % size < half,
        pltpu.roll(field, width - half, 1),
        pltpu.roll(field, half, 1),
    )
    return field * cosines + swapped * sines


def rope_tables(position, size, width):
    half = size // 2
    lane = jnp.arange(width, dtype=jnp.int32)
    freqs = jnp.exp(
        -jnp.log(jnp.float32(ROPE_BASE)) * jnp.arange(half, dtype=jnp.float32) / half
    )
    angles = position.astype(jnp.float32)[:, None] * freqs[None, :]
    cosines, sines = jnp.cos(angles), jnp.sin(angles)
    repeats = width // size
    return (
        jnp.tile(jnp.concatenate([cosines, cosines], 1), (1, repeats)),
        jnp.tile(jnp.concatenate([-sines, sines], 1), (1, repeats)),
    )


def qkv_fwd_kernel(size, x_ref, gain_ref, wq_ref, wk_ref, wv_ref, cos_ref, sin_ref, *rest):
    outs, entered = rest[:-1], rest[-1]
    step = pl.program_id(0)

    @pl.when(step == 0)
    def _():
        entered[...] = layer_norm(x_ref[...], gain_ref[...])[0].astype(BF16)

    frames = outs[0].shape[2]
    width = outs[0].shape[3]
    for place, weight in enumerate((wq_ref, wk_ref, wv_ref)):
        made = dot(entered[...], weight[...])
        for number, out in enumerate(outs):
            part = made[number * frames : (number + 1) * frames]
            if place < 2:
                part = turn(part, cos_ref[...], sin_ref[...], size)
            part = part.astype(BF16)
            for target in range(out.shape[0]):
                out[target, place] = part[:, target * width : (target + 1) * width]


def qkv_forward(stream, gain_row, weight, cosines, sines, heads, batches, size):
    rows, model = stream.shape
    wide = cosines.shape[1]
    steps = model // wide
    width = model // heads
    frames = rows // batches
    out = jax.ShapeDtypeStruct((heads, 3, frames, width), BF16)
    return pl.pallas_call(
        functools.partial(qkv_fwd_kernel, size),
        grid=(steps,),
        in_specs=[
            whole((rows, model)),
            whole((1, model)),
            pl.BlockSpec((model, wide), lambda s: (0, s)),
            pl.BlockSpec((model, wide), lambda s: (0, steps + s)),
            pl.BlockSpec((model, wide), lambda s: (0, 2 * steps + s)),
            whole(cosines.shape),
            whole(sines.shape),
        ],
        out_specs=[
            pl.BlockSpec((wide // width, 3, frames, width), lambda s: (s, 0, 0, 0))
            for _ in range(batches)
        ],
        out_shape=[out] * batches,
        scratch_shapes=[pltpu.VMEM((rows, model), BF16)],
        compiler_params=compiler_params(),
        cost_estimate=cost(6 * rows * model * model, 6 * model * model + 10 * rows * model),
        name="qkv_forward",
    )(stream, gain_row, weight, weight, weight, cosines, sines)


def qkv_bwd_kernel(size, batches, steps, core_ref, *refs):
    backs, refs = refs[:batches], refs[batches:]
    (x_ref, gain_ref, up_ref, weight_ref, cos_ref, sin_ref,
     down_ref, gain_grad_ref, keep, send, turned, total) = refs
    step = pl.program_id(0)
    model = x_ref.shape[1]
    rows_each = keep.shape[1]
    half = model // 2

    @pl.when(step == 0)
    def _():
        shaped = layer_norm(x_ref[...], gain_ref[...])[0]
        turned_rows(shaped, rows_each, core_ref[0], turned)
        total[...] = jnp.zeros_like(total)

    parts = []
    rotated = step < 2 * steps
    cosines = jnp.where(rotated, cos_ref[...], 1.0)
    sines = jnp.where(rotated, -sin_ref[...], 0.0)
    for back in backs:
        field = jnp.concatenate([back[i, 0] for i in range(back.shape[0])], 1).astype(F32)
        parts.append(turn(field, cosines, sines, size).astype(BF16))
    grad = jnp.concatenate(parts, 0)
    total[...] += dot(grad, weight_ref[...], NT)
    made = dot(turned[...], grad).astype(BF16)
    keep[...] = made[:half].reshape(keep.shape)
    send[...] = made[half:].reshape(send.shape)

    @pl.when(step == pl.num_programs(0) - 1)
    def _():
        gain = gain_ref[...]
        normed, inverse = layer_norm(x_ref[...], gain)[1:]
        through, grad_gain = norm_back(total[...], normed, inverse, gain)
        down_ref[...] = up_ref[...] + through
        gain_grad_ref[...] = grad_gain


def qkv_backward(backs, stream, gain_row, upstream, weight, cosines, sines, heads, core, size):
    rows, model = stream.shape
    wide = cosines.shape[1]
    steps = model // wide
    width = model // heads
    frames = backs[0].shape[2]
    rows_each = model // heads
    places = heads // 2
    batches = len(backs)
    share = jax.ShapeDtypeStruct((places, rows_each, 3 * model), BF16)
    grid_spec = pltpu.PrefetchScalarGridSpec(
        num_scalar_prefetch=1,
        grid=(3 * steps,),
        in_specs=[
            pl.BlockSpec(
                (wide // width, 1, frames, width), lambda s, core: (s % steps, s // steps, 0, 0)
            )
            for _ in range(batches)
        ]
        + [
            whole((rows, model)),
            whole((1, model)),
            whole((rows, model)),
            pl.BlockSpec((model, wide), lambda s, core: (0, s)),
            whole(cosines.shape),
            whole(sines.shape),
        ],
        out_specs=[
            whole((rows, model)),
            whole((1, model)),
            pl.BlockSpec((places, rows_each, wide), lambda s, core: (0, 0, s)),
            pl.BlockSpec((places, rows_each, wide), lambda s, core: (0, 0, s)),
        ],
        scratch_shapes=[pltpu.VMEM((model, rows), BF16), pltpu.VMEM((rows, model), F32)],
    )
    return pl.pallas_call(
        functools.partial(qkv_bwd_kernel, size, batches, steps),
        grid_spec=grid_spec,
        out_shape=[
            jax.ShapeDtypeStruct((rows, model), F32),
            jax.ShapeDtypeStruct((1, model), F32),
            share,
            share,
        ],
        compiler_params=compiler_params(),
        cost_estimate=cost(12 * rows * model * model, 12 * model * model + 20 * rows * model),
        name="qkv_backward",
    )(core, *backs, stream, gain_row, upstream, weight, cosines, sines)


def flipped(axis_bit, count):
    axis, bit = axis_bit
    items, heads = count
    if axis == "items":
        return [(i * heads + h, (i ^ bit) * heads + h) for i in range(items) for h in range(heads)]
    return [(i * heads + h, i * heads + (h ^ bit)) for i in range(items) for h in range(heads)]


def swap(value, axis_bit):
    count = (lax.axis_size("items"), lax.axis_size("heads"))
    return lax.ppermute(value, EVERY, flipped(axis_bit, count))


def plus(left, right):
    return (left.astype(F32) + right.astype(F32)).astype(BF16)


def halves(value, rows_each):
    places = value.shape[0] // (2 * rows_each)
    cut = value.reshape(places, 2, rows_each, value.shape[1])
    core = lax.axis_index("heads") % 2
    return tuple(
        lax.dynamic_index_in_dim(cut, which, 1, keepdims=False) for which in (core, 1 - core)
    )


def columns(value, start, size):
    return lax.dynamic_slice_in_dim(value, start * size, size, 2)


def scatter(keep, send):
    items = lax.axis_size("items")
    value = plus(keep, swap(send, ("heads", 1)))
    places, rows, wide = value.shape
    size = wide // items
    if items == 4:
        own = lax.axis_index("items")
        top, low = value[:, : rows // 2], value[:, rows // 2 :]
        across, along = own ^ 1, own ^ 2
        beyond = own ^ 3
        got_top = swap(
            jnp.concatenate([columns(top, across, size), columns(top, beyond, size)], 1),
            ("items", 1),
        )
        got_low = swap(
            jnp.concatenate([columns(low, along, size), columns(low, beyond, size)], 1),
            ("items", 2),
        )
        half = rows // 2
        send_top = plus(columns(top, along, size), got_top[:, half:])
        keep_top = plus(columns(top, own, size), got_top[:, :half])
        send_low = plus(columns(low, across, size), got_low[:, half:])
        keep_low = plus(columns(low, own, size), got_low[:, :half])
        value = jnp.concatenate(
            [
                plus(keep_top, swap(send_top, ("items", 2))),
                plus(keep_low, swap(send_low, ("items", 1))),
            ],
            1,
        )
    else:
        value = lax.psum_scatter(value, "items", scatter_dimension=2, tiled=True)
    heads = lax.axis_size("heads")
    groups = [[core + 2 * z for z in range(heads // 2)] for core in range(2)]
    value = lax.psum_scatter(
        value, "heads", scatter_dimension=0, tiled=False, axis_index_groups=groups
    )
    return value


def sum_everywhere(value):
    for axis in EVERY:
        bit = 1
        while bit < lax.axis_size(axis):
            value = value + swap(value, (axis, bit))
            bit *= 2
    return value


def edges(block, width):
    count = lax.axis_size("heads")
    forward = [(i, i + 1) for i in range(count - 1)]
    backward = [(target, source) for source, target in forward]
    low = lax.ppermute(block[:, block.shape[1] - width :], "heads", forward)
    high = lax.ppermute(block[:, :width], "heads", backward)
    return jnp.concatenate([low, block, high], axis=1)


def body(
    frames, cotangent, bucket_counts, gains, w_ffn1_in, w_ffn1_out, w_qkv, w_out,
    w_point_in, w_depth, w_point_out, w_ffn2_in, w_ffn2_out,
):
    batches, here, model = frames.shape
    head_ways = lax.axis_size("heads")
    items = lax.axis_size("items")
    group_len = here * head_ways
    size = model // HEADS
    reach = (KERNEL - 1) // 2
    rows = batches * here
    rows_each = model // head_ways
    place = lax.axis_index("heads")
    core = (place % 2).astype(jnp.int32).reshape(1)
    first = place * here
    cosines, sines = rope_tables(
        first + jnp.arange(here, dtype=jnp.int32), size, max(2 * LANES, model // head_ways)
    )
    depth_rows = w_depth.astype(F32)
    gain = [gains[i : i + 1] for i in range(6)]
    wide_position = first - reach + jnp.arange(here + 2 * reach, dtype=jnp.int32)
    group_position = jnp.arange(group_len, dtype=jnp.int32)
    seg_wide = []
    seg_group = []
    for number in range(batches):
        counts = bucket_counts[number, 0]
        seg_wide.append(segment_ids(wide_position, counts[0], counts[1], group_len))
        seg_group.append(segment_ids(group_position, counts[0], counts[1], group_len))
    seg_wide = jnp.stack(seg_wide, 0)
    seg_own = seg_wide[:, reach : reach + here]
    ranges = [block_ranges(seg) for seg in seg_group]

    stream = frames.reshape(rows, model)
    stream_one, pre_one = ffn_forward(stream, gain[0], w_ffn1_in, w_ffn1_out)
    sent = qkv_forward(stream_one, gain[1], w_qkv, cosines, sines, head_ways, batches, size)
    qkv = [
        lax.all_to_all(part, "heads", split_axis=0, concat_axis=0, tiled=True) for part in sent
    ]
    contexts, fulls, lses = [], [], []
    for number in range(batches):
        out, full, lse = attend_forward(
            qkv[number], seg_group[number][:, None], *ranges[number], size
        )
        contexts.append(
            lax.all_to_all(
                out.reshape(head_ways, here, -1), "heads", split_axis=0, concat_axis=0, tiled=True
            )
        )
        fulls.append(full)
        lses.append(lse)
    context = jnp.concatenate(
        [part.transpose(1, 0, 2).reshape(here, model) for part in contexts], 0
    )
    stream_two = stream_one + dot(context, w_out)
    shaped, conv_normed, conv_inverse = layer_norm(stream_two, gain[2])
    conv_entered = shaped.astype(BF16)
    pointwise = dot(conv_entered, w_point_in)
    linear = pointwise[:, :model]
    sigmoid_gate = jax.nn.sigmoid(pointwise[:, model:])
    gated_low = (linear * sigmoid_gate).astype(BF16).reshape(batches, here, model)
    widened = edges(gated_low, reach)
    depth_out = jnp.zeros((batches, here, model), F32)
    for offset in range(KERNEL):
        same = (seg_wide[:, offset : offset + here] == seg_own)[:, :, None]
        depth_out = depth_out + depth_rows[offset] * jnp.where(
            same, widened[:, offset : offset + here], 0.0
        )
    depth_out = depth_out.reshape(rows, model)
    depth_shaped, depth_normed, depth_inverse = layer_norm(depth_out, gain[3])
    mixed_low = (depth_shaped * jax.nn.sigmoid(depth_shaped)).astype(BF16)
    stream_three = stream_two + dot(mixed_low, w_point_out)
    stream_four, pre_two = ffn_forward(stream_three, gain[4], w_ffn2_in, w_ffn2_out)
    shaped, final_normed, final_inverse = layer_norm(stream_four, gain[5])
    layer_out = shaped.astype(BF16).reshape(frames.shape)
    grad_four, gain_five = norm_back(
        cotangent.reshape(rows, model).astype(F32), final_normed, final_inverse, gain[5]
    )
    grad_three, gain_four, *shares_two = ffn_backward(
        grad_four, stream_three, pre_two, gain[4], w_ffn2_in, w_ffn2_out, head_ways, core, F32
    )
    f2_in = scatter(*shares_two[:2])
    f2_out = scatter(*shares_two[2:])
    grad_mix = grad_three.astype(BF16)
    point_out = scatter(*halves(matmul_left(mixed_low, grad_mix).astype(BF16), rows_each))
    grad_norm_in = dot(grad_mix, w_point_out, NT) * silu_slope(depth_shaped)
    grad_depth, gain_three = norm_back(grad_norm_in, depth_normed, depth_inverse, gain[3])
    grad_depth_low = grad_depth.astype(BF16).reshape(batches, here, model)
    grad_widened = edges(grad_depth_low, reach)
    grad_depth_full = grad_depth_low.astype(F32)
    taps = []
    grad_gated = jnp.zeros((batches, here, model), F32)
    for offset in range(KERNEL):
        same = (seg_wide[:, offset : offset + here] == seg_own)[:, :, None]
        taps.append(
            jnp.sum(
                jnp.where(same, grad_depth_full * widened[:, offset : offset + here], 0.0), (0, 1)
            )
        )
        mirror = 2 * reach - offset
        same_back = (seg_wide[:, mirror : mirror + here] == seg_own)[:, :, None]
        grad_gated = grad_gated + depth_rows[offset] * jnp.where(
            same_back, grad_widened[:, mirror : mirror + here], 0.0
        )
    grad_gated = grad_gated.reshape(rows, model)
    grad_point = jnp.concatenate(
        [grad_gated * sigmoid_gate, grad_gated * linear * sigmoid_gate * (1.0 - sigmoid_gate)], 1
    ).astype(BF16)
    through, gain_two = norm_back(
        dot(grad_point, w_point_in, NT), conv_normed, conv_inverse, gain[2]
    )
    grad_two = grad_three + through
    grad_attn_out = grad_two.astype(BF16)
    grad_context = dot(grad_attn_out, w_out, NT).astype(BF16)
    backs = []
    for number in range(batches):
        part = grad_context[number * here : (number + 1) * here]
        part = part.reshape(here, head_ways, -1).transpose(1, 0, 2)
        grad_heads = lax.all_to_all(part, "heads", split_axis=0, concat_axis=0, tiled=True)
        grads = attend_backward(
            qkv[number], seg_group[number][:, None], *ranges[number], size,
            fulls[number], lses[number], grad_heads,
        )
        backs.append(lax.all_to_all(grads, "heads", split_axis=0, concat_axis=0, tiled=True))
    point_in = scatter(*halves(matmul_left(conv_entered, grad_point).astype(BF16), rows_each))
    out_proj = scatter(*halves(matmul_left(context, grad_attn_out).astype(BF16), rows_each))
    grad_one, gain_one, *shares_qkv = qkv_backward(
        backs, stream_one, gain[1], grad_two, w_qkv, cosines, sines, head_ways, core, size
    )
    qkv_grad = scatter(*shares_qkv)
    grad_zero, gain_zero, *shares_one = ffn_backward(
        grad_one, stream, pre_one, gain[0], w_ffn1_in, w_ffn1_out, head_ways, core, BF16
    )
    f1_in = scatter(*shares_one[:2])
    f1_out = scatter(*shares_one[2:])
    small = sum_everywhere(
        jnp.concatenate(
            [gain_zero, gain_one, gain_two, gain_three, gain_four, gain_five]
            + [tap[None] for tap in taps],
            0,
        )
    )
    hidden = w_ffn1_in.shape[1]

    def unfolded(share):
        each, wide = share.shape
        span = hidden // head_ways
        parts = [share[:, i * span : (i + 1) * span] for i in range(wide // span)]
        return jnp.concatenate(parts, 0).T.astype(F32)

    return (
        layer_out,
        grad_zero.reshape(frames.shape),
        small[:6],
        f1_in.astype(F32),
        unfolded(f1_out),
        qkv_grad.astype(F32),
        out_proj.astype(F32),
        point_in.astype(F32),
        small[6:],
        point_out.astype(F32),
        f2_in.astype(F32),
        unfolded(f2_out),
    )


def solution(mesh):
    split = P(None, EVERY, None)
    shares = P("heads", "items")
    in_specs = (split, split, P(None, "items", None)) + (P(),) * 10
    out_specs = (split, split, P(), shares, shares, shares, shares, shares, P()) + (shares,) * 3
    return jax.shard_map(body, mesh=mesh, in_specs=in_specs, out_specs=out_specs, check_vma=False)
```

time: 1470 us -> 757 us (0.51)
  matrix products: 457 us -> 28.7 us
  waiting for transfers between devices: 577 us -> 193 us
  Pallas kernels: 0 us -> 246 us
  local copies, waits for them, and re-layouts: 107 us -> 35.6 us
  blocking collectives: 38.7 us -> 0 us
  loops' own time: 31.6 us -> 0 us
    reduce_scatter x16 -> x8, waiting for transfers between devices: 467 us -> 0.05 us  [scatter(): lax.psum_scatter(value, 'heads', scatter_dimension=0, tiled=False, axis_i...]
    dot_general x88 -> x6, matrix products: 339 us -> 16.4 us  [dot(): return lax.dot_general(left, right, dims, preferred_element_type=F32)]
    pallas_call x0 -> x10, Pallas kernels: none -> 246 us  [the longest x2 68.4 us: attend_backward(): pl.pallas_call(functools.partial(attn_bwd_kernel, heads, size, group), gr...]
    ppermute x8 -> x49, waiting for transfers between devices: 0.02 us -> 129 us  [the longest x45 128 us: swap(): return lax.ppermute(value, EVERY, flipped(axis_bit, count))]
    dot_general x16 -> x3, matrix products: 118 us -> 12.3 us  [matmul_left(): lax.dot_general(left, right, (((0,), (0,)), ((), ())), preferred_element_...]
    all_to_all x16 -> x8, waiting for transfers between devices: 108 us -> 64.1 us  [the longest x4 34.4 us: body(): lax.all_to_all(part, 'heads', split_axis=0, concat_axis=0, tiled=True)]
    psum x1 -> x0, blocking collectives: 38.7 us -> none  [body(): gains_total, depth_total = lax.psum(small_total, ('items', 'heads'))]
    another operation x4 -> x0, loops' own time: 31.6 us -> none  [the longest x2 16 us: attend_backward(): lax.scan(one_block, (zero_keys, zero_keys), (starts, log_totals))]
  transfers between devices with their start and end apart: 40 -> 65, of which waited for: 23 -> 29; matrix products, arithmetic and copies ran while one was open for 39% -> 19% of each run, Pallas kernels for 0% -> 23%
where the time goes in v1:
time: 757 us; the launch traced here: 744 us
  Pallas kernels  246 us (32%)
  waiting for transfers between devices  193 us (25%)
  other arithmetic  125 us (17%)
  starting transfers between devices  93.8 us (12%)
  local copies, waits for them, and re-layouts  35.6 us (5%)
  matrix products  28.7 us (4%)
  between operations  21.2 us (3%)
    ppermute x45, waiting for transfers between devices, swap(): return lax.ppermute(value, EVERY, flipped(axis_bit, count))  128 us
    pallas_call x2, Pallas kernels, attend_backward(): pl.pallas_call(functools.partial(attn_bwd_kernel, heads, size, group), gr...  68.4 us
    convert_element_type x40, other arithmetic, plus(): return (left.astype(F32) + right.astype(F32)).astype(BF16)  61.8 us
    pallas_call x2, Pallas kernels, ffn_backward(): pl.pallas_call(ffn_bwd_kernel, grid_spec=grid_spec, out_shape=[jax.ShapeD...  61.5 us
    pallas_call x2, Pallas kernels, attend_forward(): pl.pallas_call(functools.partial(attn_fwd_kernel, heads, size, group), gr...  53 us
    ppermute x45, starting transfers between devices, swap(): return lax.ppermute(value, EVERY, flipped(axis_bit, count))  35.4 us
    pallas_call x2, Pallas kernels, ffn_forward(): pl.pallas_call(ffn_fwd_kernel, grid=(hidden // wide,), in_specs=[whole((r...  34.6 us
    all_to_all x4, waiting for transfers between devices, body(): lax.all_to_all(part, 'heads', split_axis=0, concat_axis=0, tiled=True)  34.4 us
  transfers between devices with their start and end apart: 65, of which 29 were waited for; matrix products, arithmetic and copies ran while one was open for 19% of the time, Pallas kernels for 23%

profile of v1, /device:TPU:0, one launch (start us, length us, event | category | flops | bytes accessed | tf_op | source)
XLA Modules:
  0.0 743.5 jit_solution(5799700589687533241)
XLA Ops:
  10.8 17.1 %ffn_forward.2 = (f32[512,1024]{1,0:T(8,128)}, f32[512,4096]{1,0:T(8,128)}) custom-call(bf16[512,1024]{1,0:T(8,128)(2,1)} %bitcast.211, f32[1,1024]{1,0:T(1,128)} %get-tuple-element.200.gain_ref, bf16[1024,4096]{1,0:T(8,128)(2,1)} %win_ref.7, bf16[4096,1024]{1,0:T(8,128)(2,1)} %wout_ref.7), custom_call_target="tpu_custom_call" | custom-call | flops 8589934592 | bytes 25165824 | tf_op jit(solution)/shard_map/ffn_forward/pallas_call | solution.py:376
  27.9 8.9 %qkv_forward.1 = (bf16[8,3,256,128]{3,2,1,0:T(8,128)(2,1)}, bf16[8,3,256,128]{3,2,1,0:T(8,128)(2,1)}) custom-call(f32[512,1024]{1,0:T(8,128)} %get-tuple-element.40.x_ref.refs_2_, f32[1,1024]{1,0:T(1,128)} %get-tuple-element.199.gain_ref.refs_3_, bf16[1024,3072]{1,0:T(8,128)(2,1)} %refs_5_.1, bf16[1024,3072]{1,0:T(8,128)(2,1)} %refs_5_.1, ...), custom_call_target="tpu_custom_call" | custom-call | flops 3221225472 | bytes 11534336 | tf_op jit(solution)/shard_map/qkv_forward/pallas_call | solution.py:571
  36.8 6.5 all-to-all-start.2
  49.9 31.3 %all-to-all-done.2.qkv_ref = bf16[8,3,256,128]{3,2,1,0:T(8,128)(2,1)} async-done(((bf16[8,3,256,128]{3,2,1,0:T(8,128)(2,1)}), bf16[8,3,256,128]{3,2,1,0:T(8,128)(2,1)}, u32[]{:S(2)}, u32[]{:S(2)}) %all-to-all-start.2) | async-done | bytes 1572896 | tf_op jit(solution)/shard_map/all_to_all | solution.py:806
  81.2 4.3 all-to-all-start
  92.9 3.1 fusion.39.segc_ref
  96.0 22.1 %attend_forward.3 = (bf16[2048,128]{1,0:T(8,128)(2,1)}, f32[2048,128]{1,0:T(8,128)}, f32[2,2048,128]{2,1,0:T(8,128)}) custom-call(s32[8]{0:T(128)} %and_select_fusion.4.low_ref, s32[8]{0:T(128)} %and_select_fusion.3.high_ref, bf16[8,3,256,128]{3,2,1,0:T(8,128)(2,1)} %all-to-all-done.2.qkv_ref, s32[2048,1]{1,0:T(8,128)} %fusion.43.segc_ref), custom_call_target="tpu_custom_call" | custom-call | flops 8589934592 | bytes 6291456 | tf_op jit(solution)/shard_map/attend_forward/pallas_call | solution.py:187
  123.3 4.1 all-to-all-start.3
  128.0 30.9 %attend_forward.2 = (bf16[2048,128]{1,0:T(8,128)(2,1)}, f32[2048,128]{1,0:T(8,128)}, f32[2,2048,128]{2,1,0:T(8,128)}) custom-call(s32[8]{0:T(128)} %and_select_fusion.6.low_ref, s32[8]{0:T(128)} %and_select_fusion.5.high_ref, bf16[8,3,256,128]{3,2,1,0:T(8,128)(2,1)} %all-to-all-done.qkv_ref, s32[2048,1]{1,0:T(8,128)} %fusion.39.segc_ref), custom_call_target="tpu_custom_call" | custom-call | flops 8589934592 | bytes 6291456 | tf_op jit(solution)/shard_map/attend_forward/pallas_call | solution.py:187
  161.0 16.4 %all-to-all-start.1 = ((bf16[8,256,128]{1,2,0:T(8,128)(2,1)}), bf16[8,256,128]{1,2,0:T(8,128)(2,1)}, u32[]{:S(2)}, u32[]{:S(2)}) async-start(bf16[8,256,128]{1,2,0:T(8,128)(2,1)} %copy.47), calls=%async_computation.1 | async-start | bytes 1048576 | tf_op jit(solution)/shard_map/all_to_all | solution.py:814
  179.2 13.6 %all-to-all-done.1 = bf16[8,256,128]{1,2,0:T(8,128)(2,1)} async-done(((bf16[8,256,128]{1,2,0:T(8,128)(2,1)}), bf16[8,256,128]{1,2,0:T(8,128)(2,1)}, u32[]{:S(2)}, u32[]{:S(2)}) %all-to-all-start.1) | async-done | bytes 524320 | tf_op jit(solution)/shard_map/all_to_all | solution.py:814
  192.8 4.0 fusion.121
  214.7 17.5 %ffn_forward.3 = (f32[512,1024]{1,0:T(8,128)}, f32[512,4096]{1,0:T(8,128)}) custom-call(f32[512,1024]{1,0:T(8,128)} %convolution_add_fusion.x_ref, f32[1,1024]{1,0:T(1,128)} %get-tuple-element.201.gain_ref, bf16[1024,4096]{1,0:T(8,128)(2,1)} %win_ref.6, bf16[4096,1024]{1,0:T(8,128)(2,1)} %wout_ref.6), custom_call_target="tpu_custom_call" | custom-call | flops 8589934592 | bytes 25165824 | tf_op jit(solution)/shard_map/ffn_forward/pallas_call | solution.py:376
  240.0 31.0 %ffn_backward.2 = (f32[512,1024]{1,0:T(8,128)}, f32[1,1024]{1,0:T(1,128)}, bf16[4,128,4096]{2,1,0:T(8,128)(2,1)}, bf16[4,128,4096]{2,1,0:T(8,128)(2,1)}, bf16[4,...) custom-call(s32[1]{0:T(128)} %bitcast.28.core_ref, f32[512,1024]{1,0:T(8,128)} %convolution_add_fusion.x_ref, ...), custom_call_target="tpu_custom_call" | custom-call | flops 17179869184 | bytes 46137344 | tf_op jit(solution)/shard_map/ffn_backward/pallas_call | solution.py:500
  292.9 3.3 multiply_reduce_fusion.2
  300.4 4.3 all-to-all-start.4
  304.8 4.5 convolution_convert_fusion.2
  313.2 4.7 convolution_convert_fusion
  320.5 4.3 all-to-all-start.6
  324.7 39.8 %attend_backward.2 = bf16[8,3,256,128]{3,2,1,0:T(8,128)(2,1)} custom-call(s32[8]{0:T(128)} %and_select_fusion.6.low_ref, s32[8]{0:T(128)} %and_select_fusion.5.high_ref, bf16[8,3,256,128]{3,2,1,0:T(8,128)(2,1)} %all-to-all-done.qkv_ref, s32[2048,1]{1,0:T(8,128)} %fusion.39.segc_ref, f32[2048,128]{1,0:T(8,128)} %get-tuple-element.46.full_ref, ...), custom_call_target="tpu_custom_call" | custom-call | flops 17179869184 | bytes 9437184 | tf_op jit(solution)/shard_map/attend_backward/pallas_call | solution.py:320
  364.5 5.1 all-to-all-start.5
  369.7 28.6 %attend_backward.3 = bf16[8,3,256,128]{3,2,1,0:T(8,128)(2,1)} custom-call(s32[8]{0:T(128)} %and_select_fusion.4.low_ref, s32[8]{0:T(128)} %and_select_fusion.3.high_ref, bf16[8,3,256,128]{3,2,1,0:T(8,128)(2,1)} %all-to-all-done.2.qkv_ref, s32[2048,1]{1,0:T(8,128)} %fusion.43.segc_ref, f32[2048,128]{1,0:T(8,128)} %get-tuple-element.50.full_ref, ...), custom_call_target="tpu_custom_call" | custom-call | flops 17179869184 | bytes 9437184 | tf_op jit(solution)/shard_map/attend_backward/pallas_call | solution.py:320
  403.8 5.1 collective-permute-done.37
  410.9 5.9 collective-permute-done.27
  425.3 4.5 all-to-all-start.7
  437.5 10.0 %collective-permute-done.32 = bf16[4,128,512]{2,1,0:T(8,128)(2,1)S(1)} collective-permute-done((bf16[4,128,512]{2,1,0:T(8,128)(2,1)S(1)}, bf16[4,128,512]{2,1,0:T(8,128)(2,1)S(1)}, u32[]{:S(2)}, u32[]{:S(2)}) %collective-permute-start.32) | collective-permute-done | bytes 524320 | tf_op jit(solution)/shard_map/ppermute | solution.py:692
  452.2 4.4 collective-permute-done.33
  459.9 16.2 %all-to-all-done.7.refs_1_ = bf16[8,3,256,128]{3,2,1,0:T(8,128)(2,1)} async-done(((bf16[8,3,256,128]{3,2,1,0:T(8,128)(2,1)}), bf16[8,3,256,128]{3,2,1,0:T(8,128)(2,1)}, u32[]{:S(2)}, u32[]{:S(2)}) %all-to-all-start.7) | async-done | bytes 1572896 | tf_op jit(solution)/shard_map/all_to_all | solution.py:892
  476.1 19.5 %qkv_backward.1 = (f32[512,1024]{1,0:T(8,128)}, f32[1,1024]{1,0:T(1,128)}, bf16[4,128,3072]{2,1,0:T(8,128)(2,1)}, bf16[4,128,3072]{2,1,0:T(8,128)(2,1)}) custom-call(s32[1]{0:T(128)} %bitcast.28.core_ref, bf16[8,3,256,128]{3,2,1,0:T(8,128)(2,1)} %all-to-all-done.5.refs_0_, bf16[8,3,256,128]{3,2,1,0:T(8,128)(2,1)} %all-to-all-done.7.refs_1_, ...), custom_call_target="tpu_custom_call" | custom-call | flops 6442450944 | bytes 23068672 | tf_op jit(solution)/shard_map/qkv_backward/pallas_call | solution.py:667
  495.7 3.7 add_convert_fusion.1
  505.0 3.7 add_convert_fusion
  513.4 30.6 %ffn_backward.3 = (bf16[512,1024]{1,0:T(8,128)(2,1)}, f32[1,1024]{1,0:T(1,128)}, bf16[4,128,4096]{2,1,0:T(8,128)(2,1)}, bf16[4,128,4096]{2,1,0:T(8,128)(2,1)}, b...) custom-call(s32[1]{0:T(128)} %bitcast.28.core_ref, bf16[512,1024]{1,0:T(8,128)(2,1)} %bitcast.212, ...), custom_call_target="tpu_custom_call" | custom-call | flops 17179869184 | bytes 46137344 | tf_op jit(solution)/shard_map/ffn_backward/pallas_call | solution.py:500
  544.0 5.4 collective-permute-done.47
  557.4 7.8 %collective-permute-done.48 = bf16[4,64,1024]{2,1,0:T(8,128)(2,1)S(1)} collective-permute-done((bf16[4,64,1024]{2,1,0:T(8,128)(2,1)S(1)}, bf16[4,64,1024]{2,1,0:T(8,128)(2,1)S(1)}, u32[]{:S(2)}, u32[]{:S(2)}) %collective-permute-start.48) | collective-permute-done | bytes 524320 | tf_op jit(solution)/shard_map/ppermute | solution.py:692
  571.4 4.0 add_convert_fusion.4
  585.4 12.2 %collective-permute-done.22 = bf16[4,128,768]{2,1,0:T(8,128)(2,1)} collective-permute-done((bf16[4,128,768]{2,1,0:T(8,128)(2,1)}, bf16[4,128,768]{2,1,0:T(8,128)(2,1)}, u32[]{:S(2)}, u32[]{:S(2)}) %collective-permute-start.22) | collective-permute-done | bytes 786464 | tf_op jit(solution)/shard_map/ppermute | solution.py:692
  603.2 5.0 add_convert_fusion.2
  612.7 3.8 add_convert_fusion.3
  625.4 11.1 %collective-permute-done.17 = bf16[4,128,1024]{2,1,0:T(8,128)(2,1)S(1)} collective-permute-done((bf16[4,128,1024]{2,1,0:T(8,128)(2,1)}, bf16[4,128,1024]{2,1,0:T(8,128)(2,1)S(1)}, u32[]{:S(2)}, u32[]{:S(2)}) %collective-permute-start.17) | collective-permute-done | bytes 1048608 | tf_op jit(solution)/shard_map/ppermute | solution.py:692
  638.8 7.1 collective-permute-done.15
  649.7 7.3 collective-permute-done.18
  658.4 9.0 %collective-permute-done.16 = bf16[4,64,1024]{2,1,0:T(8,128)(2,1)S(1)} collective-permute-done((bf16[4,64,1024]{2,1,0:T(8,128)(2,1)S(1)}, bf16[4,64,1024]{2,1,0:T(8,128)(2,1)S(1)}, u32[]{:S(2)}, u32[]{:S(2)}) %collective-permute-start.16) | collective-permute-done | bytes 524320 | tf_op jit(solution)/shard_map/ppermute | solution.py:692
  672.0 7.6 %collective-permute-done.10 = bf16[4,128,1024]{2,1,0:T(8,128)(2,1)} collective-permute-done((bf16[4,128,1024]{2,1,0:T(8,128)(2,1)}, bf16[4,128,1024]{2,1,0:T(8,128)(2,1)}, u32[]{:S(2)}, u32[]{:S(2)}) %collective-permute-start.10) | collective-permute-done | bytes 1048608 | tf_op jit(solution)/shard_map/ppermute | solution.py:692
  681.5 6.3 collective-permute-done.13
  697.0 3.4 collective-permute-done.4
  700.9 3.8 collective-permute-done.5
  707.6 6.5 collective-permute-done.7
  715.8 8.4 %collective-permute-done.8 = f32[11,1024]{1,0:T(8,128)S(1)} collective-permute-done((f32[11,1024]{1,0:T(8,128)S(1)}, f32[11,1024]{1,0:T(8,128)S(1)}, u32[]{:S(2)}, u32[]{:S(2)}) %collective-permute-start.8) | collective-permute-done | bytes 45088 | tf_op jit(solution)/shard_map/ppermute | solution.py:692
  (414 shorter events, 204.4 us)
Async XLA Ops:
  36.8 44.4 %all-to-all-start.2 = ((bf16[8,3,256,128]{3,2,1,0:T(8,128)(2,1)}), bf16[8,3,256,128]{3,2,1,0:T(8,128)(2,1)}, u32[]{:S(2)}, u32[]{:S(2)}) async-start(bf16[8,3,256,128]{3,2,1,0:T(8,128)(2,1)} %get-tuple-element.43), calls=%async_computation.2 | async-start | bytes 3145728 | tf_op jit(solution)/shard_map/all_to_all | solution.py:806
  81.2 42.1 %all-to-all-start = ((bf16[8,3,256,128]{3,2,1,0:T(8,128)(2,1)}), bf16[8,3,256,128]{3,2,1,0:T(8,128)(2,1)}, u32[]{:S(2)}, u32[]{:S(2)}) async-start(bf16[8,3,256,128]{3,2,1,0:T(8,128)(2,1)} %get-tuple-element.41), calls=%async_computation | async-start | bytes 3145728 | tf_op jit(solution)/shard_map/all_to_all | solution.py:806
  123.3 37.7 %all-to-all-start.3 = ((bf16[8,256,128]{1,2,0:T(8,128)(2,1)}), bf16[8,256,128]{1,2,0:T(8,128)(2,1)}, u32[]{:S(2)}, u32[]{:S(2)}) async-start(bf16[8,256,128]{1,2,0:T(8,128)(2,1)} %copy.48), calls=%async_computation.3 | async-start | bytes 1048576 | tf_op jit(solution)/shard_map/all_to_all | solution.py:814
  161.0 31.8 %all-to-all-start.1 = ((bf16[8,256,128]{1,2,0:T(8,128)(2,1)}), bf16[8,256,128]{1,2,0:T(8,128)(2,1)}, u32[]{:S(2)}, u32[]{:S(2)}) async-start(bf16[8,256,128]{1,2,0:T(8,128)(2,1)} %copy.47), calls=%async_computation.1 | async-start | bytes 1048576 | tf_op jit(solution)/shard_map/all_to_all | solution.py:814
  283.9 114.4 %collective-permute-start.34 = (bf16[4,128,1024]{2,1,0:T(8,128)(2,1)}, bf16[4,128,1024]{2,1,0:T(8,128)(2,1)}, u32[]{:S(2)}, u32[]{:S(2)}) collective-permute-start(bf16[4,128,1024]{2,1,0:T(8,128)(2,1)} %dynamic-slice_bitcast_fusion.1), channel_id=1, source_target_pairs={{0,1},{1,0},{2,3},{3,2},{4,5},{5,4},{6,7},{7,6},{8,9},{9,8},{10,11... | collective-permute-start | bytes 3145736 | tf_op jit(solution)/shard_map/ppermute | solution.py:692
  286.9 208.8 %collective-permute-start.39 = (bf16[4,128,4096]{2,1,0:T(8,128)(2,1)}, bf16[4,128,4096]{2,1,0:T(8,128)(2,1)}, u32[]{:S(2)}, u32[]{:S(2)}) collective-permute-start(bf16[4,128,4096]{2,1,0:T(8,128)(2,1)} %get-tuple-element.65), channel_id=1, source_target_pairs={{0,1},{1,0},{2,3},{3,2},{4,5},{5,4},{6,7},{7,6},{8,9},{9,8},{10,11... | collective-permute-start | bytes 12582920 | tf_op jit(solution)/shard_map/ppermute | solution.py:692
  286.9 217.5 %collective-permute-start.44 = (bf16[4,128,4096]{2,1,0:T(8,128)(2,1)}, bf16[4,128,4096]{2,1,0:T(8,128)(2,1)}, u32[]{:S(2)}, u32[]{:S(2)}) collective-permute-start(bf16[4,128,4096]{2,1,0:T(8,128)(2,1)} %get-tuple-element.67), channel_id=1, source_target_pairs={{0,1},{1,0},{2,3},{3,2},{4,5},{5,4},{6,7},{7,6},{8,9},{9,8},{10,11... | collective-permute-start | bytes 12582920 | tf_op jit(solution)/shard_map/ppermute | solution.py:692
  300.4 20.1 %all-to-all-start.4 = ((bf16[8,256,128]{2,1,0:T(8,128)(2,1)}), bf16[8,256,128]{2,1,0:T(8,128)(2,1)}, u32[]{:S(2)}, u32[]{:S(2)}) async-start(bf16[8,256,128]{2,1,0:T(8,128)(2,1)} %bitcast.33), calls=%async_computation.4 | async-start | bytes 1048576 | tf_op jit(solution)/shard_map/all_to_all | solution.py:887
  311.8 88.5 %collective-permute-start.24 = (bf16[4,128,1024]{2,1,0:T(8,128)(2,1)S(1)}, bf16[4,128,1024]{2,1,0:T(8,128)(2,1)}, u32[]{:S(2)}, u32[]{:S(2)}) collective-permute-start(bf16[4,128,1024]{2,1,0:T(8,128)(2,1)S(1)} %dynamic-slice_bitcast_fusion.2), channel_id=1, source_target_pairs={{0,1},{1,0},{2,3},{3,2},{4,5},{5,4},{6,7},{7,6},{8,9},{9,8},{10,11... | collective-permute-start | bytes 3145736 | tf_op jit(solution)/shard_map/ppermute | solution.py:692
  320.5 109.3 %collective-permute-start.29 = (bf16[4,128,2048]{2,1,0:T(8,128)(2,1)}, bf16[4,128,2048]{2,1,0:T(8,128)(2,1)}, u32[]{:S(2)}, u32[]{:S(2)}) collective-permute-start(bf16[4,128,2048]{2,1,0:T(8,128)(2,1)} %dynamic-slice_bitcast_fusion), channel_id=1, source_target_pairs={{0,1},{1,0},{2,3},{3,2},{4,5},{5,4},{6,7},{7,6},{8,9},{9,8},{10,11... | collective-permute-start | bytes 6291464 | tf_op jit(solution)/shard_map/ppermute | solution.py:692
  320.5 44.0 %all-to-all-start.6 = ((bf16[8,256,128]{2,1,0:T(8,128)(2,1)}), bf16[8,256,128]{2,1,0:T(8,128)(2,1)S(1)}, u32[]{:S(2)}, u32[]{:S(2)}) async-start(bf16[8,256,128]{2,1,0:T(8,128)(2,1)} %bitcast.35), calls=%async_computation.6 | async-start | bytes 1048576 | tf_op jit(solution)/shard_map/all_to_all | solution.py:887
  364.5 60.7 %all-to-all-start.5 = ((bf16[8,3,256,128]{3,2,1,0:T(8,128)(2,1)}), bf16[8,3,256,128]{3,2,1,0:T(8,128)(2,1)}, u32[]{:S(2)}, u32[]{:S(2)}) async-start(bf16[8,3,256,128]{3,2,1,0:T(8,128)(2,1)} %attend_backward.2), calls=%async_computation.5 | async-start | bytes 3145728 | tf_op jit(solution)/shard_map/all_to_all | solution.py:892
  369.6 336.5 %reduce-scatter.19.cloned.1.call-start = ((), (), s32[]{:S(2)}) async-start(), calls=%async_computation.21 | async-start | bytes 327680 | tf_op jit(solution)/shard_map/reduce_scatter | solution.py:746
  421.7 13.0 %collective-permute-start.28 = (bf16[4,64,256]{2,1,0:T(8,128)(2,1)}, bf16[4,64,256]{2,1,0:T(8,128)(2,1)S(1)}, u32[]{:S(2)}, u32[]{:S(2)}) collective-permute-start(bf16[4,64,256]{2,1,0:T(8,128)(2,1)} %add_convert_fusion.48), channel_id=1, source_target_pairs={{0,8},{1,9},{2,10},{3,11},{4,12},{5,13},{6,14},{7,15},{8,0},{9,1},... | collective-permute-start | bytes 393224 | tf_op jit(solution)/shard_map/ppermute | solution.py:692
  423.9 12.5 %collective-permute-start.26 = (bf16[4,64,256]{2,1,0:T(8,128)(2,1)}, bf16[4,64,256]{2,1,0:T(8,128)(2,1)}, u32[]{:S(2)}, u32[]{:S(2)}) collective-permute-start(bf16[4,64,256]{2,1,0:T(8,128)(2,1)} %add_convert_fusion.51), channel_id=1, source_target_pairs={{0,16},{1,17},{2,18},{3,19},{4,20},{5,21},{6,22},{7,23},{8,24},{9,... | collective-permute-start | bytes 393224 | tf_op jit(solution)/shard_map/ppermute | solution.py:692
  425.3 50.9 %all-to-all-start.7 = ((bf16[8,3,256,128]{3,2,1,0:T(8,128)(2,1)}), bf16[8,3,256,128]{3,2,1,0:T(8,128)(2,1)}, u32[]{:S(2)}, u32[]{:S(2)}) async-start(bf16[8,3,256,128]{3,2,1,0:T(8,128)(2,1)} %attend_backward.3), calls=%async_computation.7 | async-start | bytes 3145728 | tf_op jit(solution)/shard_map/all_to_all | solution.py:892
  429.8 284.5 %reduce-scatter.15.cloned.1.call-start = ((), (), s32[]{:S(2)}) async-start(), calls=%async_computation.19 | async-start | bytes 327680 | tf_op jit(solution)/shard_map/reduce_scatter | solution.py:746
  433.2 14.4 %collective-permute-start.32 = (bf16[4,128,512]{2,1,0:T(8,128)(2,1)S(1)}, bf16[4,128,512]{2,1,0:T(8,128)(2,1)S(1)}, u32[]{:S(2)}, u32[]{:S(2)}) collective-permute-start(bf16[4,128,512]{2,1,0:T(8,128)(2,1)S(1)} %pad_maximum_fusion.26), channel_id=1, source_target_pairs={{0,16},{1,17},{2,18},{3,19},{4,20},{5,21},{6,22},{7,23},{8,24},{9,... | collective-permute-start | bytes 1572872 | tf_op jit(solution)/shard_map/ppermute | solution.py:692
  434.8 14.2 %collective-permute-start.30 = (bf16[4,128,512]{2,1,0:T(8,128)(2,1)S(1)}, bf16[4,128,512]{2,1,0:T(8,128)(2,1)S(1)}, u32[]{:S(2)}, u32[]{:S(2)}) collective-permute-start(bf16[4,128,512]{2,1,0:T(8,128)(2,1)S(1)} %pad_maximum_fusion.25), channel_id=1, source_target_pairs={{0,8},{1,9},{2,10},{3,11},{4,12},{5,13},{6,14},{7,15},{8,0},{9,1},... | collective-permute-start | bytes 1572872 | tf_op jit(solution)/shard_map/ppermute | solution.py:692
  452.2 273.3 %reduce-scatter.17.cloned.1.call-start = ((), (), s32[]{:S(2)}) async-start(), calls=%async_computation.20 | async-start | bytes 655360 | tf_op jit(solution)/shard_map/reduce_scatter | solution.py:746
  459.9 267.2 %reduce-scatter.23.cloned.1.call-start = ((), (), s32[]{:S(2)}) async-start(), calls=%async_computation.23 | async-start | bytes 1310720 | tf_op jit(solution)/shard_map/reduce_scatter | solution.py:746
  495.6 75.7 %collective-permute-start.19 = (bf16[4,128,3072]{2,1,0:T(8,128)(2,1)}, bf16[4,128,3072]{2,1,0:T(8,128)(2,1)}, u32[]{:S(2)}, u32[]{:S(2)}) collective-permute-start(bf16[4,128,3072]{2,1,0:T(8,128)(2,1)} %get-tuple-element.63), channel_id=1, source_target_pairs={{0,1},{1,0},{2,3},{3,2},{4,5},{5,4},{6,7},{7,6},{8,9},{9,8},{10,11... | collective-permute-start | bytes 9437192 | tf_op jit(solution)/shard_map/ppermute | solution.py:692
  501.0 52.5 %collective-permute-start.42 = (bf16[4,128,1024]{2,1,0:T(8,128)(2,1)}, bf16[4,128,1024]{2,1,0:T(8,128)(2,1)S(1)}, u32[]{:S(2)}, u32[]{:S(2)}) collective-permute-start(bf16[4,128,1024]{2,1,0:T(8,128)(2,1)} %pad_maximum_fusion.15), channel_id=1, source_target_pairs={{0,16},{1,17},{2,18},{3,19},{4,20},{5,21},{6,22},{7,23},{8,24},{9,... | collective-permute-start | bytes 3145736 | tf_op jit(solution)/shard_map/ppermute | solution.py:692
  503.6 51.7 %collective-permute-start.40 = (bf16[4,128,1024]{2,1,0:T(8,128)(2,1)}, bf16[4,128,1024]{2,1,0:T(8,128)(2,1)}, u32[]{:S(2)}, u32[]{:S(2)}) collective-permute-start(bf16[4,128,1024]{2,1,0:T(8,128)(2,1)} %pad_maximum_fusion.14), channel_id=1, source_target_pairs={{0,8},{1,9},{2,10},{3,11},{4,12},{5,13},{6,14},{7,15},{8,0},{9,1},... | collective-permute-start | bytes 3145736 | tf_op jit(solution)/shard_map/ppermute | solution.py:692
  510.9 38.5 %collective-permute-start.47 = (bf16[4,128,1024]{2,1,0:T(8,128)(2,1)}, bf16[4,128,1024]{2,1,0:T(8,128)(2,1)}, u32[]{:S(2)}, u32[]{:S(2)}) collective-permute-start(bf16[4,128,1024]{2,1,0:T(8,128)(2,1)} %pad_maximum_fusion.18), channel_id=1, source_target_pairs={{0,16},{1,17},{2,18},{3,19},{4,20},{5,21},{6,22},{7,23},{8,24},{9,... | collective-permute-start | bytes 3145736 | tf_op jit(solution)/shard_map/ppermute | solution.py:692
  512.7 38.9 %collective-permute-start.45 = (bf16[4,128,1024]{2,1,0:T(8,128)(2,1)}, bf16[4,128,1024]{2,1,0:T(8,128)(2,1)S(1)}, u32[]{:S(2)}, u32[]{:S(2)}) collective-permute-start(bf16[4,128,1024]{2,1,0:T(8,128)(2,1)} %pad_maximum_fusion.17), channel_id=1, source_target_pairs={{0,8},{1,9},{2,10},{3,11},{4,12},{5,13},{6,14},{7,15},{8,0},{9,1},... | collective-permute-start | bytes 3145736 | tf_op jit(solution)/shard_map/ppermute | solution.py:692
  549.4 61.3 %collective-permute-start.9 = (bf16[4,128,4096]{2,1,0:T(8,128)(2,1)}, bf16[4,128,4096]{2,1,0:T(8,128)(2,1)}, u32[]{:S(2)}, u32[]{:S(2)}) collective-permute-start(bf16[4,128,4096]{2,1,0:T(8,128)(2,1)} %get-tuple-element.59), channel_id=1, source_target_pairs={{0,1},{1,0},{2,3},{3,2},{4,5},{5,4},{6,7},{7,6},{8,9},{9,8},{10,11... | collective-permute-start | bytes 12582920 | tf_op jit(solution)/shard_map/ppermute | solution.py:692
  551.6 13.6 %collective-permute-start.48 = (bf16[4,64,1024]{2,1,0:T(8,128)(2,1)S(1)}, bf16[4,64,1024]{2,1,0:T(8,128)(2,1)S(1)}, u32[]{:S(2)}, u32[]{:S(2)}) collective-permute-start(bf16[4,64,1024]{2,1,0:T(8,128)(2,1)S(1)} %add_convert_fusion.6), channel_id=1, source_target_pairs={{0,8},{1,9},{2,10},{3,11},{4,12},{5,13},{6,14},{7,15},{8,0},{9,1},... | collective-permute-start | bytes 1572872 | tf_op jit(solution)/shard_map/ppermute | solution.py:692
  553.6 13.6 %collective-permute-start.46 = (bf16[4,64,1024]{2,1,0:T(8,128)(2,1)S(1)}, bf16[4,64,1024]{2,1,0:T(8,128)(2,1)S(1)}, u32[]{:S(2)}, u32[]{:S(2)}) collective-permute-start(bf16[4,64,1024]{2,1,0:T(8,128)(2,1)S(1)} %add_convert_fusion.9), channel_id=1, source_target_pairs={{0,16},{1,17},{2,18},{3,19},{4,20},{5,21},{6,22},{7,23},{8,24},{9,... | collective-permute-start | bytes 1572872 | tf_op jit(solution)/shard_map/ppermute | solution.py:692
  555.3 47.9 %collective-permute-start.14 = (bf16[4,128,4096]{2,1,0:T(8,128)(2,1)}, bf16[4,128,4096]{2,1,0:T(8,128)(2,1)}, u32[]{:S(2)}, u32[]{:S(2)}) collective-permute-start(bf16[4,128,4096]{2,1,0:T(8,128)(2,1)} %get-tuple-element.61), channel_id=1, source_target_pairs={{0,1},{1,0},{2,3},{3,2},{4,5},{5,4},{6,7},{7,6},{8,9},{9,8},{10,11... | collective-permute-start | bytes 12582920 | tf_op jit(solution)/shard_map/ppermute | solution.py:692
  565.2 13.3 %collective-permute-start.43 = (bf16[4,64,1024]{2,1,0:T(8,128)(2,1)}, bf16[4,64,1024]{2,1,0:T(8,128)(2,1)}, u32[]{:S(2)}, u32[]{:S(2)}) collective-permute-start(bf16[4,64,1024]{2,1,0:T(8,128)(2,1)} %add_convert_fusion.12), channel_id=1, source_target_pairs={{0,8},{1,9},{2,10},{3,11},{4,12},{5,13},{6,14},{7,15},{8,0},{9,1},... | collective-permute-start | bytes 1572872 | tf_op jit(solution)/shard_map/ppermute | solution.py:692
  567.2 15.2 %collective-permute-start.41 = (bf16[4,64,1024]{2,1,0:T(8,128)(2,1)}, bf16[4,64,1024]{2,1,0:T(8,128)(2,1)}, u32[]{:S(2)}, u32[]{:S(2)}) collective-permute-start(bf16[4,64,1024]{2,1,0:T(8,128)(2,1)} %add_convert_fusion.15), channel_id=1, source_target_pairs={{0,16},{1,17},{2,18},{3,19},{4,20},{5,21},{6,22},{7,23},{8,24},{9,... | collective-permute-start | bytes 1572872 | tf_op jit(solution)/shard_map/ppermute | solution.py:692
  571.3 157.8 %reduce-scatter.21.cloned.1.call-start = ((), (), s32[]{:S(2)}) async-start(), calls=%async_computation.22 | async-start | bytes 1310720 | tf_op jit(solution)/shard_map/reduce_scatter | solution.py:746
  576.9 20.8 %collective-permute-start.22 = (bf16[4,128,768]{2,1,0:T(8,128)(2,1)}, bf16[4,128,768]{2,1,0:T(8,128)(2,1)}, u32[]{:S(2)}, u32[]{:S(2)}) collective-permute-start(bf16[4,128,768]{2,1,0:T(8,128)(2,1)} %pad_maximum_fusion.21), channel_id=1, source_target_pairs={{0,16},{1,17},{2,18},{3,19},{4,20},{5,21},{6,22},{7,23},{8,24},{9,... | collective-permute-start | bytes 2359304 | tf_op jit(solution)/shard_map/ppermute | solution.py:692
  578.5 21.7 %collective-permute-start.20 = (bf16[4,128,768]{2,1,0:T(8,128)(2,1)}, bf16[4,128,768]{2,1,0:T(8,128)(2,1)}, u32[]{:S(2)}, u32[]{:S(2)}) collective-permute-start(bf16[4,128,768]{2,1,0:T(8,128)(2,1)} %pad_maximum_fusion.20), channel_id=1, source_target_pairs={{0,8},{1,9},{2,10},{3,11},{4,12},{5,13},{6,14},{7,15},{8,0},{9,1},... | collective-permute-start | bytes 2359304 | tf_op jit(solution)/shard_map/ppermute | solution.py:692
  585.2 145.7 %reduce-scatter.13.cloned.1.call-start = ((), (), s32[]{:S(2)}) async-start(), calls=%async_computation.18 | async-start | bytes 983040 | tf_op jit(solution)/shard_map/reduce_scatter | solution.py:746
  598.8 21.7 %collective-permute-start.23 = (bf16[4,64,768]{2,1,0:T(8,128)(2,1)S(1)}, bf16[4,64,768]{2,1,0:T(8,128)(2,1)S(1)}, u32[]{:S(2)}, u32[]{:S(2)}) collective-permute-start(bf16[4,64,768]{2,1,0:T(8,128)(2,1)S(1)} %add_convert_fusion.30), channel_id=1, source_target_pairs={{0,8},{1,9},{2,10},{3,11},{4,12},{5,13},{6,14},{7,15},{8,0},{9,1},... | collective-permute-start | bytes 1179656 | tf_op jit(solution)/shard_map/ppermute | solution.py:692
  601.4 20.4 %collective-permute-start.21 = (bf16[4,64,768]{2,1,0:T(8,128)(2,1)S(1)}, bf16[4,64,768]{2,1,0:T(8,128)(2,1)S(1)}, u32[]{:S(2)}, u32[]{:S(2)}) collective-permute-start(bf16[4,64,768]{2,1,0:T(8,128)(2,1)S(1)} %add_convert_fusion.33), channel_id=1, source_target_pairs={{0,16},{1,17},{2,18},{3,19},{4,20},{5,21},{6,22},{7,23},{8,24},{9,... | collective-permute-start | bytes 1179656 | tf_op jit(solution)/shard_map/ppermute | solution.py:692
  610.2 26.3 %collective-permute-start.17 = (bf16[4,128,1024]{2,1,0:T(8,128)(2,1)}, bf16[4,128,1024]{2,1,0:T(8,128)(2,1)S(1)}, u32[]{:S(2)}, u32[]{:S(2)}) collective-permute-start(bf16[4,128,1024]{2,1,0:T(8,128)(2,1)} %pad_maximum_fusion.12), channel_id=1, source_target_pairs={{0,16},{1,17},{2,18},{3,19},{4,20},{5,21},{6,22},{7,23},{8,24},{9,... | collective-permute-start | bytes 3145736 | tf_op jit(solution)/shard_map/ppermute | solution.py:692
  619.5 26.4 %collective-permute-start.15 = (bf16[4,128,1024]{2,1,0:T(8,128)(2,1)}, bf16[4,128,1024]{2,1,0:T(8,128)(2,1)}, u32[]{:S(2)}, u32[]{:S(2)}) collective-permute-start(bf16[4,128,1024]{2,1,0:T(8,128)(2,1)} %pad_maximum_fusion.11), channel_id=1, source_target_pairs={{0,8},{1,9},{2,10},{3,11},{4,12},{5,13},{6,14},{7,15},{8,0},{9,1},... | collective-permute-start | bytes 3145736 | tf_op jit(solution)/shard_map/ppermute | solution.py:692
  624.0 108.6 %reduce-scatter.11.cloned.1.call-start = ((), (), s32[]{:S(2)}) async-start(), calls=%async_computation.17 | async-start | bytes 1310720 | tf_op jit(solution)/shard_map/reduce_scatter | solution.py:746
  625.2 44.8 %collective-permute-start.12 = (bf16[4,128,1024]{2,1,0:T(8,128)(2,1)}, bf16[4,128,1024]{2,1,0:T(8,128)(2,1)}, u32[]{:S(2)}, u32[]{:S(2)}) collective-permute-start(bf16[4,128,1024]{2,1,0:T(8,128)(2,1)} %pad_maximum_fusion.9), channel_id=1, source_target_pairs={{0,16},{1,17},{2,18},{3,19},{4,20},{5,21},{6,22},{7,23},{8,24},{9,... | collective-permute-start | bytes 3145736 | tf_op jit(solution)/shard_map/ppermute | solution.py:692
  637.8 19.3 %collective-permute-start.18 = (bf16[4,64,1024]{2,1,0:T(8,128)(2,1)S(1)}, bf16[4,64,1024]{2,1,0:T(8,128)(2,1)S(1)}, u32[]{:S(2)}, u32[]{:S(2)}) collective-permute-start(bf16[4,64,1024]{2,1,0:T(8,128)(2,1)S(1)} %add_convert_fusion.18), channel_id=1, source_target_pairs={{0,8},{1,9},{2,10},{3,11},{4,12},{5,13},{6,14},{7,15},{8,0},{9,1},... | collective-permute-start | bytes 1572872 | tf_op jit(solution)/shard_map/ppermute | solution.py:692
  647.3 20.0 %collective-permute-start.16 = (bf16[4,64,1024]{2,1,0:T(8,128)(2,1)S(1)}, bf16[4,64,1024]{2,1,0:T(8,128)(2,1)S(1)}, u32[]{:S(2)}, u32[]{:S(2)}) collective-permute-start(bf16[4,64,1024]{2,1,0:T(8,128)(2,1)S(1)} %add_convert_fusion.21), channel_id=1, source_target_pairs={{0,16},{1,17},{2,18},{3,19},{4,20},{5,21},{6,22},{7,23},{8,24},{9,... | collective-permute-start | bytes 1572872 | tf_op jit(solution)/shard_map/ppermute | solution.py:692
  649.0 30.6 %collective-permute-start.10 = (bf16[4,128,1024]{2,1,0:T(8,128)(2,1)}, bf16[4,128,1024]{2,1,0:T(8,128)(2,1)}, u32[]{:S(2)}, u32[]{:S(2)}) collective-permute-start(bf16[4,128,1024]{2,1,0:T(8,128)(2,1)} %pad_maximum_fusion.8), channel_id=1, source_target_pairs={{0,8},{1,9},{2,10},{3,11},{4,12},{5,13},{6,14},{7,15},{8,0},{9,1},... | collective-permute-start | bytes 3145736 | tf_op jit(solution)/shard_map/ppermute | solution.py:692
  669.9 64.8 %reduce-scatter.9.cloned.1.call-start = ((), (), s32[]{:S(2)}) async-start(), calls=%async_computation.16 | async-start | bytes 1310720 | tf_op jit(solution)/shard_map/reduce_scatter | solution.py:746
  671.4 16.5 %collective-permute-start.13 = (bf16[4,64,1024]{2,1,0:T(8,128)(2,1)S(1)}, bf16[4,64,1024]{2,1,0:T(8,128)(2,1)S(1)}, u32[]{:S(2)}, u32[]{:S(2)}) collective-permute-start(bf16[4,64,1024]{2,1,0:T(8,128)(2,1)S(1)} %add_convert_fusion.24), channel_id=1, source_target_pairs={{0,8},{1,9},{2,10},{3,11},{4,12},{5,13},{6,14},{7,15},{8,0},{9,1},... | collective-permute-start | bytes 1572872 | tf_op jit(solution)/shard_map/ppermute | solution.py:692
  714.2 10.0 %collective-permute-start.8 = (f32[11,1024]{1,0:T(8,128)S(1)}, f32[11,1024]{1,0:T(8,128)S(1)}, u32[]{:S(2)}, u32[]{:S(2)}) collective-permute-start(f32[11,1024]{1,0:T(8,128)S(1)} %add.651), channel_id=1, source_target_pairs={{0,4},{1,5},{2,6},{3,7},{4,0},{5,1},{6,2},{7,3},{8,12},{9,13},{10,... | collective-permute-start | bytes 135176 | tf_op jit(solution)/shard_map/ppermute | solution.py:692
  (81 other events, 888.4 us)
Sparse Core Ops, SparseCore 0:
  425.4 23.5 reduce-scatter.18
  452.3 20.7 reduce-scatter.14
  476.0 23.7 reduce-scatter.16
  571.4 25.0 reduce-scatter.22
  598.7 25.8 reduce-scatter.20
  626.7 21.9 reduce-scatter.12
  670.0 25.1 reduce-scatter.10
  697.6 28.6 reduce-scatter.8

commit v2 on v1

--- a/solution.py
+++ b/solution.py
@@ -78,6 +78,40 @@
     )
 
 
+def segment_bounds(counts, place, group):
+    longs, shorts = counts
+    long_end = longs * LONG
+    short_end = long_end + shorts * SHORT
+    start = jnp.where(place < longs, place * LONG, long_end + (place - longs) * SHORT)
+    size = jnp.where(place < longs, LONG, SHORT)
+    last = place == longs + shorts
+    return (jnp.where(last, short_end, start), jnp.where(last, group, start + size), place <= longs + shorts)
+
+
+def member_lanes(counts, first, rows, group, shift=0):
+    shape = (rows, LANES)
+    place = lax.broadcasted_iota(jnp.int32, (8, LANES), 1) - shift
+    start, end, there = segment_bounds(counts, place, group)
+    start = jnp.where(there & (place >= 0), start, group)
+    start, end = start[:1], end[:1]
+    frame = first + lax.broadcasted_iota(jnp.int32, shape, 0)
+    return (frame >= start) & (frame < end)
+
+
+def block_range(counts, step, group):
+    longs, shorts = counts
+    long_end = longs * LONG
+    short_end = long_end + shorts * SHORT
+
+    def number(frame):
+        place = jnp.where(frame < long_end, frame // LONG, longs + (frame - long_end) // SHORT)
+        return jnp.where(frame < short_end, place, longs + shorts)
+
+    first = segment_bounds(counts, number(step * BLOCK), group)[0]
+    last = segment_bounds(counts, number(step * BLOCK + BLOCK - 1), group)[1]
+    return (first // BLOCK, jnp.minimum(last + BLOCK - 1, group) // BLOCK)
+
+
 def head_lanes(shape, head, size):
     lane = lax.broadcasted_iota(jnp.int32, shape, 1)
     return (lane >= head * size) & (lane < (head + 1) * size)
@@ -98,20 +132,19 @@
     return out
 
 
-def attn_fwd_kernel(heads, size, group, low_ref, high_ref, qkv_ref, segc_ref, out_ref, full_ref, lse_ref, kcat, v_all, s_scr):
+def attn_fwd_kernel(heads, size, group, counts_ref, qkv_ref, out_ref, full_ref, lse_ref, kcat, v_all, s_scr):
     step = pl.program_id(0)
+    counts = (counts_ref[0], counts_ref[1])
     width = heads * size
     blocks = group // BLOCK
 
     @pl.when(step == 0)
     def _():
         k = qkv_ref[:, 1].reshape(group, width)
-        seg = segc_ref[...]
-        lane = lax.broadcasted_iota(jnp.int32, (group, LANES), 1)
         kcat[:, :width] = k
         if width < LANES:
             kcat[:, width:LANES] = jnp.zeros((group, LANES - width), BF16)
-        kcat[:, LANES:] = jnp.where(lane == seg, 0.0, -BIG).astype(BF16)
+        kcat[:, LANES:] = jnp.where(member_lanes(counts, 0, group, group), 0.0, -BIG).astype(BF16)
         v_all[...] = qkv_ref[:, 2].reshape(group, width)
 
     chunk = qkv_ref.shape[2]
@@ -122,8 +155,7 @@
     else:
         q = qkv_ref[pl.ds(step * per, per), 0].reshape(BLOCK, width)
     q = q.astype(F32) * (size ** -0.5)
-    lane = lax.broadcasted_iota(jnp.int32, (BLOCK, LANES), 1)
-    member = jnp.where(lane == segc_ref[rows, :], 1.0, 0.0).astype(BF16)
+    member = jnp.where(member_lanes(counts, step * BLOCK, BLOCK, group), 1.0, 0.0).astype(BF16)
     queries = []
     for head in range(heads):
         mine = q if heads == 1 else jnp.where(head_lanes(q.shape, head, size), q, 0.0)
@@ -131,7 +163,7 @@
         if width < LANES:
             mine = jnp.concatenate([mine, jnp.zeros((BLOCK, LANES - width), BF16)], 1)
         queries.append(jnp.concatenate([mine, member], 1))
-    low, high = low_ref[step], high_ref[step]
+    low, high = block_range(counts, step, group)
 
     def scores(j, tops):
         keys = kcat[pl.ds(pl.multiple_of(j * BLOCK, BLOCK), BLOCK), :]
@@ -178,7 +210,7 @@
     out_ref[...] = result.astype(BF16)
 
 
-def attend_forward(qkv, seg_column, low, high, size):
+def attend_forward(qkv, counts, size):
     sources, _, chunk, width = qkv.shape
     group = sources * chunk
     heads = width // size
@@ -189,9 +221,7 @@
         grid=(steps,),
         in_specs=[
             smem,
-            smem,
             pl.BlockSpec(qkv.shape, lambda i: (0, 0, 0, 0)),
-            pl.BlockSpec((group, 1), lambda i: (0, 0)),
         ],
         out_specs=[
             pl.BlockSpec((BLOCK, width), lambda i: (i, 0)),
@@ -211,11 +241,12 @@
         compiler_params=pltpu.CompilerParams(vmem_limit_bytes=VMEM_LIMIT),
         cost_estimate=pl.CostEstimate(flops=16 * group * group * LANES, bytes_accessed=6 << 20, transcendentals=heads * group * group),
         name="attend_forward",
-    )(low, high, qkv, seg_column)
-
-
-def attn_bwd_kernel(heads, size, group, low_ref, high_ref, qkv_ref, segc_ref, full_ref, lse_ref, grad_ref, out_ref, qcat, gcat, k_turned, dq_turned):
+    )(counts, qkv)
+
+
+def attn_bwd_kernel(heads, size, group, counts_ref, qkv_ref, full_ref, lse_ref, grad_ref, out_ref, qcat, gcat, k_turned, dq_turned):
     step = pl.program_id(0)
+    counts = (counts_ref[0], counts_ref[1])
     width = heads * size
     blocks = group // BLOCK
     chunk = qkv_ref.shape[2]
@@ -243,12 +274,11 @@
         def prepare(j, _):
             rows = pl.ds(pl.multiple_of(j * BLOCK, BLOCK), BLOCK)
             lane = lax.broadcasted_iota(jnp.int32, (BLOCK, LANES), 1)
-            seg = segc_ref[rows, :]
             q = widened(block_of(0, j).astype(F32) * (size ** -0.5))
             g = widened(grad_of(j).astype(F32))
             o = widened(full_ref[rows, :])
             product = g * o
-            member = jnp.where(lane == seg + 3, 1.0, 0.0)
+            member = jnp.where(member_lanes(counts, j * BLOCK, BLOCK, group, 3), 1.0, 0.0)
             for head in range(heads):
                 own = head_lanes((BLOCK, LANES), head, size)
                 lse = lse_ref[head, rows, :]
@@ -266,8 +296,8 @@
 
     lane = lax.broadcasted_iota(jnp.int32, (BLOCK, LANES), 1)
     rows = pl.ds(pl.multiple_of(step * BLOCK, BLOCK), BLOCK)
-    seg = segc_ref[rows, :]
-    tail = jnp.where(lane < 3, 1.0, jnp.where(lane == seg + 3, 0.0, -BIG)).astype(BF16)
+    member = member_lanes(counts, step * BLOCK, BLOCK, group, 3)
+    tail = jnp.where(lane < 3, 1.0, jnp.where(member, 0.0, -BIG)).astype(BF16)
     keys = jnp.concatenate([widened(block_of(1, step)), tail], 1)
     ones = jnp.where(lane < 3, 1.0, 0.0).astype(BF16)
     values = jnp.concatenate([widened(block_of(2, step)), ones], 1)
@@ -287,7 +317,8 @@
         return (dk, dv)
 
     zero = jnp.zeros((BLOCK, LANES), F32)
-    dk, dv = lax.fori_loop(low_ref[step], high_ref[step], one, (zero, zero))
+    low, high = block_range(counts, step, group)
+    dk, dv = lax.fori_loop(low, high, one, (zero, zero))
     dk = dk[:, :width].astype(BF16)
     dv = dv[:, :width].astype(BF16)
     if BLOCK == chunk:
@@ -310,21 +341,18 @@
         lax.fori_loop(0, blocks, finish, 0)
 
 
-def attend_backward(qkv, seg_column, low, high, size, full, lse, grad):
+def attend_backward(qkv, counts, size, full, lse, grad):
     sources, _, chunk, width = qkv.shape
     group = sources * chunk
     heads = width // size
     steps = group // BLOCK
     smem = pl.BlockSpec(memory_space=pltpu.SMEM)
-    whole = lambda shape: pl.BlockSpec(shape, lambda i: (0,) * len(shape))
     return pl.pallas_call(
         functools.partial(attn_bwd_kernel, heads, size, group),
         grid=(steps,),
         in_specs=[
             smem,
-            smem,
             whole(qkv.shape),
-            whole((group, 1)),
             whole(full.shape),
             whole(lse.shape),
             whole(grad.shape),
@@ -340,15 +368,11 @@
         compiler_params=pltpu.CompilerParams(vmem_limit_bytes=VMEM_LIMIT),
         cost_estimate=pl.CostEstimate(flops=32 * group * group * LANES, bytes_accessed=9 << 20, transcendentals=heads * group * group),
         name="attend_backward",
-    )(low, high, qkv, seg_column, full, lse, grad)
-
-
-def block_ranges(seg):
-    blocks = seg.reshape(-1, BLOCK)
-    first, last = blocks[:, 0], blocks[:, -1]
-    low = jnp.sum(seg[None, :] < first[:, None], 1) // BLOCK
-    high = (jnp.sum(seg[None, :] <= last[:, None], 1) + BLOCK - 1) // BLOCK
-    return (low.astype(jnp.int32), high.astype(jnp.int32))
+    )(counts, qkv, full, lse, grad)
+
+
+def half_gate(field):
+    return 0.5 * jnp.tanh(0.5 * field) + 0.5
 
 
 def ffn_fwd_kernel(x_ref, gain_ref, win_ref, wout_ref, out_ref, pre_ref, entered, total):
@@ -361,7 +385,7 @@
 
     pre = dot(entered[...], win_ref[...])
     pre_ref[...] = pre
-    hidden = (pre * jax.nn.sigmoid(pre)).astype(BF16)
+    hidden = (pre * half_gate(pre)).astype(BF16)
     total[...] += dot(hidden, wout_ref[...])
 
     @pl.when(step == pl.num_programs(0) - 1)
@@ -405,51 +429,94 @@
         target[pl.ds(pl.multiple_of(place, rows_each), rows_each), :] = part
 
 
+def ffn_out_kernel(core_ref, up_ref, pre_ref, keep, send, turned_up):
+    step = pl.program_id(0)
+    model = up_ref.shape[1]
+    items, _, rows_each, wide_each = keep.shape
+
+    @pl.when(step == 0)
+    def _():
+        turned_up[...] = jnp.transpose(0.5 * up_ref[...]).astype(BF16)
+
+    pre = pre_ref[...]
+    hidden = (pre * half_gate(pre)).astype(BF16)
+    grad = dot(turned_up[...], hidden).astype(BF16)
+    wide = grad.shape[1]
+    parts = model // rows_each // items
+
+    def place(target):
+        for group in range(model // rows_each):
+            part = group % parts
+            target[group // parts, 0, :, part * wide : (part + 1) * wide] = grad[
+                group * rows_each : (group + 1) * rows_each
+            ]
+
+    @pl.when(step % 2 == 0)
+    def _():
+        place(keep)
+
+    @pl.when(step % 2 == 1)
+    def _():
+        place(send)
+
+
+def paired(s, core):
+    return 2 * (s // 2) + (s + core[0]) % 2
+
+
+def ffn_out_grad(upstream, pre_act, heads, core, items):
+    rows, model = upstream.shape
+    hidden = pre_act.shape[1]
+    wide = hidden // heads
+    rows_each = model // heads
+    share = jax.ShapeDtypeStruct((items, heads // 2, rows_each, hidden // items), BF16)
+    block = pl.BlockSpec(
+        (items, 1, rows_each, hidden // items), lambda s, core: (0, s // 2, 0, 0)
+    )
+    grid_spec = pltpu.PrefetchScalarGridSpec(
+        num_scalar_prefetch=1,
+        grid=(heads,),
+        in_specs=[
+            whole((rows, model)),
+            pl.BlockSpec((rows, wide), lambda s, core: (0, paired(s, core))),
+        ],
+        out_specs=[block, block],
+        scratch_shapes=[pltpu.VMEM((model, rows), BF16)],
+    )
+    return pl.pallas_call(
+        ffn_out_kernel,
+        grid_spec=grid_spec,
+        out_shape=[share, share],
+        compiler_params=compiler_params(),
+        cost_estimate=cost(2 * rows * model * hidden, 2 * model * hidden + 4 * rows * hidden),
+        name="ffn_out_grad",
+    )(core, upstream, pre_act)
+
+
 def ffn_bwd_kernel(
     core_ref, x_ref, gain_ref, up_ref, pre_ref, win_ref, wout_ref,
-    down_ref, gain_grad_ref, in_keep, in_send, out_keep, out_send,
-    entered, turned, turned_up, total,
+    down_ref, gain_grad_ref, keep, send, entered, turned, total,
 ):
     step = pl.program_id(0)
-    core = core_ref[0]
     model = x_ref.shape[1]
-    rows_each = in_keep.shape[1]
+    rows_each = keep.shape[2]
     half = model // 2
 
     @pl.when(step == 0)
     def _():
         shaped = layer_norm(x_ref[...].astype(F32), gain_ref[...])[0]
-        turned_rows(shaped, rows_each, core, turned)
-        halved = 0.5 * up_ref[...]
-        turned_up[...] = jnp.transpose(halved).astype(BF16)
-        entered[...] = halved.astype(BF16)
+        turned_rows(shaped, rows_each, core_ref[0], turned)
+        entered[...] = (0.5 * up_ref[...]).astype(BF16)
         total[...] = jnp.zeros_like(total)
 
     pre = pre_ref[...]
-    gate = jax.nn.sigmoid(pre)
-    hidden = (pre * gate).astype(BF16)
+    gate = half_gate(pre)
     grad_hidden = dot(entered[...], wout_ref[...], NT)
     grad_pre = (grad_hidden * (gate * (1.0 + pre * (1.0 - gate)))).astype(BF16)
     total[...] += dot(grad_pre, win_ref[...], NT)
     grad_in = dot(turned[...], grad_pre).astype(BF16)
-    in_keep[...] = grad_in[:half].reshape(in_keep.shape)
-    in_send[...] = grad_in[half:].reshape(in_send.shape)
-    grad_out = dot(turned_up[...], hidden).astype(BF16)
-    wide = grad_out.shape[1]
-
-    def place(target):
-        for group in range(model // rows_each):
-            target[0, :, group * wide : (group + 1) * wide] = grad_out[
-                group * rows_each : (group + 1) * rows_each
-            ]
-
-    @pl.when(step % 2 == 0)
-    def _():
-        place(out_keep)
-
-    @pl.when(step % 2 == 1)
-    def _():
-        place(out_send)
+    keep[...] = grad_in[:half].reshape(keep.shape)
+    send[...] = grad_in[half:].reshape(send.shape)
 
     @pl.when(step == pl.num_programs(0) - 1)
     def _():
@@ -460,17 +527,17 @@
         gain_grad_ref[...] = grad_gain
 
 
-def ffn_backward(upstream, stream, pre_act, gain_row, weight_in, weight_out, heads, core, down_type):
+def ffn_backward(
+    upstream, stream, pre_act, gain_row, weight_in, weight_out, heads, core, items, down_type
+):
     rows, model = stream.shape
     hidden = weight_in.shape[1]
     wide = hidden // heads
     rows_each = model // heads
     places = heads // 2
-
-    def at(s, core):
-        return 2 * (s // 2) + (s + core[0]) % 2
-
-    share = jax.ShapeDtypeStruct((places, rows_each, hidden), BF16)
+    each = hidden // items // wide
+    share = jax.ShapeDtypeStruct((items, places, rows_each, hidden // items), BF16)
+    block = pl.BlockSpec((1, places, rows_each, wide), lambda s, core: (s // each, 0, 0, s % each))
     grid_spec = pltpu.PrefetchScalarGridSpec(
         num_scalar_prefetch=1,
         grid=(heads,),
@@ -478,21 +545,13 @@
             whole((rows, model)),
             whole((1, model)),
             whole((rows, model)),
-            pl.BlockSpec((rows, wide), lambda s, core: (0, at(s, core))),
-            pl.BlockSpec((model, wide), lambda s, core: (0, at(s, core))),
-            pl.BlockSpec((wide, model), lambda s, core: (at(s, core), 0)),
-        ],
-        out_specs=[
-            whole((rows, model)),
-            whole((1, model)),
-            pl.BlockSpec((places, rows_each, wide), lambda s, core: (0, 0, at(s, core))),
-            pl.BlockSpec((places, rows_each, wide), lambda s, core: (0, 0, at(s, core))),
-            pl.BlockSpec((1, rows_each, hidden), lambda s, core: (s // 2, 0, 0)),
-            pl.BlockSpec((1, rows_each, hidden), lambda s, core: (s // 2, 0, 0)),
-        ],
+            pl.BlockSpec((rows, wide), lambda s, core: (0, s)),
+            pl.BlockSpec((model, wide), lambda s, core: (0, s)),
+            pl.BlockSpec((wide, model), lambda s, core: (s, 0)),
+        ],
+        out_specs=[whole((rows, model)), whole((1, model)), block, block],
         scratch_shapes=[
             pltpu.VMEM((rows, model), BF16),
-            pltpu.VMEM((model, rows), BF16),
             pltpu.VMEM((model, rows), BF16),
             pltpu.VMEM((rows, model), F32),
         ],
@@ -503,11 +562,12 @@
         out_shape=[
             jax.ShapeDtypeStruct((rows, model), down_type),
             jax.ShapeDtypeStruct((1, model), F32),
-            share, share, share, share,
+            share,
+            share,
         ],
         compiler_params=compiler_params(),
         cost_estimate=cost(
-            8 * rows * model * hidden, 8 * model * hidden + 4 * rows * hidden + 8 * rows * model
+            6 * rows * model * hidden, 6 * model * hidden + 4 * rows * hidden + 8 * rows * model
         ),
         name="ffn_backward",
     )(core, stream, gain_row, upstream, pre_act, weight_in, weight_out)
@@ -598,7 +658,7 @@
      down_ref, gain_grad_ref, keep, send, turned, total) = refs
     step = pl.program_id(0)
     model = x_ref.shape[1]
-    rows_each = keep.shape[1]
+    rows_each = keep.shape[2]
     half = model // 2
 
     @pl.when(step == 0)
@@ -629,7 +689,7 @@
         gain_grad_ref[...] = grad_gain
 
 
-def qkv_backward(backs, stream, gain_row, upstream, weight, cosines, sines, heads, core, size):
+def qkv_backward(backs, stream, gain_row, upstream, weight, cosines, sines, heads, core, items, size):
     rows, model = stream.shape
     wide = cosines.shape[1]
     steps = model // wide
@@ -638,7 +698,9 @@
     rows_each = model // heads
     places = heads // 2
     batches = len(backs)
-    share = jax.ShapeDtypeStruct((places, rows_each, 3 * model), BF16)
+    share = jax.ShapeDtypeStruct((items, places, rows_each, 3 * model // items), BF16)
+    each = 3 * model // items // wide
+    block = pl.BlockSpec((1, places, rows_each, wide), lambda s, core: (s // each, 0, 0, s % each))
     grid_spec = pltpu.PrefetchScalarGridSpec(
         num_scalar_prefetch=1,
         grid=(3 * steps,),
@@ -659,8 +721,8 @@
         out_specs=[
             whole((rows, model)),
             whole((1, model)),
-            pl.BlockSpec((places, rows_each, wide), lambda s, core: (0, 0, s)),
-            pl.BlockSpec((places, rows_each, wide), lambda s, core: (0, 0, s)),
+            block,
+            block,
         ],
         scratch_shapes=[pltpu.VMEM((model, rows), BF16), pltpu.VMEM((rows, model), F32)],
     )
@@ -692,61 +754,79 @@
     return lax.ppermute(value, EVERY, flipped(axis_bit, count))
 
 
-def plus(left, right):
-    return (left.astype(F32) + right.astype(F32)).astype(BF16)
+def plus(*terms):
+    total = terms[0].astype(F32)
+    for term in terms[1:]:
+        total = total + term.astype(F32)
+    return total.astype(BF16)
 
 
 def halves(value, rows_each):
     places = value.shape[0] // (2 * rows_each)
-    cut = value.reshape(places, 2, rows_each, value.shape[1])
+    items = lax.axis_size("items")
+    cut = value.reshape(places, 2, rows_each, items, -1).transpose(1, 3, 0, 2, 4)
     core = lax.axis_index("heads") % 2
     return tuple(
-        lax.dynamic_index_in_dim(cut, which, 1, keepdims=False) for which in (core, 1 - core)
-    )
-
-
-def columns(value, start, size):
-    return lax.dynamic_slice_in_dim(value, start * size, size, 2)
-
-
-def scatter(keep, send):
-    items = lax.axis_size("items")
-    value = plus(keep, swap(send, ("heads", 1)))
-    places, rows, wide = value.shape
-    size = wide // items
-    if items == 4:
+        lax.dynamic_index_in_dim(cut, which, 0, keepdims=False) for which in (core, 1 - core)
+    )
+
+
+def pick(value, place, dim):
+    return lax.dynamic_index_in_dim(value, place, dim, keepdims=False)
+
+
+class Scatter:
+    def __init__(self, keep, send):
+        self.keep, self.other = keep, swap(send, ("heads", 1))
+        self.sends = (send,)
+        self.spread = lax.axis_size("items") == 4
+
+    def first(self):
+        if not self.spread:
+            return
         own = lax.axis_index("items")
-        top, low = value[:, : rows // 2], value[:, rows // 2 :]
-        across, along = own ^ 1, own ^ 2
-        beyond = own ^ 3
-        got_top = swap(
-            jnp.concatenate([columns(top, across, size), columns(top, beyond, size)], 1),
-            ("items", 1),
+        self.x, self.y = own % 2, own // 2
+        shape = (2, 2) + self.keep.shape[1:]
+        keep, other = self.keep.reshape(shape), self.other.reshape(shape)
+        half = shape[3] // 2
+        self.top = [part[:, :, :, :half] for part in (keep, other)]
+        self.low = [part[:, :, :, half:] for part in (keep, other)]
+        top = plus(*[pick(part, 1 - self.x, 1) for part in self.top])
+        low = plus(*[pick(part, 1 - self.y, 0) for part in self.low])
+        self.sends = (top, low)
+        self.got_top, self.got_low = swap(top, ("items", 1)), swap(low, ("items", 2))
+
+    def second(self):
+        if not self.spread:
+            return
+        top = [pick(part, self.x, 1) for part in self.top] + [self.got_top]
+        low = [pick(part, self.y, 0) for part in self.low] + [self.got_low]
+        send_top = plus(*[pick(part, 1 - self.y, 0) for part in top])
+        send_low = plus(*[pick(part, 1 - self.x, 0) for part in low])
+        self.top = [pick(part, self.y, 0) for part in top]
+        self.low = [pick(part, self.x, 0) for part in low]
+        self.sends = (send_top, send_low)
+        self.last_top, self.last_low = swap(send_top, ("items", 2)), swap(send_low, ("items", 1))
+
+    def third(self):
+        if self.spread:
+            value = jnp.concatenate(
+                [plus(*self.top, self.last_top), plus(*self.low, self.last_low)], 1
+            )
+        else:
+            value = plus(self.keep, self.other)[0]
+            value = lax.psum_scatter(value, "items", scatter_dimension=2, tiled=True)
+        heads = lax.axis_size("heads")
+        groups = [[core + 2 * z for z in range(heads // 2)] for core in range(2)]
+        self.sends = (value,)
+        self.result = lax.psum_scatter(
+            value, "heads", scatter_dimension=0, tiled=False, axis_index_groups=groups
         )
-        got_low = swap(
-            jnp.concatenate([columns(low, along, size), columns(low, beyond, size)], 1),
-            ("items", 2),
-        )
-        half = rows // 2
-        send_top = plus(columns(top, along, size), got_top[:, half:])
-        keep_top = plus(columns(top, own, size), got_top[:, :half])
-        send_low = plus(columns(low, across, size), got_low[:, half:])
-        keep_low = plus(columns(low, own, size), got_low[:, :half])
-        value = jnp.concatenate(
-            [
-                plus(keep_top, swap(send_top, ("items", 2))),
-                plus(keep_low, swap(send_low, ("items", 1))),
-            ],
-            1,
-        )
-    else:
-        value = lax.psum_scatter(value, "items", scatter_dimension=2, tiled=True)
-    heads = lax.axis_size("heads")
-    groups = [[core + 2 * z for z in range(heads // 2)] for core in range(2)]
-    value = lax.psum_scatter(
-        value, "heads", scatter_dimension=0, tiled=False, axis_index_groups=groups
-    )
-    return value
+
+
+def after(value, *scatters):
+    sends = [send for scatter in scatters for send in scatter.sends]
+    return lax.optimization_barrier((value, *sends))[0]
 
 
 def sum_everywhere(value):
@@ -773,7 +853,7 @@
 ):
     batches, here, model = frames.shape
     head_ways = lax.axis_size("heads")
-    items = lax.axis_size("items")
+    items = 4 if lax.axis_size("items") == 4 else 1
     group_len = here * head_ways
     size = model // HEADS
     reach = (KERNEL - 1) // 2
@@ -788,16 +868,14 @@
     depth_rows = w_depth.astype(F32)
     gain = [gains[i : i + 1] for i in range(6)]
     wide_position = first - reach + jnp.arange(here + 2 * reach, dtype=jnp.int32)
-    group_position = jnp.arange(group_len, dtype=jnp.int32)
     seg_wide = []
-    seg_group = []
+    seg_counts = []
     for number in range(batches):
         counts = bucket_counts[number, 0]
         seg_wide.append(segment_ids(wide_position, counts[0], counts[1], group_len))
-        seg_group.append(segment_ids(group_position, counts[0], counts[1], group_len))
+        seg_counts.append(counts)
     seg_wide = jnp.stack(seg_wide, 0)
     seg_own = seg_wide[:, reach : reach + here]
-    ranges = [block_ranges(seg) for seg in seg_group]
 
     stream = frames.reshape(rows, model)
     stream_one, pre_one = ffn_forward(stream, gain[0], w_ffn1_in, w_ffn1_out)
@@ -808,7 +886,7 @@
     contexts, fulls, lses = [], [], []
     for number in range(batches):
         out, full, lse = attend_forward(
-            qkv[number], seg_group[number][:, None], *ranges[number], size
+            qkv[number], seg_counts[number], size
         )
         contexts.append(
             lax.all_to_all(
@@ -844,13 +922,16 @@
     grad_four, gain_five = norm_back(
         cotangent.reshape(rows, model).astype(F32), final_normed, final_inverse, gain[5]
     )
-    grad_three, gain_four, *shares_two = ffn_backward(
-        grad_four, stream_three, pre_two, gain[4], w_ffn2_in, w_ffn2_out, head_ways, core, F32
-    )
-    f2_in = scatter(*shares_two[:2])
-    f2_out = scatter(*shares_two[2:])
+    two_out = Scatter(*ffn_out_grad(grad_four, pre_two, head_ways, core, items))
+    grad_four = after(grad_four, two_out)
+    grad_three, gain_four, *shares = ffn_backward(
+        grad_four, stream_three, pre_two, gain[4], w_ffn2_in, w_ffn2_out, head_ways, core, items, F32
+    )
+    two_in = Scatter(*shares)
+    two_out.first()
+    grad_three = after(grad_three, two_in, two_out)
     grad_mix = grad_three.astype(BF16)
-    point_out = scatter(*halves(matmul_left(mixed_low, grad_mix).astype(BF16), rows_each))
+    point_out = matmul_left(mixed_low, grad_mix).astype(BF16)
     grad_norm_in = dot(grad_mix, w_point_out, NT) * silu_slope(depth_shaped)
     grad_depth, gain_three = norm_back(grad_norm_in, depth_normed, depth_inverse, gain[3])
     grad_depth_low = grad_depth.astype(BF16).reshape(batches, here, model)
@@ -870,7 +951,8 @@
         grad_gated = grad_gated + depth_rows[offset] * jnp.where(
             same_back, grad_widened[:, mirror : mirror + here], 0.0
         )
-    grad_gated = grad_gated.reshape(rows, model)
+    two_in.first()
+    grad_gated = after(grad_gated.reshape(rows, model), two_in)
     grad_point = jnp.concatenate(
         [grad_gated * sigmoid_gate, grad_gated * linear * sigmoid_gate * (1.0 - sigmoid_gate)], 1
     ).astype(BF16)
@@ -880,27 +962,61 @@
     grad_two = grad_three + through
     grad_attn_out = grad_two.astype(BF16)
     grad_context = dot(grad_attn_out, w_out, NT).astype(BF16)
-    backs = []
+    point_in = matmul_left(conv_entered, grad_point).astype(BF16)
+    out_proj = matmul_left(context, grad_attn_out).astype(BF16)
+    middle = [halves(part, rows_each) for part in (point_out, point_in, out_proj)]
+    middle = [jnp.concatenate([part[i] for part in middle], 3) for i in range(2)]
+    if items == 1:
+        middle = [
+            part.transpose(1, 2, 0, 3).reshape(1, part.shape[1], part.shape[2], -1)
+            for part in middle
+        ]
+    middle = Scatter(*middle)
+    grad_heads = []
     for number in range(batches):
         part = grad_context[number * here : (number + 1) * here]
         part = part.reshape(here, head_ways, -1).transpose(1, 0, 2)
-        grad_heads = lax.all_to_all(part, "heads", split_axis=0, concat_axis=0, tiled=True)
+        grad_heads.append(
+            lax.all_to_all(part, "heads", split_axis=0, concat_axis=0, tiled=True)
+        )
+    backs = []
+    for number in range(batches):
+        if number == 0:
+            two_out.second()
+            grad_heads[number] = after(grad_heads[number], two_out, middle)
+        if number == 1:
+            two_out.third()
+            two_in.second()
+            middle.first()
+            grad_heads[number] = after(grad_heads[number], two_out, two_in, middle)
         grads = attend_backward(
-            qkv[number], seg_group[number][:, None], *ranges[number], size,
-            fulls[number], lses[number], grad_heads,
+            qkv[number], seg_counts[number], size, fulls[number], lses[number], grad_heads[number]
         )
         backs.append(lax.all_to_all(grads, "heads", split_axis=0, concat_axis=0, tiled=True))
-    point_in = scatter(*halves(matmul_left(conv_entered, grad_point).astype(BF16), rows_each))
-    out_proj = scatter(*halves(matmul_left(context, grad_attn_out).astype(BF16), rows_each))
-    grad_one, gain_one, *shares_qkv = qkv_backward(
-        backs, stream_one, gain[1], grad_two, w_qkv, cosines, sines, head_ways, core, size
-    )
-    qkv_grad = scatter(*shares_qkv)
-    grad_zero, gain_zero, *shares_one = ffn_backward(
-        grad_one, stream, pre_one, gain[0], w_ffn1_in, w_ffn1_out, head_ways, core, BF16
-    )
-    f1_in = scatter(*shares_one[:2])
-    f1_out = scatter(*shares_one[2:])
+    two_in.third()
+    middle.second()
+    backs[-1] = after(backs[-1], two_in, middle)
+    grad_one, gain_one, *shares = qkv_backward(
+        backs, stream_one, gain[1], grad_two, w_qkv, cosines, sines, head_ways, core, items, size
+    )
+    attn = Scatter(*shares)
+    middle.third()
+    grad_one = after(grad_one, attn, middle)
+    one_out = Scatter(*ffn_out_grad(grad_one, pre_one, head_ways, core, items))
+    attn.first()
+    grad_one = after(grad_one, one_out, attn)
+    grad_zero, gain_zero, *shares = ffn_backward(
+        grad_one, stream, pre_one, gain[0], w_ffn1_in, w_ffn1_out, head_ways, core, items, BF16
+    )
+    one_in = Scatter(*shares)
+    one_out.first()
+    attn.second()
+    one_in.first()
+    one_out.second()
+    attn.third()
+    one_in.second()
+    one_out.third()
+    one_in.third()
     small = sum_everywhere(
         jnp.concatenate(
             [gain_zero, gain_one, gain_two, gain_three, gain_four, gain_five]
@@ -916,19 +1032,25 @@
         parts = [share[:, i * span : (i + 1) * span] for i in range(wide // span)]
         return jnp.concatenate(parts, 0).T.astype(F32)
 
+    middle_parts = []
+    start = 0
+    for weight in (w_point_out, w_point_in, w_out):
+        each = weight.shape[1] // lax.axis_size("items")
+        middle_parts.append(middle.result[:, start : start + each].astype(F32))
+        start += each
     return (
         layer_out,
         grad_zero.reshape(frames.shape),
         small[:6],
-        f1_in.astype(F32),
-        unfolded(f1_out),
-        qkv_grad.astype(F32),
-        out_proj.astype(F32),
-        point_in.astype(F32),
+        one_in.result.astype(F32),
+        unfolded(one_out.result),
+        attn.result.astype(F32),
+        middle_parts[2],
+        middle_parts[1],
         small[6:],
-        point_out.astype(F32),
-        f2_in.astype(F32),
-        unfolded(f2_out),
+        middle_parts[0],
+        two_in.result.astype(F32),
+        unfolded(two_out.result),
     )
 
 

time: 757 us -> 820 us (1.083)
  local copies, waits for them, and re-layouts: 35.6 us -> 101 us
  blocking collectives: 0 us -> 44.3 us
  other arithmetic: 125 us -> 88.7 us
  Pallas kernels: 246 us -> 279 us
  starting transfers between devices: 93.8 us -> 72.7 us
  waiting for transfers between devices: 193 us -> 174 us
    all_to_all x0 -> x1, blocking collectives: none -> 44.3 us  [body(): lax.all_to_all(part, 'heads', split_axis=0, concat_axis=0, tiled=True)]
    slice x9 -> x13, local copies, waits for them, and re-layouts: 4.14 us -> 41.2 us  [the longest x8 25.6 us: first(): self.low = [part[:, :, :, half:] for part in (keep, other)]]
    ppermute x45 -> x35, waiting for transfers between devices: 128 us -> 159 us  [swap(): return lax.ppermute(value, EVERY, flipped(axis_bit, count))]
    all_to_all x4 -> x3, waiting for transfers between devices: 34.4 us -> 5.27 us  [body(): lax.all_to_all(part, 'heads', split_axis=0, concat_axis=0, tiled=True)]
    pallas_call x0 -> x2, Pallas kernels: none -> 28.4 us  [ffn_out_grad(): pl.pallas_call(ffn_out_kernel, grid_spec=grid_spec, out_shape=[share, sha...]
    reshape x0 -> x3, local copies, waits for them, and re-layouts: none -> 17.5 us  [halves(): value.reshape(places, 2, rows_each, items, -1).transpose(1, 3, 0, 2, 4)]
    all_to_all x2, waiting for transfers between devices: 16.2 us -> 0.01 us  [body(): lax.all_to_all(grads, 'heads', split_axis=0, concat_axis=0, tiled=True)]
    convert_element_type x46 -> x41, other arithmetic: 71.7 us -> 56.3 us  [the longest x36 47.6 us: plus(): return total.astype(BF16)]
  transfers between devices with their start and end apart: 65 -> 52, of which waited for: 29 -> 22; matrix products, arithmetic and copies ran while one was open for 19% -> 15% of each run, Pallas kernels for 23% -> 25%
where the time goes in v2:
time: 820 us; the launch traced here: 808 us
  Pallas kernels  279 us (34%)
  waiting for transfers between devices  174 us (21%)
  local copies, waits for them, and re-layouts  101 us (12%)
  other arithmetic  88.7 us (11%)
  starting transfers between devices  72.7 us (9%)
  blocking collectives  44.3 us (5%)
  matrix products  27.7 us (3%)
  between operations  21.1 us (3%)
    ppermute x35, waiting for transfers between devices, swap(): return lax.ppermute(value, EVERY, flipped(axis_bit, count))  159 us
    pallas_call x2, Pallas kernels, attend_backward(): pl.pallas_call(functools.partial(attn_bwd_kernel, heads, size, group), gr...  79 us
    pallas_call x2, Pallas kernels, attend_forward(): pl.pallas_call(functools.partial(attn_fwd_kernel, heads, size, group), gr...  60 us
    pallas_call x2, Pallas kernels, ffn_backward(): pl.pallas_call(ffn_bwd_kernel, grid_spec=grid_spec, out_shape=[jax.ShapeD...  48.7 us
    convert_element_type x36, other arithmetic, plus(): return total.astype(BF16)  47.6 us
    all_to_all x1, blocking collectives, body(): lax.all_to_all(part, 'heads', split_axis=0, concat_axis=0, tiled=True)  44.3 us
    pallas_call x2, Pallas kernels, ffn_forward(): pl.pallas_call(ffn_fwd_kernel, grid=(hidden // wide,), in_specs=[whole((r...  34.5 us
    ppermute x35, starting transfers between devices, swap(): return lax.ppermute(value, EVERY, flipped(axis_bit, count))  32.7 us
  transfers between devices with their start and end apart: 52, of which 22 were waited for; matrix products, arithmetic and copies ran while one was open for 15% of the time, Pallas kernels for 25%

profile of v2, /device:TPU:0, one launch (start us, length us, event | category | flops | bytes accessed | tf_op | source)
XLA Modules:
  0.0 808.1 jit_solution(7965254030320223463)
XLA Ops:
  10.8 17.1 %ffn_forward.2 = (f32[512,1024]{1,0:T(8,128)}, f32[512,4096]{1,0:T(8,128)}) custom-call(bf16[512,1024]{1,0:T(8,128)(2,1)} %bitcast.421, f32[1,1024]{1,0:T(1,128)} %get-tuple-element.168.gain_ref, bf16[1024,4096]{1,0:T(8,128)(2,1)} %win_ref.7, bf16[4096,1024]{1,0:T(8,128)(2,1)} %wout_ref.7), custom_call_target="tpu_custom_call" | custom-call | flops 8589934592 | bytes 25165824 | tf_op jit(solution)/shard_map/ffn_forward/pallas_call | solution.py:400
  27.9 8.9 %qkv_forward.1 = (bf16[8,3,256,128]{3,2,1,0:T(8,128)(2,1)}, bf16[8,3,256,128]{3,2,1,0:T(8,128)(2,1)}) custom-call(f32[512,1024]{1,0:T(8,128)} %get-tuple-element.48.x_ref.refs_2_, f32[1,1024]{1,0:T(1,128)} %get-tuple-element.167.gain_ref.refs_3_, bf16[1024,3072]{1,0:T(8,128)(2,1)} %refs_5_.1, bf16[1024,3072]{1,0:T(8,128)(2,1)} %refs_5_.1, ...), custom_call_target="tpu_custom_call" | custom-call | flops 3221225472 | bytes 11534336 | tf_op jit(solution)/shard_map/qkv_forward/pallas_call | solution.py:631
  36.8 44.3 %all_to_all.40.qkv_ref = bf16[8,3,256,128]{3,2,1,0:T(8,128)(2,1)} all-to-all(bf16[8,3,256,128]{3,2,1,0:T(8,128)(2,1)} %get-tuple-element.49), channel_id=1, replica_groups=mesh['items'=4,'heads'=8] {'heads'}, dimensions={0} | all-to-all | bytes 3145728 | tf_op jit(solution)/shard_map/all_to_all | solution.py:884
  81.1 4.4 all-to-all-start.2
  86.0 30.0 %attend_forward.2 = (bf16[2048,128]{1,0:T(8,128)(2,1)}, f32[2048,128]{1,0:T(8,128)}, f32[2,2048,128]{2,1,0:T(8,128)}) custom-call(s32[2]{0:T(128)} %get-tuple-element.187.counts_ref, bf16[8,3,256,128]{3,2,1,0:T(8,128)(2,1)} %all_to_all.40.qkv_ref), custom_call_target="tpu_custom_call" | custom-call | flops 8589934592 | bytes 6291456 | tf_op jit(solution)/shard_map/attend_forward/pallas_call | solution.py:219
  118.1 5.3 all-to-all-done.2.qkv_ref
  123.3 4.1 all-to-all-start.1
  127.5 30.0 %attend_forward.3 = (bf16[2048,128]{1,0:T(8,128)(2,1)}, f32[2048,128]{1,0:T(8,128)}, f32[2,2048,128]{2,1,0:T(8,128)}) custom-call(s32[2]{0:T(128)} %get-tuple-element.188.counts_ref, bf16[8,3,256,128]{3,2,1,0:T(8,128)(2,1)} %all-to-all-done.2.qkv_ref), custom_call_target="tpu_custom_call" | custom-call | flops 8589934592 | bytes 6291456 | tf_op jit(solution)/shard_map/attend_forward/pallas_call | solution.py:219
  159.6 5.0 all-to-all-start.3
  172.2 7.9 all-to-all-done.3
  180.0 4.0 fusion.127
  201.9 17.4 %ffn_forward.3 = (f32[512,1024]{1,0:T(8,128)}, f32[512,4096]{1,0:T(8,128)}) custom-call(f32[512,1024]{1,0:T(8,128)} %convolution_add_fusion.x_ref, f32[1,1024]{1,0:T(1,128)} %get-tuple-element.169.gain_ref, bf16[1024,4096]{1,0:T(8,128)(2,1)} %win_ref.6, bf16[4096,1024]{1,0:T(8,128)(2,1)} %wout_ref.6), custom_call_target="tpu_custom_call" | custom-call | flops 8589934592 | bytes 25165824 | tf_op jit(solution)/shard_map/ffn_forward/pallas_call | solution.py:400
  227.1 14.2 %ffn_out_grad.2 = (bf16[4,4,128,1024]{3,2,1,0:T(8,128)(2,1)}, bf16[4,4,128,1024]{3,2,1,0:T(8,128)(2,1)}) custom-call(s32[1]{0:T(128)} %bitcast.26.core_ref, f32[512,1024]{1,0:T(8,128)} %get-tuple-element.58.up_ref, f32[512,4096]{1,0:T(8,128)} %get-tuple-element.56.pre_ref), custom_call_target="tpu_custom_call" | custom-call | flops 4294967296 | bytes 16777216 | tf_op jit(solution)/shard_map/ffn_out_grad/pallas_call | solution.py:486
  243.2 24.7 %ffn_backward.2 = (f32[512,1024]{1,0:T(8,128)}, f32[1,1024]{1,0:T(1,128)}, bf16[4,4,128,1024]{3,2,1,0:T(8,128)(2,1)}, bf16[4,4,128,1024]{3,2,1,0:T(8,128)(2,1)}) custom-call(s32[1]{0:T(128)} %bitcast.26.core_ref, f32[512,1024]{1,0:T(8,128)} %convolution_add_fusion.x_ref, f32[1,1024]{1,0:T(1,128)} %get-tuple-element.169.gain_ref, ...), custom_call_target="tpu_custom_call" | custom-call | flops 12884901888 | bytes 37748736 | tf_op jit(solution)/shard_map/ffn_backward/pallas_call | solution.py:559
  277.0 6.4 fusion.114
  297.9 4.7 reshape.662
  314.1 4.6 convolution_convert_fusion
  318.7 4.0 multiply_reduce_fusion.2
  322.7 8.2 %reshape.663 = bf16[4,2,128,4,512]{4,3,2,1,0:T(4,128)(2,1)} reshape(bf16[1024,2048]{1,0:T(8,128)(2,1)} %convolution_convert_fusion) | data formatting | bytes 8388608 | tf_op jit(solution)/shard_map/reshape | solution.py:767
  330.9 5.8 dynamic-slice_bitcast_fusion
  338.8 3.8 convolution_convert_fusion.1
  342.6 4.5 reshape.664
  367.3 14.2 %collective-permute-done.6 = bf16[2,4,64,1024]{3,2,1,0:T(8,128)(2,1)S(1)} collective-permute-done((bf16[2,4,64,1024]{3,2,1,0:T(8,128)(2,1)}, bf16[2,4,64,1024]{3,2,1,0:T(8,128)(2,1)S(1)}, u32[]{:S(2)}, u32[]{:S(2)}) %collective-permute-start.6) | collective-permute-done | bytes 1048608 | tf_op jit(solution)/shard_map/ppermute | solution.py:754
  388.1 4.3 all-to-all-start.6
  393.7 10.4 %collective-permute-done.10 = bf16[2,4,64,1024]{3,2,1,0:T(8,128)(2,1)} collective-permute-done((bf16[2,4,64,1024]{3,2,1,0:T(8,128)(2,1)}, bf16[2,4,64,1024]{3,2,1,0:T(8,128)(2,1)}, u32[]{:S(2)}, u32[]{:S(2)}) %collective-permute-start.10) | collective-permute-done | bytes 1048608 | tf_op jit(solution)/shard_map/ppermute | solution.py:754
  409.0 5.2 collective-permute-done.8
  425.1 3.6 all-to-all-start.4
  428.6 39.4 %attend_backward.3 = bf16[8,3,256,128]{3,2,1,0:T(8,128)(2,1)} custom-call(s32[2]{0:T(128)} %get-tuple-element.188.counts_ref, bf16[8,3,256,128]{3,2,1,0:T(8,128)(2,1)} %all-to-all-done.2.qkv_ref, f32[2048,128]{1,0:T(8,128)} %get-tuple-element.66.full_ref, f32[2,2048,128]{2,1,0:T(8,128)} %get-tuple-element.67.lse_ref, ...), custom_call_target="tpu_custom_call" | custom-call | flops 17179869184 | bytes 9437184 | tf_op jit(solution)/shard_map/attend_backward/pallas_call | solution.py:350
  468.1 5.1 all-to-all-start.7
  473.2 39.6 %attend_backward.2 = bf16[8,3,256,128]{3,2,1,0:T(8,128)(2,1)} custom-call(s32[2]{0:T(128)} %get-tuple-element.187.counts_ref, bf16[8,3,256,128]{3,2,1,0:T(8,128)(2,1)} %all_to_all.40.qkv_ref, f32[2048,128]{1,0:T(8,128)} %get-tuple-element.54.full_ref, f32[2,2048,128]{2,1,0:T(8,128)} %get-tuple-element.55.lse_ref, bf16[8,256,128]{2,1,0:T(8,128)(2,1)} %copy-done.60), custom_call_target="tpu_custom_call" | custom-call | flops 17179869184 | bytes 9437184 | tf_op jit(solution)/shard_map/attend_backward/pallas_call | solution.py:350
  512.8 5.2 all-to-all-start.5
  522.2 10.7 %collective-permute-done.13 = bf16[4,64,1024]{2,1,0:T(8,128)(2,1)S(1)} collective-permute-done((bf16[4,64,1024]{2,1,0:T(8,128)(2,1)S(1)}, bf16[4,64,1024]{2,1,0:T(8,128)(2,1)S(1)}, u32[]{:S(2)}, u32[]{:S(2)}) %collective-permute-start.13) | collective-permute-done | bytes 524320 | tf_op jit(solution)/shard_map/ppermute | solution.py:754
  534.5 21.8 %collective-permute-done.14 = bf16[4,64,1024]{2,1,0:T(8,128)(2,1)S(1)} collective-permute-done((bf16[4,64,1024]{2,1,0:T(8,128)(2,1)S(1)}, bf16[4,64,1024]{2,1,0:T(8,128)(2,1)S(1)}, u32[]{:S(2)}, u32[]{:S(2)}) %collective-permute-start.14) | collective-permute-done | bytes 524320 | tf_op jit(solution)/shard_map/ppermute | solution.py:754
  562.4 19.2 %qkv_backward.1 = (f32[512,1024]{1,0:T(8,128)}, f32[1,1024]{1,0:T(1,128)}, bf16[4,4,128,768]{3,2,1,0:T(8,128)(2,1)}, bf16[4,4,128,768]{3,2,1,0:T(8,128)(2,1)}) custom-call(s32[1]{0:T(128)} %bitcast.26.core_ref, bf16[8,3,256,128]{3,2,1,0:T(8,128)(2,1)} %all-to-all-done.5.refs_0_, bf16[8,3,256,128]{3,2,1,0:T(8,128)(2,1)} %all-to-all-done.7.refs_1_, ...), custom_call_target="tpu_custom_call" | custom-call | flops 6442450944 | bytes 23068672 | tf_op jit(solution)/shard_map/qkv_backward/pallas_call | solution.py:729
  582.7 13.3 %collective-permute-done.17 = bf16[4,64,1024]{2,1,0:T(8,128)(2,1)S(1)} collective-permute-done((bf16[4,64,1024]{2,1,0:T(8,128)(2,1)S(1)}, bf16[4,64,1024]{2,1,0:T(8,128)(2,1)S(1)}, u32[]{:S(2)}, u32[]{:S(2)}) %collective-permute-start.17) | collective-permute-done | bytes 524320 | tf_op jit(solution)/shard_map/ppermute | solution.py:754
  600.5 14.2 %ffn_out_grad.3 = (bf16[4,4,128,1024]{3,2,1,0:T(8,128)(2,1)}, bf16[4,4,128,1024]{3,2,1,0:T(8,128)(2,1)}) custom-call(s32[1]{0:T(128)} %bitcast.26.core_ref, f32[512,1024]{1,0:T(8,128)} %get-tuple-element.76.up_ref, f32[512,4096]{1,0:T(8,128)} %get-tuple-element.73.pre_ref), custom_call_target="tpu_custom_call" | custom-call | flops 4294967296 | bytes 16777216 | tf_op jit(solution)/shard_map/ffn_out_grad/pallas_call | solution.py:486
  622.0 24.0 %ffn_backward.3 = (bf16[512,1024]{1,0:T(8,128)(2,1)}, f32[1,1024]{1,0:T(1,128)}, bf16[4,4,128,1024]{3,2,1,0:T(8,128)(2,1)}, bf16[4,4,128,1024]{3,2,1,0:T(8,128)(2,1)}) custom-call(s32[1]{0:T(128)} %bitcast.26.core_ref, bf16[512,1024]{1,0:T(8,128)(2,1)} %bitcast.422, f32[1,1024]{1,0:T(1,128)} %get-tuple-element.168.gain_ref, ...), custom_call_target="tpu_custom_call" | custom-call | flops 12884901888 | bytes 37748736 | tf_op jit(solution)/shard_map/ffn_backward/pallas_call | solution.py:559
  650.3 3.8 fusion.108
  656.4 10.8 %collective-permute-done.35 = bf16[2,4,64,768]{3,2,1,0:T(8,128)(2,1)S(1)} collective-permute-done((bf16[2,4,64,768]{3,2,1,0:T(8,128)(2,1)S(1)}, bf16[2,4,64,768]{3,2,1,0:T(8,128)(2,1)S(1)}, u32[]{:S(2)}, u32[]{:S(2)}) %collective-permute-start.35) | collective-permute-done | bytes 786464 | tf_op jit(solution)/shard_map/ppermute | solution.py:754
  672.2 7.2 collective-permute-done.36
  679.6 17.5 %collective-permute-done.38 = bf16[4,64,768]{2,1,0:T(8,128)(2,1)S(1)} collective-permute-done((bf16[4,64,768]{2,1,0:T(8,128)(2,1)S(1)}, bf16[4,64,768]{2,1,0:T(8,128)(2,1)S(1)}, u32[]{:S(2)}, u32[]{:S(2)}) %collective-permute-start.38) | collective-permute-done | bytes 393248 | tf_op jit(solution)/shard_map/ppermute | solution.py:754
  704.2 4.3 fusion.109
  708.5 3.4 collective-permute-done.32
  716.3 4.2 fusion.110
  727.2 17.6 %collective-permute-done.26 = bf16[2,4,64,1024]{3,2,1,0:T(8,128)(2,1)} collective-permute-done((bf16[2,4,64,1024]{3,2,1,0:T(8,128)(2,1)S(1)}, bf16[2,4,64,1024]{3,2,1,0:T(8,128)(2,1)}, u32[]{:S(2)}, u32[]{:S(2)}) %collective-permute-start.26) | collective-permute-done | bytes 1048608 | tf_op jit(solution)/shard_map/ppermute | solution.py:754
  753.0 7.5 collective-permute-done.27
  780.2 4.5 collective-permute-done.23
  787.5 6.5 collective-permute-done.24
  (377 shorter events, 210.4 us)
Async XLA Ops:
  81.1 42.3 %all-to-all-start.2 = ((bf16[8,3,256,128]{3,2,1,0:T(8,128)(2,1)}), bf16[8,3,256,128]{3,2,1,0:T(8,128)(2,1)}, u32[]{:S(2)}, u32[]{:S(2)}) async-start(bf16[8,3,256,128]{3,2,1,0:T(8,128)(2,1)} %get-tuple-element.51), calls=%async_computation.2 | async-start | bytes 3145728 | tf_op jit(solution)/shard_map/all_to_all | solution.py:884
  123.3 36.3 %all-to-all-start.1 = ((bf16[8,256,128]{1,2,0:T(8,128)(2,1)}), bf16[8,256,128]{1,2,0:T(8,128)(2,1)}, u32[]{:S(2)}, u32[]{:S(2)}) async-start(bf16[8,256,128]{1,2,0:T(8,128)(2,1)} %copy.91), calls=%async_computation.1 | async-start | bytes 1048576 | tf_op jit(solution)/shard_map/all_to_all | solution.py:892
  159.6 20.4 %all-to-all-start.3 = ((bf16[8,256,128]{1,2,0:T(8,128)(2,1)}), bf16[8,256,128]{1,2,0:T(8,128)(2,1)}, u32[]{:S(2)}, u32[]{:S(2)}) async-start(bf16[8,256,128]{1,2,0:T(8,128)(2,1)} %copy.92), calls=%async_computation.3 | async-start | bytes 1048576 | tf_op jit(solution)/shard_map/all_to_all | solution.py:892
  241.3 32.9 %collective-permute-start.2 = (bf16[4,4,128,1024]{3,2,1,0:T(8,128)(2,1)}, bf16[4,4,128,1024]{3,2,1,0:T(8,128)(2,1)}, u32[]{:S(2)}, u32[]{:S(2)}) collective-permute-start(bf16[4,4,128,1024]{3,2,1,0:T(8,128)(2,1)} %get-tuple-element.57), channel_id=1, source_target_pairs={{0,1},{1,0},{2,3},{3,2},{4,5},{5,4},{6,7},{7,6},{8,9},{9,8},{10,11... | collective-permute-start | bytes 12582920 | tf_op jit(solution)/shard_map/ppermute | solution.py:754
  267.9 9.0 %collective-permute-start.5 = (bf16[4,4,128,1024]{3,2,1,0:T(8,128)(2,1)}, bf16[4,4,128,1024]{3,2,1,0:T(8,128)(2,1)}, u32[]{:S(2)}, u32[]{:S(2)}) collective-permute-start(bf16[4,4,128,1024]{3,2,1,0:T(8,128)(2,1)} %get-tuple-element.60), channel_id=1, source_target_pairs={{0,1},{1,0},{2,3},{3,2},{4,5},{5,4},{6,7},{7,6},{8,9},{9,8},{10,11... | collective-permute-start | bytes 12582920 | tf_op jit(solution)/shard_map/ppermute | solution.py:754
  293.6 17.0 %collective-permute-start.3 = (bf16[2,2,1024]{2,1,0:T(2,128)(2,1)S(1)}, bf16[2,2,1024]{2,1,0:T(2,128)(2,1)S(1)}, u32[]{:S(2)}, u32[]{:S(2)}) collective-permute-start(bf16[2,2,1024]{2,1,0:T(2,128)(2,1)S(1)} %get-tuple-element.154), channel_id=1, source_target_pairs={{1,0},{2,1},{3,2},{4,3},{5,4},{6,5},{7,6},{9,8},{10,9},{11,10},{12... | collective-permute-start | bytes 24584 | tf_op jit(solution)/shard_map/ppermute | solution.py:846
  294.9 15.7 %collective-permute-start.4 = (bf16[2,2,1024]{2,1,0:T(2,128)(2,1)S(1)}, bf16[2,2,1024]{2,1,0:T(2,128)(2,1)S(1)}, u32[]{:S(2)}, u32[]{:S(2)}) collective-permute-start(bf16[2,2,1024]{2,1,0:T(2,128)(2,1)S(1)} %get-tuple-element.155), channel_id=1, source_target_pairs={{0,1},{1,2},{2,3},{3,4},{4,5},{5,6},{6,7},{8,9},{9,10},{10,11},{11... | collective-permute-start | bytes 24584 | tf_op jit(solution)/shard_map/ppermute | solution.py:845
  353.6 65.0 %collective-permute-start.12 = (bf16[4,4,128,1024]{3,2,1,0:T(8,128)(2,1)}, bf16[4,4,128,1024]{3,2,1,0:T(8,128)(2,1)}, u32[]{:S(2)}, u32[]{:S(2)}) collective-permute-start(bf16[4,4,128,1024]{3,2,1,0:T(8,128)(2,1)} %pad_maximum_fusion), channel_id=1, source_target_pairs={{0,1},{1,0},{2,3},{3,2},{4,5},{5,4},{6,7},{7,6},{8,9},{9,8},{10,11... | collective-permute-start | bytes 12582920 | tf_op jit(solution)/shard_map/ppermute | solution.py:754
  355.3 26.2 %collective-permute-start.6 = (bf16[2,4,64,1024]{3,2,1,0:T(8,128)(2,1)}, bf16[2,4,64,1024]{3,2,1,0:T(8,128)(2,1)S(1)}, u32[]{:S(2)}, u32[]{:S(2)}) collective-permute-start(bf16[2,4,64,1024]{3,2,1,0:T(8,128)(2,1)} %fusion.39), channel_id=1, source_target_pairs={{0,8},{1,9},{2,10},{3,11},{4,12},{5,13},{6,14},{7,15},{8,0},{9,1},... | collective-permute-start | bytes 3145736 | tf_op jit(solution)/shard_map/ppermute | solution.py:754
  355.3 28.9 %collective-permute-start.7 = (bf16[2,4,64,1024]{3,2,1,0:T(8,128)(2,1)}, bf16[2,4,64,1024]{3,2,1,0:T(8,128)(2,1)S(1)}, u32[]{:S(2)}, u32[]{:S(2)}) collective-permute-start(bf16[2,4,64,1024]{3,2,1,0:T(8,128)(2,1)} %fusion.30), channel_id=1, source_target_pairs={{0,16},{1,17},{2,18},{3,19},{4,20},{5,21},{6,22},{7,23},{8,24},{9,... | collective-permute-start | bytes 3145736 | tf_op jit(solution)/shard_map/ppermute | solution.py:754
  355.3 48.8 %collective-permute-start.10 = (bf16[2,4,64,1024]{3,2,1,0:T(8,128)(2,1)}, bf16[2,4,64,1024]{3,2,1,0:T(8,128)(2,1)}, u32[]{:S(2)}, u32[]{:S(2)}) collective-permute-start(bf16[2,4,64,1024]{3,2,1,0:T(8,128)(2,1)} %fusion.31), channel_id=1, source_target_pairs={{0,8},{1,9},{2,10},{3,11},{4,12},{5,13},{6,14},{7,15},{8,0},{9,1},... | collective-permute-start | bytes 3145736 | tf_op jit(solution)/shard_map/ppermute | solution.py:754
  357.3 49.2 %collective-permute-start.11 = (bf16[2,4,64,1024]{3,2,1,0:T(8,128)(2,1)}, bf16[2,4,64,1024]{3,2,1,0:T(8,128)(2,1)}, u32[]{:S(2)}, u32[]{:S(2)}) collective-permute-start(bf16[2,4,64,1024]{3,2,1,0:T(8,128)(2,1)} %fusion.32), channel_id=1, source_target_pairs={{0,16},{1,17},{2,18},{3,19},{4,20},{5,21},{6,22},{7,23},{8,24},{9,... | collective-permute-start | bytes 3145736 | tf_op jit(solution)/shard_map/ppermute | solution.py:754
  384.2 30.1 %collective-permute-start.8 = (bf16[4,64,1024]{2,1,0:T(8,128)(2,1)}, bf16[4,64,1024]{2,1,0:T(8,128)(2,1)S(1)}, u32[]{:S(2)}, u32[]{:S(2)}) collective-permute-start(bf16[4,64,1024]{2,1,0:T(8,128)(2,1)} %fusion.74), channel_id=1, source_target_pairs={{0,16},{1,17},{2,18},{3,19},{4,20},{5,21},{6,22},{7,23},{8,24},{9,... | collective-permute-start | bytes 1572872 | tf_op jit(solution)/shard_map/ppermute | solution.py:754
  386.8 29.0 %collective-permute-start.9 = (bf16[4,64,1024]{2,1,0:T(8,128)(2,1)}, bf16[4,64,1024]{2,1,0:T(8,128)(2,1)}, u32[]{:S(2)}, u32[]{:S(2)}) collective-permute-start(bf16[4,64,1024]{2,1,0:T(8,128)(2,1)} %fusion.73), channel_id=1, source_target_pairs={{0,8},{1,9},{2,10},{3,11},{4,12},{5,13},{6,14},{7,15},{8,0},{9,1},... | collective-permute-start | bytes 1572872 | tf_op jit(solution)/shard_map/ppermute | solution.py:754
  388.1 37.0 %all-to-all-start.6 = ((bf16[8,256,128]{2,1,0:T(8,128)(2,1)}), bf16[8,256,128]{2,1,0:T(8,128)(2,1)}, u32[]{:S(2)}, u32[]{:S(2)}) async-start(bf16[8,256,128]{2,1,0:T(8,128)(2,1)} %bitcast.52), calls=%async_computation.6 | async-start | bytes 1048576 | tf_op jit(solution)/shard_map/all_to_all | solution.py:980
  425.1 43.0 %all-to-all-start.4 = ((bf16[8,256,128]{2,1,0:T(8,128)(2,1)}), bf16[8,256,128]{2,1,0:T(8,128)(2,1)S(1)}, u32[]{:S(2)}, u32[]{:S(2)}) async-start(bf16[8,256,128]{2,1,0:T(8,128)(2,1)} %bitcast.40), calls=%async_computation.4 | async-start | bytes 1048576 | tf_op jit(solution)/shard_map/all_to_all | solution.py:980
  468.1 44.7 %all-to-all-start.7 = ((bf16[8,3,256,128]{3,2,1,0:T(8,128)(2,1)}), bf16[8,3,256,128]{3,2,1,0:T(8,128)(2,1)}, u32[]{:S(2)}, u32[]{:S(2)}) async-start(bf16[8,3,256,128]{3,2,1,0:T(8,128)(2,1)} %attend_backward.3), calls=%async_computation.7 | async-start | bytes 3145728 | tf_op jit(solution)/shard_map/all_to_all | solution.py:995
  512.8 49.7 %all-to-all-start.5 = ((bf16[8,3,256,128]{3,2,1,0:T(8,128)(2,1)}), bf16[8,3,256,128]{3,2,1,0:T(8,128)(2,1)}, u32[]{:S(2)}, u32[]{:S(2)}) async-start(bf16[8,3,256,128]{3,2,1,0:T(8,128)(2,1)} %attend_backward.2), calls=%async_computation.5 | async-start | bytes 3145728 | tf_op jit(solution)/shard_map/all_to_all | solution.py:995
  518.0 249.7 %reduce-scatter.15.cloned.1.call-start = ((), (), s32[]{:S(2)}) async-start(), calls=%async_computation.18 | async-start | bytes 1310720 | tf_op jit(solution)/shard_map/reduce_scatter | solution.py:822
  518.0 14.8 %collective-permute-start.13 = (bf16[4,64,1024]{2,1,0:T(8,128)(2,1)S(1)}, bf16[4,64,1024]{2,1,0:T(8,128)(2,1)S(1)}, u32[]{:S(2)}, u32[]{:S(2)}) collective-permute-start(bf16[4,64,1024]{2,1,0:T(8,128)(2,1)S(1)} %copy-done.62), channel_id=1, source_target_pairs={{0,16},{1,17},{2,18},{3,19},{4,20},{5,21},{6,22},{7,23},{8,24},{9,... | collective-permute-start | bytes 1572872 | tf_op jit(solution)/shard_map/ppermute | solution.py:754
  518.1 41.0 %collective-permute-start.16 = (bf16[2,4,64,1024]{3,2,1,0:T(8,128)(2,1)}, bf16[2,4,64,1024]{3,2,1,0:T(8,128)(2,1)}, u32[]{:S(2)}, u32[]{:S(2)}) collective-permute-start(bf16[2,4,64,1024]{3,2,1,0:T(8,128)(2,1)} %fusion.34), channel_id=1, source_target_pairs={{0,16},{1,17},{2,18},{3,19},{4,20},{5,21},{6,22},{7,23},{8,24},{9,... | collective-permute-start | bytes 3145736 | tf_op jit(solution)/shard_map/ppermute | solution.py:754
  520.1 40.6 %collective-permute-start.15 = (bf16[2,4,64,1024]{3,2,1,0:T(8,128)(2,1)S(1)}, bf16[2,4,64,1024]{3,2,1,0:T(8,128)(2,1)}, u32[]{:S(2)}, u32[]{:S(2)}) collective-permute-start(bf16[2,4,64,1024]{3,2,1,0:T(8,128)(2,1)S(1)} %fusion.33), channel_id=1, source_target_pairs={{0,8},{1,9},{2,10},{3,11},{4,12},{5,13},{6,14},{7,15},{8,0},{9,1},... | collective-permute-start | bytes 3145736 | tf_op jit(solution)/shard_map/ppermute | solution.py:754
  520.1 36.2 %collective-permute-start.14 = (bf16[4,64,1024]{2,1,0:T(8,128)(2,1)S(1)}, bf16[4,64,1024]{2,1,0:T(8,128)(2,1)S(1)}, u32[]{:S(2)}, u32[]{:S(2)}) collective-permute-start(bf16[4,64,1024]{2,1,0:T(8,128)(2,1)S(1)} %copy-done.61), channel_id=1, source_target_pairs={{0,8},{1,9},{2,10},{3,11},{4,12},{5,13},{6,14},{7,15},{8,0},{9,1},... | collective-permute-start | bytes 1572872 | tf_op jit(solution)/shard_map/ppermute | solution.py:754
  581.7 35.3 %collective-permute-start.19 = (bf16[4,4,128,768]{3,2,1,0:T(8,128)(2,1)}, bf16[4,4,128,768]{3,2,1,0:T(8,128)(2,1)}, u32[]{:S(2)}, u32[]{:S(2)}) collective-permute-start(bf16[4,4,128,768]{3,2,1,0:T(8,128)(2,1)} %get-tuple-element.71), channel_id=1, source_target_pairs={{0,1},{1,0},{2,3},{3,2},{4,5},{5,4},{6,7},{7,6},{8,9},{9,8},{10,11... | collective-permute-start | bytes 9437192 | tf_op jit(solution)/shard_map/ppermute | solution.py:754
  581.7 14.3 %collective-permute-start.17 = (bf16[4,64,1024]{2,1,0:T(8,128)(2,1)S(1)}, bf16[4,64,1024]{2,1,0:T(8,128)(2,1)S(1)}, u32[]{:S(2)}, u32[]{:S(2)}) collective-permute-start(bf16[4,64,1024]{2,1,0:T(8,128)(2,1)S(1)} %fusion.60), channel_id=1, source_target_pairs={{0,16},{1,17},{2,18},{3,19},{4,20},{5,21},{6,22},{7,23},{8,24},{9,... | collective-permute-start | bytes 1572872 | tf_op jit(solution)/shard_map/ppermute | solution.py:754
  582.1 189.9 %reduce-scatter.17.cloned.1.call-start = ((), (), s32[]{:S(2)}) async-start(), calls=%async_computation.19 | async-start | bytes 1310720 | tf_op jit(solution)/shard_map/reduce_scatter | solution.py:822
  582.4 15.4 %collective-permute-start.18 = (bf16[4,64,1024]{2,1,0:T(8,128)(2,1)S(1)}, bf16[4,64,1024]{2,1,0:T(8,128)(2,1)S(1)}, u32[]{:S(2)}, u32[]{:S(2)}) collective-permute-start(bf16[4,64,1024]{2,1,0:T(8,128)(2,1)S(1)} %fusion.59), channel_id=1, source_target_pairs={{0,8},{1,9},{2,10},{3,11},{4,12},{5,13},{6,14},{7,15},{8,0},{9,1},... | collective-permute-start | bytes 1572872 | tf_op jit(solution)/shard_map/ppermute | solution.py:754
  614.7 35.5 %collective-permute-start.30 = (bf16[4,4,128,1024]{3,2,1,0:T(8,128)(2,1)}, bf16[4,4,128,1024]{3,2,1,0:T(8,128)(2,1)}, u32[]{:S(2)}, u32[]{:S(2)}) collective-permute-start(bf16[4,4,128,1024]{3,2,1,0:T(8,128)(2,1)} %get-tuple-element.74), channel_id=1, source_target_pairs={{0,1},{1,0},{2,3},{3,2},{4,5},{5,4},{6,7},{7,6},{8,9},{9,8},{10,11... | collective-permute-start | bytes 12582920 | tf_op jit(solution)/shard_map/ppermute | solution.py:754
  614.7 163.9 %reduce-scatter.13.cloned.1.call-start = ((), (), s32[]{:S(2)}) async-start(), calls=%async_computation.17 | async-start | bytes 1310720 | tf_op jit(solution)/shard_map/reduce_scatter | solution.py:822
  646.1 70.3 %collective-permute-start.25 = (bf16[4,4,128,1024]{3,2,1,0:T(8,128)(2,1)}, bf16[4,4,128,1024]{3,2,1,0:T(8,128)(2,1)}, u32[]{:S(2)}, u32[]{:S(2)}) collective-permute-start(bf16[4,4,128,1024]{3,2,1,0:T(8,128)(2,1)} %get-tuple-element.82), channel_id=1, source_target_pairs={{0,1},{1,0},{2,3},{3,2},{4,5},{5,4},{6,7},{7,6},{8,9},{9,8},{10,11... | collective-permute-start | bytes 12582920 | tf_op jit(solution)/shard_map/ppermute | solution.py:754
  646.6 148.6 %reduce-scatter.11.cloned.1.call-start = ((), (), s32[]{:S(2)}) async-start(), calls=%async_computation.16 | async-start | bytes 983040 | tf_op jit(solution)/shard_map/reduce_scatter | solution.py:822
  646.7 20.5 %collective-permute-start.35 = (bf16[2,4,64,768]{3,2,1,0:T(8,128)(2,1)S(1)}, bf16[2,4,64,768]{3,2,1,0:T(8,128)(2,1)S(1)}, u32[]{:S(2)}, u32[]{:S(2)}) collective-permute-start(bf16[2,4,64,768]{3,2,1,0:T(8,128)(2,1)S(1)} %fusion.75), channel_id=1, source_target_pairs={{0,8},{1,9},{2,10},{3,11},{4,12},{5,13},{6,14},{7,15},{8,0},{9,1},... | collective-permute-start | bytes 2359304 | tf_op jit(solution)/shard_map/ppermute | solution.py:754
  649.8 20.1 %collective-permute-start.37 = (bf16[2,4,64,768]{3,2,1,0:T(8,128)(2,1)S(1)}, bf16[2,4,64,768]{3,2,1,0:T(8,128)(2,1)S(1)}, u32[]{:S(2)}, u32[]{:S(2)}) collective-permute-start(bf16[2,4,64,768]{3,2,1,0:T(8,128)(2,1)S(1)} %fusion.76), channel_id=1, source_target_pairs={{0,16},{1,17},{2,18},{3,19},{4,20},{5,21},{6,22},{7,23},{8,24},{9,... | collective-permute-start | bytes 2359304 | tf_op jit(solution)/shard_map/ppermute | solution.py:754
  654.6 42.7 %collective-permute-start.31 = (bf16[2,4,64,1024]{3,2,1,0:T(8,128)(2,1)S(1)}, bf16[2,4,64,1024]{3,2,1,0:T(8,128)(2,1)S(1)}, u32[]{:S(2)}, u32[]{:S(2)}) collective-permute-start(bf16[2,4,64,1024]{3,2,1,0:T(8,128)(2,1)S(1)} %fusion.37), channel_id=1, source_target_pairs={{0,8},{1,9},{2,10},{3,11},{4,12},{5,13},{6,14},{7,15},{8,0},{9,1},... | collective-permute-start | bytes 3145736 | tf_op jit(solution)/shard_map/ppermute | solution.py:754
  667.3 12.1 %collective-permute-start.36 = (bf16[4,64,768]{2,1,0:T(8,128)(2,1)S(1)}, bf16[4,64,768]{2,1,0:T(8,128)(2,1)S(1)}, u32[]{:S(2)}, u32[]{:S(2)}) collective-permute-start(bf16[4,64,768]{2,1,0:T(8,128)(2,1)S(1)} %fusion.80), channel_id=1, source_target_pairs={{0,16},{1,17},{2,18},{3,19},{4,20},{5,21},{6,22},{7,23},{8,24},{9,... | collective-permute-start | bytes 1179656 | tf_op jit(solution)/shard_map/ppermute | solution.py:754
  668.1 31.9 %collective-permute-start.33 = (bf16[2,4,64,1024]{3,2,1,0:T(8,128)(2,1)S(1)}, bf16[2,4,64,1024]{3,2,1,0:T(8,128)(2,1)}, u32[]{:S(2)}, u32[]{:S(2)}) collective-permute-start(bf16[2,4,64,1024]{3,2,1,0:T(8,128)(2,1)S(1)} %fusion.38), channel_id=1, source_target_pairs={{0,16},{1,17},{2,18},{3,19},{4,20},{5,21},{6,22},{7,23},{8,24},{9,... | collective-permute-start | bytes 3145736 | tf_op jit(solution)/shard_map/ppermute | solution.py:754
  670.1 27.0 %collective-permute-start.38 = (bf16[4,64,768]{2,1,0:T(8,128)(2,1)S(1)}, bf16[4,64,768]{2,1,0:T(8,128)(2,1)S(1)}, u32[]{:S(2)}, u32[]{:S(2)}) collective-permute-start(bf16[4,64,768]{2,1,0:T(8,128)(2,1)S(1)} %fusion.77), channel_id=1, source_target_pairs={{0,8},{1,9},{2,10},{3,11},{4,12},{5,13},{6,14},{7,15},{8,0},{9,1},... | collective-permute-start | bytes 1179656 | tf_op jit(solution)/shard_map/ppermute | solution.py:754
  698.5 13.4 %collective-permute-start.32 = (bf16[4,64,1024]{2,1,0:T(8,128)(2,1)}, bf16[4,64,1024]{2,1,0:T(8,128)(2,1)}, u32[]{:S(2)}, u32[]{:S(2)}) collective-permute-start(bf16[4,64,1024]{2,1,0:T(8,128)(2,1)} %fusion.45), channel_id=1, source_target_pairs={{0,16},{1,17},{2,18},{3,19},{4,20},{5,21},{6,22},{7,23},{8,24},{9,... | collective-permute-start | bytes 1572872 | tf_op jit(solution)/shard_map/ppermute | solution.py:754
  699.7 97.2 %reduce-scatter.9.cloned.1.call-start = ((), (), s32[]{:S(2)}) async-start(), calls=%async_computation.15 | async-start | bytes 1310720 | tf_op jit(solution)/shard_map/reduce_scatter | solution.py:822
  701.7 12.9 %collective-permute-start.34 = (bf16[4,64,1024]{2,1,0:T(8,128)(2,1)S(1)}, bf16[4,64,1024]{2,1,0:T(8,128)(2,1)S(1)}, u32[]{:S(2)}, u32[]{:S(2)}) collective-permute-start(bf16[4,64,1024]{2,1,0:T(8,128)(2,1)S(1)} %fusion.42), channel_id=1, source_target_pairs={{0,8},{1,9},{2,10},{3,11},{4,12},{5,13},{6,14},{7,15},{8,0},{9,1},... | collective-permute-start | bytes 1572872 | tf_op jit(solution)/shard_map/ppermute | solution.py:754
  721.8 22.9 %collective-permute-start.26 = (bf16[2,4,64,1024]{3,2,1,0:T(8,128)(2,1)S(1)}, bf16[2,4,64,1024]{3,2,1,0:T(8,128)(2,1)}, u32[]{:S(2)}, u32[]{:S(2)}) collective-permute-start(bf16[2,4,64,1024]{3,2,1,0:T(8,128)(2,1)S(1)} %fusion.35), channel_id=1, source_target_pairs={{0,8},{1,9},{2,10},{3,11},{4,12},{5,13},{6,14},{7,15},{8,0},{9,1},... | collective-permute-start | bytes 3145736 | tf_op jit(solution)/shard_map/ppermute | solution.py:754
  724.4 74.6 %reduce-scatter.7.cloned.1.call-start = ((), (), s32[]{:S(2)}) async-start(), calls=%async_computation.14 | async-start | bytes 1310720 | tf_op jit(solution)/shard_map/reduce_scatter | solution.py:822
  726.6 25.2 %collective-permute-start.28 = (bf16[2,4,64,1024]{3,2,1,0:T(8,128)(2,1)S(1)}, bf16[2,4,64,1024]{3,2,1,0:T(8,128)(2,1)S(1)}, u32[]{:S(2)}, u32[]{:S(2)}) collective-permute-start(bf16[2,4,64,1024]{3,2,1,0:T(8,128)(2,1)S(1)} %fusion.36), channel_id=1, source_target_pairs={{0,16},{1,17},{2,18},{3,19},{4,20},{5,21},{6,22},{7,23},{8,24},{9,... | collective-permute-start | bytes 3145736 | tf_op jit(solution)/shard_map/ppermute | solution.py:754
  746.4 14.1 %collective-permute-start.27 = (bf16[4,64,1024]{2,1,0:T(8,128)(2,1)S(1)}, bf16[4,64,1024]{2,1,0:T(8,128)(2,1)S(1)}, u32[]{:S(2)}, u32[]{:S(2)}) collective-permute-start(bf16[4,64,1024]{2,1,0:T(8,128)(2,1)S(1)} %fusion.51), channel_id=1, source_target_pairs={{0,16},{1,17},{2,18},{3,19},{4,20},{5,21},{6,22},{7,23},{8,24},{9,... | collective-permute-start | bytes 1572872 | tf_op jit(solution)/shard_map/ppermute | solution.py:754
  752.1 10.1 %collective-permute-start.29 = (bf16[4,64,1024]{2,1,0:T(8,128)(2,1)S(1)}, bf16[4,64,1024]{2,1,0:T(8,128)(2,1)S(1)}, u32[]{:S(2)}, u32[]{:S(2)}) collective-permute-start(bf16[4,64,1024]{2,1,0:T(8,128)(2,1)S(1)} %fusion.48), channel_id=1, source_target_pairs={{0,8},{1,9},{2,10},{3,11},{4,12},{5,13},{6,14},{7,15},{8,0},{9,1},... | collective-permute-start | bytes 1572872 | tf_op jit(solution)/shard_map/ppermute | solution.py:754
  766.8 4.3 collective-permute-start.20
  776.8 7.9 collective-permute-start.23
  784.8 9.2 %collective-permute-start.24 = (f32[11,1024]{1,0:T(8,128)S(1)}, f32[11,1024]{1,0:T(8,128)S(1)}, u32[]{:S(2)}, u32[]{:S(2)}) collective-permute-start(f32[11,1024]{1,0:T(8,128)S(1)} %add.984), channel_id=1, source_target_pairs={{0,4},{1,5},{2,6},{3,7},{4,0},{5,1},{6,2},{7,3},{8,12},{9,13},{10,... | collective-permute-start | bytes 135176 | tf_op jit(solution)/shard_map/ppermute | solution.py:754
  (80 other events, 741.2 us)
Sparse Core Ops, SparseCore 0:
  582.2 27.4 reduce-scatter.14
  614.9 26.5 reduce-scatter.16
  646.7 26.4 reduce-scatter.12
  699.9 23.6 reduce-scatter.10
  725.8 26.3 reduce-scatter.8
  763.9 30.5 reduce-scatter.6
